TPU v7x, 32 devices: a whole 2x2x4 slice. The times are simulated.
32 devices in a mesh: grp: 4 (over y, core), tok: 8 (over z, x).
Axes of the slice: x: 2, y: 2, z: 4, core: 2. Of those that a mesh axis runs over, the one named last changes fastest.
Arguments:
- tokens: bfloat16 [4, 1024, 1280], P('grp', 'tok'), may hold values from -6 to 6
- seg_lengths: int32 [4, 16], P('grp'), may hold values from 1 to 256, 1024 in all within a row
- prefix_keys: bfloat16 [4, 2048, 1280], P('grp', 'tok'), may hold values from -6 to 6
- prefix_values: bfloat16 [4, 2048, 1280], P('grp', 'tok'), may hold values from -0.4375 to 0.4375
- w_qkv: bfloat16 [1280, 3840], replicated, may hold values from -0.15625 to 0.15625
- w_out: bfloat16 [1280, 1280], replicated, may hold values from -0.15625 to 0.15625
- qk_scale: float32 [1280], replicated, may hold values from 0.3 to 10
- attn_rate: float32 [1280], replicated, may hold values from 0.05 to 0.5
- w_up: bfloat16 [1280, 5120], P(None, 'grp'), may hold values from -0.15625 to 0.15625
- w_gate: bfloat16 [1280, 5120], P(None, 'grp'), may hold values from -0.15625 to 0.15625
- w_down: bfloat16 [5120, 1280], P('grp'), may hold values from -0.078125 to 0.078125
- up_scale: float32 [5120], P('grp'), may hold values from 0.5 to 2
- gate_scale: float32 [5120], P('grp'), may hold values from 0.5 to 2
- mlp_rate: float32 [1280], replicated, may hold values from 0.05 to 0.5
Outputs:
- mixed: bfloat16 [4, 1024, 1280], P('grp', 'tok')
Inputs may be any that keep to these rules, and one draw needn't show every extreme that they name: `seg_lengths`: row g lists the lengths of group g's 16 requests in order of position; they sum to 1024 and the longest is exactly 256.
All inputs are finite; a program needn't handle non-finite values.
Results may differ from a plain program's by a relative error of at most 0.0085.
The roundings to bfloat16 on the way count: a program that leaves them out, or rounds other values in their place, can miss the bound.
Values may be sent and summed in bfloat16 or wider, within the bound.
No kernel may reach another device: no remote copies, remote signals or barrier semaphores. Data moves between devices by JAX's collectives and lax.ppermute only.
A program may use at most 128 MiB of HBM per device.

v0:
```python
import math

import jax
import jax.numpy as jnp
from jax import lax
from jax.sharding import PartitionSpec as P

D = 1280
HEADS = 20
HEAD = 64


EPS = 1e-06


def from_behind(shard, axis, by):
    length = lax.axis_size(axis)
    pairs = [(i, i + by) for i in range(length) if 0 <= i + by < length]
    return lax.ppermute(shard, axis, pairs)


def unit(vector):
    return vector * lax.rsqrt(jnp.sum(vector * vector, axis=-1, keepdims=True) + EPS)


def head_unit(vector, scaling):
    per_head = vector.reshape(vector.shape[0], HEADS, HEAD)
    return unit(per_head) * scaling.reshape(HEADS, HEAD)


def segment_of(position, lengths):
    bounds = jnp.cumsum(lengths, dtype=jnp.int32)
    return jnp.sum((position[:, None] >= bounds[None, :]).astype(jnp.int32), axis=1)


def block_state(query, keys, values, allowed):
    scores = math.sqrt(HEAD) * jnp.einsum(
        "rhd,khd->rhk", query, keys, preferred_element_type=jnp.float32
    )
    if allowed is not None:
        scores = jnp.where(allowed[:, None, :], scores, -jnp.inf)
    maximum = jnp.max(scores, axis=-1)
    weights = jnp.exp(scores - maximum[..., None])
    totals = jnp.sum(weights, axis=-1)
    blended = jnp.einsum(
        "rhk,khd->rhd", weights.astype(jnp.bfloat16), values, preferred_element_type=jnp.float32
    )
    return ((blended / totals[..., None]).astype(jnp.bfloat16), maximum, totals)


def start_state(block):
    blended, maximum, totals = block
    return (maximum, totals, totals[..., None] * blended.astype(jnp.float32))


def merge_block(running, block):
    maximum, totals, accum = running
    blended, block_max, block_sum = block
    new_max = jnp.maximum(maximum, block_max)
    shrink_old = jnp.exp(maximum - new_max)
    weight_new = jnp.exp(block_max - new_max) * block_sum
    return (
        new_max,
        totals * shrink_old + weight_new,
        accum * shrink_old[..., None] + weight_new[..., None] * blended.astype(jnp.float32),
    )


def earlier_pairs(suffix_keys, suffix_values):
    arrived = []
    for distance in (2, 1):
        arrived.append(from_behind((suffix_keys, suffix_values), "tok", distance))
    return arrived


def body(
    tokens,
    seg_lengths,
    prefix_keys,
    prefix_values,
    w_qkv,
    w_out,
    qk_scale,
    attn_rate,
    w_up,
    w_gate,
    w_down,
    up_scale,
    gate_scale,
    mlp_rate,
):
    row_count = tokens.shape[1]
    tok_place = lax.axis_index("tok")
    hidden_state = unit(tokens[0].astype(jnp.float32))
    projected = jnp.dot(
        hidden_state.astype(jnp.bfloat16), w_qkv, preferred_element_type=jnp.float32
    )
    query = head_unit(projected[:, :D], qk_scale).astype(jnp.bfloat16)
    suffix_keys = head_unit(projected[:, D : 2 * D], qk_scale).astype(jnp.bfloat16)
    suffix_values = projected[:, 2 * D :].astype(jnp.bfloat16).reshape(row_count, HEADS, HEAD)
    cached_keys = head_unit(prefix_keys[0].astype(jnp.float32), qk_scale).astype(jnp.bfloat16)
    cached_values = prefix_values[0].reshape(prefix_values.shape[1], HEADS, HEAD)
    shard_rows = cached_keys.shape[0]
    lengths = seg_lengths[0]
    query_pos = tok_place * row_count + jnp.arange(row_count, dtype=jnp.int32)
    query_seg = segment_of(query_pos, lengths)
    arrived = earlier_pairs(suffix_keys, suffix_values)
    window_keys = jnp.concatenate([arrived[0][0], arrived[1][0], suffix_keys], axis=0)
    window_values = jnp.concatenate([arrived[0][1], arrived[1][1], suffix_values], axis=0)
    key_pos = (tok_place - 2) * row_count + jnp.arange(3 * row_count, dtype=jnp.int32)
    key_seg = segment_of(key_pos, lengths)
    allowed = (
        (key_seg[None, :] == query_seg[:, None])
        & (key_pos[None, :] <= query_pos[:, None])
        & (key_pos[None, :] >= 0)
    )
    begin = start_state(block_state(query, window_keys, window_values, allowed))

    def add_block(running, matched):
        return (merge_block(running, block_state(query, matched[0], matched[1], None)), None)

    pieces = (
        lax.all_gather(cached_keys, "tok", axis=0, tiled=True),
        lax.all_gather(cached_values, "tok", axis=0, tiled=True),
    )
    piece_rows = pieces[0].shape[0]
    block_rows = math.gcd(piece_rows, max(shard_rows, 512))
    stack_keys = pieces[0].reshape(piece_rows // block_rows, block_rows, HEADS, HEAD)
    stack_values = pieces[1].reshape(piece_rows // block_rows, block_rows, HEADS, HEAD)
    result, ignored = lax.scan(add_block, begin, (stack_keys, stack_values))
    maximum, totals, accum = result
    attn_mix = (accum / totals[..., None]).astype(jnp.bfloat16).reshape(row_count, D)
    attended = unit(jnp.dot(attn_mix, w_out, preferred_element_type=jnp.float32))
    hidden_state = unit(hidden_state + attn_rate * (attended - hidden_state))
    flattened = hidden_state.astype(jnp.bfloat16)
    piece = lax.all_gather(flattened, "grp", axis=0, tiled=True)
    up_part = jnp.dot(piece, w_up, preferred_element_type=jnp.float32) * up_scale
    gate_part = jnp.dot(piece, w_gate, preferred_element_type=jnp.float32) * (
        gate_scale * math.sqrt(D)
    )
    act = (up_part * jax.nn.silu(gate_part)).astype(jnp.bfloat16)
    partials = jnp.dot(act, w_down, preferred_element_type=jnp.float32)
    summed = lax.psum_scatter(
        partials.astype(jnp.bfloat16), "grp", scatter_dimension=0, tiled=True
    ).astype(jnp.float32)
    mlp_dir = unit(summed)
    hidden_state = unit(hidden_state + mlp_rate * (mlp_dir - hidden_state))
    return (math.sqrt(D) * hidden_state).astype(jnp.bfloat16)[None]


def solution(mesh):
    in_specs = (
        P("grp", "tok", None),
        P("grp", None),
        P("grp", "tok", None),
        P("grp", "tok", None),
        P(),
        P(),
        P(),
        P(),
        P(None, "grp"),
        P(None, "grp"),
        P("grp", None),
        P("grp"),
        P("grp"),
        P(),
    )
    out_specs = P("grp", "tok", None)
    return jax.shard_map(body, mesh=mesh, in_specs=in_specs, out_specs=out_specs, check_vma=False)
```

profile of v0, /device:TPU:0, one launch (start us, length us, event | category | flops | bytes accessed | tf_op | source)
XLA Modules:
  0.0 316.8 jit_solution(17108080410088033840)
XLA Ops:
  6.5 0.9 mul.227
  7.5 2.2 copy.39
  9.7 1.3 fusion.56
  11.0 2.2 fusion.58
  13.2 2.2 copy.40
  15.5 1.1 fusion.93
  16.6 5.4 %fusion.95 = f32[128,3840]{1,0:T(8,128)S(1)} fusion(bf16[1280,3840]{1,0:T(8,128)(2,1)} %param.20, bf16[1,128,1280]{2,1,0:T(8,128)(2,1)} %param.16, f32[128]{0:T(128)S(1)} %add_rsqrt_fusion.7), kind=kOutput, calls=%fused_computation.88 | convolution fusion | flops 1258782720 | bytes 12124672 | tf_op jit(solution)/shard_map/dot_general | solution.py:95
  22.0 1.2 copy-done.2
  23.3 1.2 fusion.105
  24.4 2.2 copy.36
  26.7 2.2 copy.35
  28.9 1.2 multiply_reduce_fusion.3
  30.0 1.2 multiply_reduce_fusion.4
  31.2 2.4 multiply_convert_fusion.2
  33.6 5.6 %collective-permute-start = (bf16[128,20,64]{0,2,1:T(8,128)(2,1)}, bf16[128,20,64]{0,2,1:T(8,128)(2,1)}, u32[]{:S(2)}, u32[]{:S(2)}) collective-permute-start(bf16[128,20,64]{0,2,1:T(8,128)(2,1)} %get-tuple-element.83), channel_id=1, source_target_pairs={{0,2},{1,3},{2,4},{3,5},{4,6},{5,7},{8,10},{9,11},{10,12},{11,13},... | collective-permute-start | bytes 983048 | tf_op jit(solution)/shard_map/ppermute | solution.py:19
  39.2 4.1 %collective-permute-start.1 = (bf16[128,20,64]{0,2,1:T(8,128)(2,1)}, bf16[128,20,64]{0,2,1:T(8,128)(2,1)}, u32[]{:S(2)}, u32[]{:S(2)}) collective-permute-start(bf16[128,20,64]{0,2,1:T(8,128)(2,1)} %get-tuple-element.83), channel_id=1, source_target_pairs={{0,1},{1,2},{2,3},{3,4},{4,5},{5,6},{6,7},{8,9},{9,10},{10,11},{11... | collective-permute-start | bytes 983048 | tf_op jit(solution)/shard_map/ppermute | solution.py:19
  43.4 1.9 slice.17
  45.2 1.9 copy.37
  47.1 2.8 collective-permute-start.2
  49.9 4.2 %collective-permute-start.3 = (bf16[128,20,64]{0,2,1:T(8,128)(2,1)}, bf16[128,20,64]{0,2,1:T(8,128)(2,1)}, u32[]{:S(2)}, u32[]{:S(2)}) collective-permute-start(bf16[128,20,64]{0,2,1:T(8,128)(2,1)} %bitcast.147), channel_id=1, source_target_pairs={{0,1},{1,2},{2,3},{3,4},{4,5},{5,6},{6,7},{8,9},{9,10},{10,11},{11... | collective-permute-start | bytes 983048 | tf_op jit(solution)/shard_map/ppermute | solution.py:19
  54.2 0.1 reduce
  54.6 0.2 and_and_fusion
  54.8 2.2 fusion.48
  57.0 0.8 fusion.46
  57.8 4.9 %collective-permute-done.2 = bf16[128,20,64]{0,2,1:T(8,128)(2,1)} collective-permute-done((bf16[128,20,64]{0,2,1:T(8,128)(2,1)}, bf16[128,20,64]{0,2,1:T(8,128)(2,1)}, u32[]{:S(2)}, u32[]{:S(2)}) %collective-permute-start.2) | collective-permute-done | bytes 327712 | tf_op jit(solution)/shard_map/ppermute | solution.py:19
  62.8 3.1 fusion.71
  65.9 52.7 %all-gather.4.cloned.1.call-done = bf16[2048,20,64]{0,2,1:T(8,128)(2,1)} async-done(((bf16[256,20,64]{0,2,1:T(8,128)(2,1)}), bf16[2048,20,64]{0,2,1:T(8,128)(2,1)}) %all-gather.4.cloned.1.call-update) | async-done | bytes 5242896 | tf_op jit(solution)/shard_map/all_gather | solution.py:123
  118.5 5.6 %copy.50 = bf16[20,8,4,8,512]{4,3,1,0,2:T(8,128)(2,1)} copy(bf16[20,8,4,8,512]{4,3,2,1,0:T(8,128)(2,1)} %bitcast.141) | data formatting | bytes 10485760 | tf_op jit(solution)/shard_map/reshape | solution.py:128
  124.2 85.2 %all-gather.6.cloned.1.call-done = bf16[2048,20,64]{0,2,1:T(8,128)(2,1)} async-done(((bf16[256,20,64]{0,2,1:T(8,128)(2,1)}), bf16[2048,20,64]{0,2,1:T(8,128)(2,1)}) %all-gather.6.cloned.1.call-update) | async-done | bytes 5242896 | tf_op jit(solution)/shard_map/all_gather | solution.py:124
  209.4 5.6 %copy.49 = bf16[20,8,4,8,512]{4,3,1,0,2:T(8,128)(2,1)} copy(bf16[20,8,4,8,512]{4,3,2,1,0:T(8,128)(2,1)} %bitcast.142) | data formatting | bytes 10485760 | tf_op jit(solution)/shard_map/reshape | solution.py:129
  215.0 27.5 %while.14 = (s32[]{:T(128)}, f32[128,20]{0,1:T(8,128)S(1)}, f32[128,20]{0,1:T(8,128)S(1)}, f32[128,20,64]{0,2,1:T(8,128)}, bf16[4,512,20,64]{1,3,2,0:T(8,128)(2,...) while((s32[]{:T(128)}, f32[128,20]{0,1:T(8,128)S(1)}, ...), condition=%wide.region_12.13_spmd, body=%wide.region_9.12_spmd.sunk | while | flops 347023360 | bytes 25386124 | solution.py:130
  215.0 2.4 bitcast_reduce_fusion.2
  217.4 0.9 fusion.124
  218.3 0.2 copy-done.4
  218.5 2.6 fusion.125
  221.1 0.8 copy-done.5
  221.9 2.4 bitcast_reduce_fusion.2
  224.3 0.9 fusion.124
  225.2 0.2 copy-done.4
  225.4 2.6 fusion.125
  227.9 0.8 copy-done.5
  228.8 2.4 bitcast_reduce_fusion.2
  231.2 0.9 fusion.124
  232.1 0.2 copy-done.4
  232.2 2.6 fusion.125
  234.8 0.8 copy-done.5
  235.7 2.4 bitcast_reduce_fusion.2
  238.1 0.9 fusion.124
  239.0 0.2 copy-done.4
  239.1 2.6 fusion.125
  241.7 0.8 copy-done.5
  242.6 1.2 divide_convert_fusion
  243.8 2.6 multiply_reduce_fusion.2
  246.5 0.3 multiply_reduce_fusion.1
  246.8 0.8 copy-done.1
  247.7 0.8 multiply_convert_fusion.3
  248.5 0.2 reduce-scatter.2.cloned.1.call-start
  248.8 16.3 %all-gather.8.cloned.1.call-done = bf16[512,1280]{1,0:T(8,128)(2,1)} async-done(((bf16[128,1280]{1,0:T(8,128)(2,1)}), bf16[512,1280]{1,0:T(8,128)(2,1)}) %all-gather.8.cloned.1.call-update) | async-done | bytes 1310736 | tf_op jit(solution)/shard_map/all_gather | solution.py:136
  265.1 4.7 %convolution_multiply_fusion = f32[512,1280]{1,0:T(8,128)} fusion(bf16[512,1280]{1,0:T(8,128)(2,1)} %all-gather.8.cloned.1.call-done, bf16[1280,1280]{1,0:T(8,128)(2,1)S(1)} %copy-done, f32[1280]{0:T(1024)S(1)} %broadcast_multiply_fusion), kind=kOutput, calls=%fused_computation.31 | convolution fusion | flops 1678376960 | bytes 7214080 | tf_op jit(solution)/shard_map/dot_general | solution.py:138
  269.8 9.0 %convolution_convert_fusion = bf16[512,1280]{1,0:T(8,128)(2,1)} fusion(bf16[1280,1280]{1,0:T(8,128)(2,1)} %param.26, bf16[512,1280]{1,0:T(8,128)(2,1)} %all-gather.8.cloned.1.call-done, bf16[1280,1280]{1,0:T(8,128)(2,1)} %param.24, f32[512,1280]{1,0:T(8,128)} %convolution_multiply_fusion, f32[1280]{0:T(1024)S(1)} %copy-done.11), kind=kOutput, calls=%fused_computation.36 | convolution fusion | flops 3360686080 | bytes 11801600 | tf_op jit(solution)/shard_map/dot_general | solution.py:142
  278.8 26.7 %reduce-scatter.2.cloned.1.call-done = bf16[128,1280]{1,0:T(8,128)(2,1)} async-done(((bf16[512,1280]{1,0:T(8,128)(2,1)}), bf16[128,1280]{1,0:T(8,128)(2,1)}) %reduce-scatter.2.cloned.1.call-update) | async-done | bytes 327696 | tf_op jit(solution)/shard_map/reduce_scatter | solution.py:143
  305.4 1.1 fusion.88
  306.6 1.5 multiply_reduce_fusion
  308.1 2.2 fusion.94
  (55 shorter events, 0.6 us)
Async XLA Ops:
  6.5 258.5 %copy-start = (bf16[1280,1280]{1,0:T(8,128)(2,1)S(1)}, bf16[1280,1280]{1,0:T(8,128)(2,1)}, u32[]{:S(2)}) copy-start(bf16[1280,1280]{1,0:T(8,128)(2,1)} %param.25) | copy-start | bytes 9830404
  6.5 112.0 %all-gather.4.cloned.1.call-start = ((), (), s32[]{:S(2)}) async-start(), calls=%async_computation.1 | async-start | bytes 5898240 | tf_op jit(solution)/shard_map/all_gather | solution.py:123
  13.2 196.2 %all-gather.6.cloned.1.call-start = ((), (), s32[]{:S(2)}) async-start(), calls=%async_computation.2 | async-start | bytes 5898240 | tf_op jit(solution)/shard_map/all_gather | solution.py:124
  15.4 249.6 %all-gather.8.cloned.1.call-start = ((), (), s32[]{:S(2)}) async-start(), calls=%async_computation.3 | async-start | bytes 1638400 | tf_op jit(solution)/shard_map/all_gather | solution.py:136
  22.0 1.3 copy-start.2
  26.7 27.4 %copy-start.10 = (s32[1,16]{1,0:T(1,128)S(1)}, s32[1,16]{1,0:T(1,128)}, u32[]{:S(2)}) copy-start(s32[1,16]{1,0:T(1,128)} %param.17) | copy-start | bytes 196
  33.6 21.2 %collective-permute-start = (bf16[128,20,64]{0,2,1:T(8,128)(2,1)}, bf16[128,20,64]{0,2,1:T(8,128)(2,1)}, u32[]{:S(2)}, u32[]{:S(2)}) collective-permute-start(bf16[128,20,64]{0,2,1:T(8,128)(2,1)} %get-tuple-element.83), channel_id=1, source_target_pairs={{0,2},{1,3},{2,4},{3,5},{4,6},{5,7},{8,10},{9,11},{10,12},{11,13},... | collective-permute-start | bytes 983048 | tf_op jit(solution)/shard_map/ppermute | solution.py:19
  39.2 15.5 %collective-permute-start.1 = (bf16[128,20,64]{0,2,1:T(8,128)(2,1)}, bf16[128,20,64]{0,2,1:T(8,128)(2,1)}, u32[]{:S(2)}, u32[]{:S(2)}) collective-permute-start(bf16[128,20,64]{0,2,1:T(8,128)(2,1)} %get-tuple-element.83), channel_id=1, source_target_pairs={{0,1},{1,2},{2,3},{3,4},{4,5},{5,6},{6,7},{8,9},{9,10},{10,11},{11... | collective-permute-start | bytes 983048 | tf_op jit(solution)/shard_map/ppermute | solution.py:19
  47.1 15.6 %collective-permute-start.2 = (bf16[128,20,64]{0,2,1:T(8,128)(2,1)}, bf16[128,20,64]{0,2,1:T(8,128)(2,1)}, u32[]{:S(2)}, u32[]{:S(2)}) collective-permute-start(bf16[128,20,64]{0,2,1:T(8,128)(2,1)} %bitcast.146), channel_id=1, source_target_pairs={{0,2},{1,3},{2,4},{3,5},{4,6},{5,7},{8,10},{9,11},{10,12},{11,13},... | collective-permute-start | bytes 983048 | tf_op jit(solution)/shard_map/ppermute | solution.py:19
  49.9 12.8 %collective-permute-start.3 = (bf16[128,20,64]{0,2,1:T(8,128)(2,1)}, bf16[128,20,64]{0,2,1:T(8,128)(2,1)}, u32[]{:S(2)}, u32[]{:S(2)}) collective-permute-start(bf16[128,20,64]{0,2,1:T(8,128)(2,1)} %bitcast.147), channel_id=1, source_target_pairs={{0,1},{1,2},{2,3},{3,4},{4,5},{5,6},{6,7},{8,9},{9,10},{10,11},{11... | collective-permute-start | bytes 983048 | tf_op jit(solution)/shard_map/ppermute | solution.py:19
  57.0 5.7 %copy-start.6 = (bf16[128,1280]{0,1:T(8,128)(2,1)S(1)}, bf16[128,1280]{0,1:T(8,128)(2,1)}, u32[]{:S(2)}) copy-start(bf16[128,1280]{0,1:T(8,128)(2,1)} %copy.37) | copy-start | bytes 983044
  217.4 1.1 copy-start.4
  221.1 0.9 copy-start.5
  224.3 1.1 copy-start.4
  227.9 0.9 copy-start.5
  231.2 1.1 copy-start.4
  234.8 0.9 copy-start.5
  238.0 1.1 copy-start.4
  241.7 0.9 copy-start.5
  242.6 3.9 %copy-start.3 = (bf16[1,128,1280]{2,1,0:T(8,128)(2,1)S(1)}, bf16[1,128,1280]{2,1,0:T(8,128)(2,1)}, u32[]{:S(2)}) copy-start(bf16[1,128,1280]{2,1,0:T(8,128)(2,1)} %param.16) | copy-start | bytes 983044
  242.6 3.9 %copy-start.8 = (f32[1280]{0:T(1024)S(1)}, f32[1280]{0:T(1024)}, u32[]{:S(2)}) copy-start(f32[1280]{0:T(1024)} %param.23) | copy-start | bytes 15364
  243.8 5.0 %copy-start.9 = (f32[1280]{0:T(1024)S(1)}, f32[1280]{0:T(1024)}, u32[]{:S(2)}) copy-start(f32[1280]{0:T(1024)} %param.28) | copy-start | bytes 15364
  246.8 0.9 copy-start.1
  248.5 56.9 %reduce-scatter.2.cloned.1.call-start = ((), (), s32[]{:S(2)}) async-start(), calls=%async_computation.4 | async-start | bytes 1638400 | tf_op jit(solution)/shard_map/reduce_scatter | solution.py:143
  248.8 21.0 %copy-start.11 = (f32[1280]{0:T(1024)S(1)}, f32[1280]{0:T(1024)}, u32[]{:S(2)}) copy-start(f32[1280]{0:T(1024)} %param.27) | copy-start | bytes 15364
  269.7 36.8 %copy-start.7 = (f32[1280]{0:T(1024)S(1)}, f32[1280]{0:T(1024)}, u32[]{:S(2)}) copy-start(f32[1280]{0:T(1024)} %param.29) | copy-start | bytes 15364
Sparse Core Ops, SparseCore 0:
  13.3 105.1 all-gather.3
  120.6 88.7 all-gather.5
  248.6 16.3 all-gather.7
  278.9 26.5 reduce-scatter.1
where the time goes:
time: 318 us; the launch traced here: 317 us
  waiting for transfers between devices  186 us (58%)
  matrix products  46.8 us (15%)
  local copies, waits for them, and re-layouts  32.3 us (10%)
  other arithmetic  21.4 us (7%)
  starting transfers between devices  17 us (5%)
  between operations  13.3 us (4%)
    all_gather x1, waiting for transfers between devices, body(): lax.all_gather(cached_values, 'tok', axis=0, tiled=True)  85.2 us
    all_gather x1, waiting for transfers between devices, body(): lax.all_gather(cached_keys, 'tok', axis=0, tiled=True)  52.7 us
    reduce_scatter x1, waiting for transfers between devices, body(): lax.psum_scatter(partials.astype(jnp.bfloat16), 'grp', scatter_dimension=...  26.7 us
    ppermute x4, starting transfers between devices, from_behind(): return lax.ppermute(shard, axis, pairs)  16.7 us
    all_gather x1, waiting for transfers between devices, body(): piece = lax.all_gather(flattened, 'grp', axis=0, tiled=True)  16.3 us
    dot_general x5, matrix products, block_state(): jnp.einsum('rhk,khd->rhd', weights.astype(jnp.bfloat16), values, preferre...  13.4 us
    dot_general x5, matrix products, block_state(): jnp.einsum('rhd,khd->rhk', query, keys, preferred_element_type=jnp.float32)  11.6 us
    dot_general x1, matrix products, body(): partials = jnp.dot(act, w_down, preferred_element_type=jnp.float32)  8.98 us
  transfers between devices with their start and end apart: 8, of which 5 were waited for; matrix products, arithmetic and copies ran while one was open for 11% of the time, Pallas kernels for 0%

commit v1 on v0

v1 whole, which is shorter than its diff:
```python
import functools
import math

import jax
import jax.numpy as jnp
from jax import lax
from jax.experimental import pallas as pl
from jax.experimental.pallas import tpu as pltpu
from jax.sharding import PartitionSpec as P

D = 1280
HEADS = 20
HEAD = 64
EPS = 1e-06
SQ = 4
HQ = HEADS // SQ
QD = HQ * HEAD
LSE = 32
NEG = -1e30
MIB = 1 << 20

f32 = jnp.float32
bf16 = jnp.bfloat16


def unit(vector):
    return vector * lax.rsqrt(jnp.sum(vector * vector, axis=-1, keepdims=True) + EPS)


def head_unit_t(block, scale):
    dims, rows = block.shape
    per_head = block.reshape(dims // HEAD, HEAD, rows)
    total = jnp.sum(per_head * per_head, axis=1, keepdims=True)
    return (per_head * lax.rsqrt(total + EPS)).reshape(dims, rows) * scale


def params(limit=48):
    return pltpu.CompilerParams(vmem_limit_bytes=limit * MIB)


def vmem():
    return pl.BlockSpec(memory_space=pltpu.VMEM)


def smem():
    return pl.BlockSpec(memory_space=pltpu.SMEM)


def cost(flops, nbytes, trans=0):
    return pl.CostEstimate(flops=int(flops), bytes_accessed=int(nbytes), transcendentals=int(trans))


def quarter(i, m):
    return pl.multiple_of(jnp.bitwise_xor(i, m) * QD, QD)


def prefix_kernel(place, keys, values, scale, *rest):
    outs, scratch = rest[:SQ], rest[SQ]
    rows = keys.shape[0]
    i = lax.rem(place[0], SQ)
    for c in range(D // 128):
        cols = slice(c * 128, (c + 1) * 128)
        scale_t = jnp.broadcast_to(scale[:, cols], (128, 128)).T
        scale_t = jnp.concatenate([scale_t] * (rows // 128), axis=1)
        key_t = keys[:, cols].astype(f32).T
        scratch[cols, :] = head_unit_t(key_t, scale_t).astype(bf16)
        scratch[D + c * 128 : D + (c + 1) * 128, :] = values[:, cols].astype(f32).T.astype(bf16)
    for m in range(SQ):
        at = quarter(i, m)
        outs[m][:QD, :] = scratch[pl.ds(at, QD), :]
        outs[m][QD:, :] = scratch[pl.ds(D + at, QD), :]


def prefix_call(place, keys, values, scale):
    rows = keys.shape[0]
    return pl.pallas_call(
        prefix_kernel,
        out_shape=[jax.ShapeDtypeStruct((2 * QD, rows), bf16)] * SQ,
        in_specs=[smem(), vmem(), vmem(), vmem()],
        out_specs=[vmem()] * SQ,
        scratch_shapes=[pltpu.VMEM((2 * D, rows), bf16)],
        compiler_params=params(),
        cost_estimate=cost(0, 4 * rows * D * 2),
        name="prefix_prep",
    )(place, keys, values, scale)


QKV_BLOCK = 640


def qkv_kernel(place, tokens, weights, scale, *rest):
    full, query_outs, (hidden, scratch) = rest[:SQ], rest[SQ : 2 * SQ], rest[2 * SQ :]
    step = pl.program_id(0)
    per_part = D // QKV_BLOCK

    @pl.when(step == 0)
    def _():
        hidden[...] = unit(tokens[...].astype(f32)).astype(bf16)

    out = jnp.dot(hidden[...], weights[...], preferred_element_type=f32)
    at = pl.multiple_of(step * QKV_BLOCK, QKV_BLOCK)

    @pl.when(step < 2 * per_part)
    def _():
        times = jnp.where(step < per_part, math.sqrt(HEAD), 1.0)
        for c in range(QKV_BLOCK // 128):
            cols = slice(c * 128, (c + 1) * 128)
            scale_t = jnp.broadcast_to(scale[:, cols], (128, 128)).T
            block = head_unit_t(out[:, cols].T, scale_t[:, : out.shape[0]])
            scratch[pl.ds(at + c * 128, 128), :] = (block * times).astype(bf16)

    @pl.when(step >= 2 * per_part)
    def _():
        for c in range(QKV_BLOCK // 128):
            scratch[pl.ds(at + c * 128, 128), :] = out[:, c * 128 : (c + 1) * 128].T.astype(bf16)

    @pl.when(step == 3 * per_part - 1)
    def _():
        i = lax.rem(place[0], SQ)
        for m in range(SQ):
            start = quarter(i, m)
            query_outs[m][...] = scratch[pl.ds(start, QD), :]
            for part in range(3):
                full[m][part * QD : (part + 1) * QD, :] = scratch[pl.ds(part * D + start, QD), :]


def qkv_call(place, tokens, weights, scale):
    rows = tokens.shape[0]
    per_part = D // QKV_BLOCK
    whole = lambda j, place: (0, 0)
    return pl.pallas_call(
        qkv_kernel,
        out_shape=[jax.ShapeDtypeStruct((3 * QD, rows), bf16)] * SQ
        + [jax.ShapeDtypeStruct((QD, rows), bf16)] * SQ,
        grid_spec=pltpu.PrefetchScalarGridSpec(
            num_scalar_prefetch=1,
            grid=(3 * per_part,),
            in_specs=[
                pl.BlockSpec((rows, D), whole),
                pl.BlockSpec((D, QKV_BLOCK), lambda j, place: (0, j)),
                pl.BlockSpec((1, QKV_BLOCK), lambda j, place: (0, lax.rem(j, per_part))),
            ],
            out_specs=[pl.BlockSpec((3 * QD, rows), whole)] * SQ
            + [pl.BlockSpec((QD, rows), whole)] * SQ,
            scratch_shapes=[pltpu.VMEM((rows, D), bf16), pltpu.VMEM((3 * D, rows), bf16)],
        ),
        compiler_params=params(),
        cost_estimate=cost(2 * rows * D * 3 * D, 3 * D * D * 2),
        name="qkv",
    )(place, tokens, weights, scale)


def block_state(score, values_t):
    top = jnp.max(score, axis=0, keepdims=True)
    weights = jnp.exp(score - top)
    total = jnp.sum(weights, axis=0, keepdims=True)
    blended = jnp.dot(values_t, weights.astype(bf16), preferred_element_type=f32)
    return (blended * (1.0 / total)).astype(bf16).astype(f32), top, total


def merge(states):
    top = functools.reduce(jnp.maximum, [s[1] for s in states])
    weights = [jnp.exp(s[1] - top) * s[2] for s in states]
    total = functools.reduce(jnp.add, weights)
    accum = functools.reduce(jnp.add, [w * s[0] for w, s in zip(weights, states)])
    return accum * (1.0 / total), top + jnp.log(total)


def attend_kernel(shift, place, lengths, *rest):
    suffix = rest[:SQ]
    prefix = rest[SQ : 2 * SQ]
    rest = rest[2 * SQ :]
    if shift:
        queries, rest = rest[:SQ], rest[SQ:]
    else:
        queries = suffix
    outs, (query, keys, values, out, lse) = rest[:SQ], rest[SQ:]
    rows = suffix[0].shape[1]
    i = lax.rem(place[0], SQ)
    square = lax.div(place[0], SQ)
    query_square = jnp.bitwise_xor(square, shift)
    for m in range(SQ):
        lanes = pl.ds(pl.multiple_of(jnp.bitwise_xor(i, m) * rows, rows), rows)
        query[:, lanes] = queries[m][:QD, :]
        keys[:, lanes] = suffix[m][QD : 2 * QD, :]
        values[:, lanes] = suffix[m][2 * QD :, :]
    lse[...] = jnp.zeros_like(lse)

    position = query_square * (SQ * rows) + lax.broadcasted_iota(jnp.int32, (1, SQ * rows), 1)
    first = jnp.zeros((1, SQ * rows), jnp.int32)
    bound = jnp.int32(0)
    for r in range(lengths.shape[1]):
        bound = bound + lengths[0, r]
        first = jnp.where(position >= bound, bound, first)

    def own(h, j, key_from, key_to):
        head = slice(h * HEAD, (h + 1) * HEAD)
        lanes = slice(j * rows, (j + 1) * rows)
        span = slice(key_from * rows, key_to * rows)
        score = jnp.dot(
            keys[head, span].astype(f32).T.astype(bf16), query[head, lanes], preferred_element_type=f32
        )
        key_at = (square * SQ + key_from) * rows + lax.broadcasted_iota(jnp.int32, score.shape, 0)
        allowed = (key_at >= first[:, lanes]) & (key_at <= position[:, lanes])
        return block_state(jnp.where(allowed, score, NEG), values[head, span])

    def run(with_suffix):
        for h in range(HQ):
            head = slice(h * HEAD, (h + 1) * HEAD)
            head_v = slice(QD + h * HEAD, QD + (h + 1) * HEAD)
            keys_n = [prefix[m][head, :].astype(f32).T.astype(bf16) for m in range(SQ)]
            for c in range(0, SQ, 2):
                lanes = slice(c * rows, (c + 2) * rows)
                states = [
                    block_state(
                        jnp.dot(keys_n[m], query[head, lanes], preferred_element_type=f32),
                        prefix[m][head_v, :],
                    )
                    for m in range(SQ)
                ]
                extra = None
                if with_suffix and not shift:
                    extra = [own(h, j, max(0, j - 2), j + 1) for j in (c, c + 1)]
                elif with_suffix and c == 0:
                    extra = [own(h, j, SQ - 2 + j, SQ) for j in (0, 1)]
                if extra:
                    states.append(tuple(jnp.concatenate(p, axis=1) for p in zip(*extra)))
                mixed, level = merge(states)
                out[head, lanes] = mixed.astype(bf16)
                lse[h : h + 1, lanes] = level

    if shift:
        follows = query_square == square + 1
        pl.when(follows)(lambda: run(True))
        pl.when(jnp.logical_not(follows))(lambda: run(False))
    else:
        run(True)

    level = lse[...]
    high = level.astype(bf16).astype(f32)
    middle = (level - high).astype(bf16).astype(f32)
    low = level - high - middle
    pieces = jnp.concatenate([high, middle, low, jnp.zeros_like(low)], axis=0).astype(bf16)
    out[QD:, :] = pieces
    for m in range(SQ):
        lanes = pl.ds(pl.multiple_of(jnp.bitwise_xor(i, m) * rows, rows), rows)
        outs[m][...] = out[:, lanes]


def attend_call(shift, place, lengths, suffix, prefix, queries):
    rows = suffix[0].shape[1]
    span = prefix[0].shape[1]
    ins = [*suffix, *prefix, *queries]
    pairs = SQ * rows * SQ * span * HQ
    return pl.pallas_call(
        functools.partial(attend_kernel, shift),
        out_shape=[jax.ShapeDtypeStruct((QD + LSE, rows), bf16)] * SQ,
        in_specs=[smem(), smem()] + [vmem()] * len(ins),
        out_specs=[vmem()] * SQ,
        scratch_shapes=[
            pltpu.VMEM((QD, SQ * rows), bf16),
            pltpu.VMEM((QD, SQ * rows), bf16),
            pltpu.VMEM((QD, SQ * rows), bf16),
            pltpu.VMEM((QD + LSE, SQ * rows), bf16),
            pltpu.VMEM((8, SQ * rows), f32),
        ],
        compiler_params=params(),
        cost_estimate=cost(4 * 4 * HEAD * pairs, 4 * MIB, pairs),
        name="attend_cross" if shift else "attend_own",
    )(place, lengths, *ins)


def project_kernel(count, place, tokens, rate, w_hbm, *rest):
    parts = rest[: SQ * count]
    hidden_out, flat_out, mix, w_out, sem = rest[SQ * count :]
    copy = pltpu.make_async_copy(w_hbm, w_out, sem)
    copy.start()
    i = lax.rem(place[0], SQ)
    for m in range(SQ):
        group = [parts[s * SQ + m] for s in range(count)]
        levels = []
        for part in group:
            pieces = part[QD:, :].astype(f32)
            levels.append(pieces[0:8, :] + pieces[8:16, :] + pieces[16:24, :])
        top = functools.reduce(jnp.maximum, levels)
        weights = [jnp.exp(v - top) for v in levels]
        inverse = 1.0 / functools.reduce(jnp.add, weights)
        weights = [w * inverse for w in weights]
        start = quarter(i, m)
        for h in range(HQ):
            head = slice(h * HEAD, (h + 1) * HEAD)
            mixed = functools.reduce(
                jnp.add, [w[h : h + 1, :] * p[head, :].astype(f32) for w, p in zip(weights, group)]
            )
            mix[pl.ds(start + h * HEAD, HEAD), :] = mixed.astype(bf16)
    hidden = unit(tokens[...].astype(f32))
    attn = jnp.concatenate(
        [mix[c * 128 : (c + 1) * 128, :].astype(f32).T.astype(bf16) for c in range(D // 128)], axis=1
    )
    copy.wait()
    attended = unit(jnp.dot(attn, w_out[...], preferred_element_type=f32))
    hidden = unit(hidden + rate[...] * (attended - hidden))
    hidden_out[...] = hidden
    flat_out[...] = hidden.astype(bf16)


def project_call(place, tokens, rate, w_out, parts):
    rows = tokens.shape[0]
    return pl.pallas_call(
        functools.partial(project_kernel, len(parts) // SQ),
        out_shape=[jax.ShapeDtypeStruct((rows, D), f32), jax.ShapeDtypeStruct((rows, D), bf16)],
        in_specs=[smem(), vmem(), vmem(), pl.BlockSpec(memory_space=pl.ANY)] + [vmem()] * len(parts),
        out_specs=[vmem()] * 2,
        scratch_shapes=[
            pltpu.VMEM((D, rows), bf16),
            pltpu.VMEM((D, D), bf16),
            pltpu.SemaphoreType.DMA,
        ],
        compiler_params=params(),
        cost_estimate=cost(2 * rows * D * D, D * D * 2),
        name="project",
    )(place, tokens, rate, w_out, *parts)


FF_BLOCK = 256


def mlp_kernel(first, second, w_up, w_gate, w_down, up_scale, gate_scale, keep, send, rows_in, total):
    step = pl.program_id(0)
    rows = first.shape[0]

    @pl.when(step == 0)
    def _():
        rows_in[:rows, :] = first[...]
        rows_in[rows:, :] = second[...]

    data = rows_in[...]
    up = jnp.dot(data, w_up[...], preferred_element_type=f32) * up_scale[...]
    gate = jnp.dot(data, w_gate[...], preferred_element_type=f32) * (gate_scale[...] * math.sqrt(D))
    act = (up * (gate / (1.0 + jnp.exp(-gate)))).astype(bf16)
    part = jnp.dot(act, w_down[...], preferred_element_type=f32)

    @pl.when(step == 0)
    def _():
        total[...] = part

    @pl.when(step > 0)
    def _():
        total[...] += part

    @pl.when(step == pl.num_programs(0) - 1)
    def _():
        keep[...] = total[:rows, :]
        send[...] = total[rows:, :].astype(bf16)


def mlp_call(first, second, w_up, w_gate, w_down, up_scale, gate_scale):
    rows = first.shape[0]
    units = w_up.shape[1]
    whole = lambda j: (0, 0)
    across = lambda j: (0, j)
    return pl.pallas_call(
        mlp_kernel,
        grid=(units // FF_BLOCK,),
        out_shape=[jax.ShapeDtypeStruct((rows, D), f32), jax.ShapeDtypeStruct((rows, D), bf16)],
        in_specs=[
            pl.BlockSpec((rows, D), whole),
            pl.BlockSpec((rows, D), whole),
            pl.BlockSpec((D, FF_BLOCK), across),
            pl.BlockSpec((D, FF_BLOCK), across),
            pl.BlockSpec((FF_BLOCK, D), lambda j: (j, 0)),
            pl.BlockSpec((1, FF_BLOCK), across),
            pl.BlockSpec((1, FF_BLOCK), across),
        ],
        out_specs=[pl.BlockSpec((rows, D), whole)] * 2,
        scratch_shapes=[pltpu.VMEM((2 * rows, D), bf16), pltpu.VMEM((2 * rows, D), f32)],
        compiler_params=params(),
        cost_estimate=cost(2 * 2 * rows * D * units * 3, 3 * D * units * 2, 2 * rows * units),
        name="mlp",
    )(first, second, w_up, w_gate, w_down, up_scale, gate_scale)


def add_kernel(kept, arrived, out):
    out[...] = (kept[...] + arrived[...].astype(f32)).astype(bf16)


def add_call(kept, arrived):
    return pl.pallas_call(
        add_kernel,
        out_shape=jax.ShapeDtypeStruct(kept.shape, bf16),
        in_specs=[vmem()] * 2,
        out_specs=vmem(),
        cost_estimate=cost(kept.size, kept.size * 8),
        name="add_partials",
    )(kept, arrived)


def final_kernel(hidden, rate, kept, *rest):
    arrived, out = rest[:-1], rest[-1]
    total = kept[...]
    for part in arrived:
        total = total + part[...].astype(f32)
    state = hidden[...]
    state = unit(state + rate[...] * (unit(total) - state))
    out[...] = (math.sqrt(D) * state).astype(bf16)


def final_call(hidden, rate, kept, arrived):
    return pl.pallas_call(
        final_kernel,
        out_shape=jax.ShapeDtypeStruct(hidden.shape, bf16),
        in_specs=[vmem()] * (3 + len(arrived)),
        out_specs=vmem(),
        cost_estimate=cost(hidden.size * 10, hidden.size * 12),
        name="finish",
    )(hidden, rate, kept, *arrived)


def swap(shard, axis, mask):
    length = lax.axis_size(axis)
    return lax.ppermute(shard, axis, [(j, j ^ mask) for j in range(length)])


def body(
    tokens,
    seg_lengths,
    prefix_keys,
    prefix_values,
    w_qkv,
    w_out,
    qk_scale,
    attn_rate,
    w_up,
    w_gate,
    w_down,
    up_scale,
    gate_scale,
    mlp_rate,
):
    squares = lax.axis_size("tok") // SQ
    place = lax.axis_index("tok").astype(jnp.int32).reshape(1)
    own = tokens[0]
    scale = qk_scale.reshape(1, D)

    prefix = prefix_call(place, prefix_keys[0], prefix_values[0], scale)
    prefix = [prefix[0]] + [swap(prefix[m], "tok", m) for m in range(1, SQ)]
    sent = qkv_call(place, own, w_qkv, scale)
    suffix = [sent[0]] + [swap(sent[m], "tok", m) for m in range(1, SQ)]
    crossed = [[swap(sent[SQ + m], "tok", SQ * s + m) for m in range(SQ)] for s in range(1, squares)]

    parts = attend_call(0, place, seg_lengths, suffix, prefix, [])
    gathered = [parts[0]] + [swap(parts[m], "tok", m) for m in range(1, SQ)]
    for s in range(1, squares):
        parts = attend_call(s, place, seg_lengths, suffix, prefix, crossed[s - 1])
        gathered += [swap(parts[m], "tok", SQ * s + m) for m in range(SQ)]
    hidden, flat = project_call(place, own, attn_rate.reshape(1, D), w_out, gathered)

    weights = (w_up, w_gate, w_down, up_scale.reshape(1, -1), gate_scale.reshape(1, -1))
    chips = lax.axis_size("grp") // 2
    remote = [swap(flat, "grp", 2 * c) for c in range(1, chips)]
    keep, send = mlp_call(flat, swap(flat, "grp", 1), *weights)
    arrived = [swap(send, "grp", 1)]
    for c in range(1, chips):
        rows = remote[c - 1]
        kept, send = mlp_call(rows, swap(rows, "grp", 1), *weights)
        arrived.append(swap(add_call(kept, swap(send, "grp", 1)), "grp", 2 * c))
    return final_call(hidden, mlp_rate.reshape(1, D), keep, arrived)[None]


def solution(mesh):
    in_specs = (
        P("grp", "tok", None),
        P("grp", None),
        P("grp", "tok", None),
        P("grp", "tok", None),
        P(),
        P(),
        P(),
        P(),
        P(None, "grp"),
        P(None, "grp"),
        P("grp", None),
        P("grp"),
        P("grp"),
        P(),
    )
    out_specs = P("grp", "tok", None)
    return jax.shard_map(body, mesh=mesh, in_specs=in_specs, out_specs=out_specs, check_vma=False)
```

time: 318 us -> 142 us (0.45)
  waiting for transfers between devices: 186 us -> 45.1 us
  Pallas kernels: 0 us -> 57 us
  matrix products: 46.8 us -> 0 us
  local copies, waits for them, and re-layouts: 32.3 us -> 6.32 us
  other arithmetic: 21.4 us -> 0 us
  starting transfers between devices: 17 us -> 32.7 us
  between operations: 13.3 us -> 0.19 us
    all_gather x3 -> x0, waiting for transfers between devices: 154 us -> none  [the longest x1 85.2 us: body(): lax.all_gather(cached_values, 'tok', axis=0, tiled=True)]
    pallas_call x0 -> x9, Pallas kernels: none -> 57 us  [the longest x2 28.4 us: attend_call(): pl.pallas_call(functools.partial(attend_kernel, shift), out_shape=[jax.Sh...]
    dot_general x14 -> x0, matrix products: 46.8 us -> none  [the longest x5 13.4 us: block_state(): jnp.einsum('rhk,khd->rhd', weights.astype(jnp.bfloat16), values, preferre...]
    ppermute x4 -> x23, waiting for transfers between devices: 4.94 us -> 45.1 us  [swap(): return lax.ppermute(shard, axis, [(j, j ^ mask) for j in range(length)])]
    reduce_scatter x1 -> x0, waiting for transfers between devices: 26.7 us -> none  [body(): lax.psum_scatter(partials.astype(jnp.bfloat16), 'grp', scatter_dimension=...]
    ppermute x4 -> x23, starting transfers between devices: 16.7 us -> 32.7 us  [swap(): return lax.ppermute(shard, axis, [(j, j ^ mask) for j in range(length)])]
    reduce_sum x14 -> x0, other arithmetic: 12.1 us -> none  [the longest x7 7.62 us: unit(): jnp.sum(vector * vector, axis=-1, keepdims=True) + EPS]
    reshape x2 -> x5, local copies, waits for them, and re-layouts: 11.3 us -> 1.31 us  [the longest x1 0.7 us: body(): scale = qk_scale.reshape(1, D)]
  transfers between devices with their start and end apart: 8 -> 23, of which waited for: 5 -> 9; matrix products, arithmetic and copies ran while one was open for 11% -> 0% of each run, Pallas kernels for 0% -> 23%
where the time goes in v1:
time: 142 us; the launch traced here: 141 us
  Pallas kernels  57 us (40%)
  waiting for transfers between devices  45.1 us (32%)
  starting transfers between devices  32.7 us (23%)
  local copies, waits for them, and re-layouts  6.32 us (4%)
    ppermute x23, waiting for transfers between devices, swap(): return lax.ppermute(shard, axis, [(j, j ^ mask) for j in range(length)])  45.1 us
    ppermute x23, starting transfers between devices, swap(): return lax.ppermute(shard, axis, [(j, j ^ mask) for j in range(length)])  32.7 us
    pallas_call x2, Pallas kernels, attend_call(): pl.pallas_call(functools.partial(attend_kernel, shift), out_shape=[jax.Sh...  28.4 us
    pallas_call x2, Pallas kernels, mlp_call(): pl.pallas_call(mlp_kernel, grid=(units // FF_BLOCK,), out_shape=[jax.Shap...  14.1 us
    pallas_call x1, Pallas kernels, qkv_call(): pl.pallas_call(qkv_kernel, out_shape=[jax.ShapeDtypeStruct((3 * QD, rows)...  7.62 us
    unnamed x34, local copies, waits for them, and re-layouts  5.01 us
  transfers between devices with their start and end apart: 23, of which 9 were waited for; matrix products, arithmetic and copies ran while one was open for 0% of the time, Pallas kernels for 23%

profile of v1, /device:TPU:0, one launch (start us, length us, event | category | flops | bytes accessed | tf_op | source)
XLA Modules:
  0.0 141.3 jit_solution(7683444622228076773)
XLA Ops:
  0.0 0.7 reshape.20.scale
  0.7 1.0 copy-done.2
  1.7 7.6 %qkv.1 = (bf16[960,128]{1,0:T(8,128)(2,1)S(1)}, bf16[960,128]{1,0:T(8,128)(2,1)S(1)}, bf16[960,128]{1,0:T(8,128)(2,1)S(1)}, bf16[960,128]{1,0:T(8,128)(2,1)S(1)}...) custom-call(s32[1]{0:T(128)} %bitcast.place, ...), custom_call_target="tpu_custom_call" | custom-call | flops 1258291200 | bytes 9830400 | tf_op jit(solution)/shard_map/qkv/pallas_call | solution.py:131
  9.3 3.0 %collective-permute-start = (bf16[960,128]{1,0:T(8,128)(2,1)S(1)}, bf16[960,128]{1,0:T(8,128)(2,1)S(1)}, u32[]{:S(2)}, u32[]{:S(2)}) collective-permute-start(bf16[960,128]{1,0:T(8,128)(2,1)S(1)} %get-tuple-element.32), channel_id=1, source_target_pairs={{0,1},{1,0},{2,3},{3,2},{4,5},{5,4},{6,7},{7,6},{8,9},{9,8},{10,11... | collective-permute-start | bytes 737288 | tf_op jit(solution)/shard_map/ppermute | solution.py:421
  12.3 2.6 %collective-permute-start.10 = (bf16[320,128]{1,0:T(8,128)(2,1)S(1)}, bf16[320,128]{1,0:T(8,128)(2,1)S(1)}, u32[]{:S(2)}, u32[]{:S(2)}) collective-permute-start(bf16[320,128]{1,0:T(8,128)(2,1)S(1)} %get-tuple-element.44), channel_id=1, source_target_pairs={{0,5},{1,4},{2,7},{3,6},{4,1},{5,0},{6,3},{7,2},{8,13},{9,12},{10,... | collective-permute-start | bytes 245768 | tf_op jit(solution)/shard_map/ppermute | solution.py:421
  14.9 1.4 collective-permute-start.11
  16.2 3.4 %collective-permute-start.12 = (bf16[320,128]{1,0:T(8,128)(2,1)S(1)}, bf16[320,128]{1,0:T(8,128)(2,1)S(1)}, u32[]{:S(2)}, u32[]{:S(2)}) collective-permute-start(bf16[320,128]{1,0:T(8,128)(2,1)S(1)} %get-tuple-element.46), channel_id=1, source_target_pairs={{0,7},{1,6},{2,5},{3,4},{4,3},{5,2},{6,1},{7,0},{8,15},{9,14},{10,... | collective-permute-start | bytes 245768 | tf_op jit(solution)/shard_map/ppermute | solution.py:421
  19.6 0.0 collective-permute-start.9
  19.6 0.7 prefix_prep.1
  20.3 5.2 %collective-permute-done.10.rest_9_ = bf16[320,128]{1,0:T(8,128)(2,1)S(1)} collective-permute-done((bf16[320,128]{1,0:T(8,128)(2,1)S(1)}, bf16[320,128]{1,0:T(8,128)(2,1)S(1)}, u32[]{:S(2)}, u32[]{:S(2)}) %collective-permute-start.10) | collective-permute-done | bytes 81952 | tf_op jit(solution)/shard_map/ppermute | solution.py:421
  25.5 0.0 collective-permute-start.3
  25.5 0.0 collective-permute-done.11.rest_10_
  25.5 1.3 collective-permute-start.4
  26.8 0.0 collective-permute-done.12.rest_11_
  26.8 2.7 %collective-permute-start.5 = (bf16[640,256]{1,0:T(8,128)(2,1)S(1)}, bf16[640,256]{1,0:T(8,128)(2,1)S(1)}, u32[]{:S(2)}, u32[]{:S(2)}) collective-permute-start(bf16[640,256]{1,0:T(8,128)(2,1)S(1)} %get-tuple-element.38), channel_id=1, source_target_pairs={{0,3},{1,2},{2,1},{3,0},{4,7},{5,6},{6,5},{7,4},{8,11},{9,10},{10,... | collective-permute-start | bytes 983048 | tf_op jit(solution)/shard_map/ppermute | solution.py:421
  29.5 0.1 collective-permute-done.9.rest_8_
  29.6 0.5 collective-permute-start.1
  30.1 0.0 collective-permute-done.rest_1_
  30.1 2.5 %collective-permute-start.2 = (bf16[960,128]{1,0:T(8,128)(2,1)S(1)}, bf16[960,128]{1,0:T(8,128)(2,1)S(1)}, u32[]{:S(2)}, u32[]{:S(2)}) collective-permute-start(bf16[960,128]{1,0:T(8,128)(2,1)S(1)} %get-tuple-element.34), channel_id=1, source_target_pairs={{0,3},{1,2},{2,1},{3,0},{4,7},{5,6},{6,5},{7,4},{8,11},{9,10},{10,... | collective-permute-start | bytes 737288 | tf_op jit(solution)/shard_map/ppermute | solution.py:421
  32.6 16.4 %collective-permute-done.1.rest_2_ = bf16[960,128]{1,0:T(8,128)(2,1)S(1)} collective-permute-done((bf16[960,128]{1,0:T(8,128)(2,1)S(1)}, bf16[960,128]{1,0:T(8,128)(2,1)S(1)}, u32[]{:S(2)}, u32[]{:S(2)}) %collective-permute-start.1) | collective-permute-done | bytes 245792 | tf_op jit(solution)/shard_map/ppermute | solution.py:421
  49.0 5.6 %collective-permute-done.2.rest_3_ = bf16[960,128]{1,0:T(8,128)(2,1)S(1)} collective-permute-done((bf16[960,128]{1,0:T(8,128)(2,1)S(1)}, bf16[960,128]{1,0:T(8,128)(2,1)S(1)}, u32[]{:S(2)}, u32[]{:S(2)}) %collective-permute-start.2) | collective-permute-done | bytes 245792 | tf_op jit(solution)/shard_map/ppermute | solution.py:421
  54.6 0.0 collective-permute-done.3.rest_5_
  54.6 0.0 collective-permute-done.4.rest_6_
  54.6 0.0 collective-permute-done.5.rest_7_
  54.6 12.7 %attend_cross.1 = (bf16[352,128]{1,0:T(8,128)(2,1)S(1)}, bf16[352,128]{1,0:T(8,128)(2,1)S(1)}, bf16[352,128]{1,0:T(8,128)(2,1)S(1)}, bf16[352,128]{1,0:T(8,128)(2,1)S(1)}) custom-call(s32[1]{0:T(128)} %bitcast.place, s32[1,16]{1,0:T(1,128)S(1)} %copy-done.9, bf16[960,128]{1,0:T(8,128)(2,1)S(1)} %get-tuple-element.31.rest_0_, ...), custom_call_target="tpu_custom_call" | custom-call | flops 2684354560 | bytes 4194304 | tf_op jit(solution)/shard_map/attend_cross/pallas_call | solution.py:255
  67.3 1.5 %collective-permute-start.13 = (bf16[352,128]{1,0:T(8,128)(2,1)S(1)}, bf16[352,128]{1,0:T(8,128)(2,1)S(1)}, u32[]{:S(2)}, u32[]{:S(2)}) collective-permute-start(bf16[352,128]{1,0:T(8,128)(2,1)S(1)} %get-tuple-element.47), channel_id=1, source_target_pairs={{0,4},{1,5},{2,6},{3,7},{4,0},{5,1},{6,2},{7,3},{8,12},{9,13},{10,... | collective-permute-start | bytes 270344 | tf_op jit(solution)/shard_map/ppermute | solution.py:421
  68.8 1.4 %collective-permute-start.14 = (bf16[352,128]{1,0:T(8,128)(2,1)S(1)}, bf16[352,128]{1,0:T(8,128)(2,1)S(1)}, u32[]{:S(2)}, u32[]{:S(2)}) collective-permute-start(bf16[352,128]{1,0:T(8,128)(2,1)S(1)} %get-tuple-element.48), channel_id=1, source_target_pairs={{0,5},{1,4},{2,7},{3,6},{4,1},{5,0},{6,3},{7,2},{8,13},{9,12},{10,... | collective-permute-start | bytes 270344 | tf_op jit(solution)/shard_map/ppermute | solution.py:421
  70.3 3.4 %collective-permute-start.15 = (bf16[352,128]{1,0:T(8,128)(2,1)S(1)}, bf16[352,128]{1,0:T(8,128)(2,1)S(1)}, u32[]{:S(2)}, u32[]{:S(2)}) collective-permute-start(bf16[352,128]{1,0:T(8,128)(2,1)S(1)} %get-tuple-element.49), channel_id=1, source_target_pairs={{0,6},{1,7},{2,4},{3,5},{4,2},{5,3},{6,0},{7,1},{8,14},{9,15},{10,... | collective-permute-start | bytes 270344 | tf_op jit(solution)/shard_map/ppermute | solution.py:421
  73.7 1.3 collective-permute-start.16
  75.0 15.7 %attend_own.1 = (bf16[352,128]{1,0:T(8,128)(2,1)S(1)}, bf16[352,128]{1,0:T(8,128)(2,1)S(1)}, bf16[352,128]{1,0:T(8,128)(2,1)S(1)}, bf16[352,128]{1,0:T(8,128)(2,1)S(1)}) custom-call(s32[1]{0:T(128)} %bitcast.place, s32[1,16]{1,0:T(1,128)S(1)} %copy-done.9, bf16[960,128]{1,0:T(8,128)(2,1)S(1)} %get-tuple-element.31.rest_0_, ...), custom_call_target="tpu_custom_call" | custom-call | flops 2684354560 | bytes 4194304 | tf_op jit(solution)/shard_map/attend_own/pallas_call | solution.py:255
  90.7 0.0 copy-start.14
  90.7 0.0 copy-start.15
  90.7 0.0 copy-start
  90.7 0.6 collective-permute-start.6
  91.4 0.0 collective-permute-done.13.rest_4_
  91.4 0.0 collective-permute-start.7
  91.4 0.0 collective-permute-done.14.rest_5_
  91.4 2.9 %collective-permute-start.8 = (bf16[352,128]{1,0:T(8,128)(2,1)S(1)}, bf16[352,128]{1,0:T(8,128)(2,1)S(1)}, u32[]{:S(2)}, u32[]{:S(2)}) collective-permute-start(bf16[352,128]{1,0:T(8,128)(2,1)S(1)} %get-tuple-element.42), channel_id=1, source_target_pairs={{0,3},{1,2},{2,1},{3,0},{4,7},{5,6},{6,5},{7,4},{8,11},{9,10},{10,... | collective-permute-start | bytes 270344 | tf_op jit(solution)/shard_map/ppermute | solution.py:421
  94.3 0.0 collective-permute-done.15.rest_6_
  94.3 0.0 collective-permute-done.16.rest_7_
  94.3 1.9 %collective-permute-done.6.rest_1_ = bf16[352,128]{1,0:T(8,128)(2,1)S(1)} collective-permute-done((bf16[352,128]{1,0:T(8,128)(2,1)S(1)}, bf16[352,128]{1,0:T(8,128)(2,1)S(1)}, u32[]{:S(2)}, u32[]{:S(2)}) %collective-permute-start.6) | collective-permute-done | bytes 90144 | tf_op jit(solution)/shard_map/ppermute | solution.py:421
  96.3 0.0 collective-permute-done.7.rest_2_
  96.3 1.5 %collective-permute-done.8.rest_3_ = bf16[352,128]{1,0:T(8,128)(2,1)S(1)} collective-permute-done((bf16[352,128]{1,0:T(8,128)(2,1)S(1)}, bf16[352,128]{1,0:T(8,128)(2,1)S(1)}, u32[]{:S(2)}, u32[]{:S(2)}) %collective-permute-start.8) | collective-permute-done | bytes 90144 | tf_op jit(solution)/shard_map/ppermute | solution.py:421
  97.8 1.7 %project.1 = (f32[128,1280]{1,0:T(8,128)S(1)}, bf16[128,1280]{1,0:T(8,128)(2,1)S(1)}) custom-call(s32[1]{0:T(128)} %bitcast.place, bf16[128,1280]{1,0:T(8,128)(2,1)S(1)} %bitcast.6, f32[1,1280]{1,0:T(1,128)S(1)} %reshape.19.rate, bf16[1280,1280]{1,0:T(8,128)(2,1)S(1)} %copy-done.1, bf16[352,128]{1,0:T(8,128)(2,1)S(1)} %get-tuple-element.39.rest_0_, ...), custom_call_target="tpu_custom_call" | custom-call | flops 419430400 | bytes 3276800 | tf_op jit(solution)/shard_map/project/pallas_call | solution.py:309
  99.5 0.8 copy-done.7
  100.3 1.5 %collective-permute-start.19 = (bf16[128,1280]{1,0:T(8,128)(2,1)S(1)}, bf16[128,1280]{1,0:T(8,128)(2,1)S(1)}, u32[]{:S(2)}, u32[]{:S(2)}) collective-permute-start(bf16[128,1280]{1,0:T(8,128)(2,1)S(1)} %get-tuple-element.52.first), channel_id=1, source_target_pairs={{0,16},{8,24},{16,0},{24,8},{1,17},{9,25},{17,1},{25,9},{2,18},{10... | collective-permute-start | bytes 983048 | tf_op jit(solution)/shard_map/ppermute | solution.py:421
  101.9 5.5 %collective-permute-done.19.first = bf16[128,1280]{1,0:T(8,128)(2,1)S(1)} collective-permute-done((bf16[128,1280]{1,0:T(8,128)(2,1)S(1)}, bf16[128,1280]{1,0:T(8,128)(2,1)S(1)}, u32[]{:S(2)}, u32[]{:S(2)}) %collective-permute-start.19) | collective-permute-done | bytes 327712 | tf_op jit(solution)/shard_map/ppermute | solution.py:421
  107.4 0.0 collective-permute-start.20
  107.4 0.6 collective-permute-start.17
  108.0 1.0 collective-permute-done.20.second
  109.0 7.0 %mlp.3 = (f32[128,1280]{1,0:T(8,128)S(1)}, bf16[128,1280]{1,0:T(8,128)(2,1)S(1)}) custom-call(bf16[128,1280]{1,0:T(8,128)(2,1)S(1)} %collective-permute-done.19.first, bf16[128,1280]{1,0:T(8,128)(2,1)S(1)} %collective-permute-done.20.second, bf16[1280,1280]{1,0:T(8,128)(2,1)S(1)} %copy-done, bf16[1280,1280]{1,0:T(8,128)(2,1)} %w_gate.3, ...), custom_call_target="tpu_custom_call" | custom-call | flops 2516582400 | bytes 9830400 | tf_op jit(solution)/shard_map/mlp/pallas_call | solution.py:362
  116.1 0.8 copy-done.4
  116.9 0.1 collective-permute-start.21
  117.1 7.0 %mlp.2 = (f32[128,1280]{1,0:T(8,128)S(1)}, bf16[128,1280]{1,0:T(8,128)(2,1)S(1)}) custom-call(bf16[128,1280]{1,0:T(8,128)(2,1)S(1)} %get-tuple-element.52.first, bf16[128,1280]{1,0:T(8,128)(2,1)S(1)} %collective-permute-done.17.second, bf16[1280,1280]{1,0:T(8,128)(2,1)S(1)} %copy-done, bf16[1280,1280]{1,0:T(8,128)(2,1)} %w_gate.3, ...), custom_call_target="tpu_custom_call" | custom-call | flops 2516582400 | bytes 9830400 | tf_op jit(solution)/shard_map/mlp/pallas_call | solution.py:362
  124.1 0.9 copy-done.8
  125.0 0.4 collective-permute-start.18
  125.4 0.7 copy-done.10
  126.1 2.0 %add_partials.1 = bf16[128,1280]{1,0:T(8,128)(2,1)} custom-call(f32[128,1280]{1,0:T(8,128)} %copy-done.4, bf16[128,1280]{1,0:T(8,128)(2,1)} %copy-done.10), custom_call_target="tpu_custom_call" | custom-call | flops 163840 | bytes 1310720 | tf_op jit(solution)/shard_map/add_partials/pallas_call | solution.py:388
  128.1 1.5 %collective-permute-start.22 = (bf16[128,1280]{1,0:T(8,128)(2,1)}, bf16[128,1280]{1,0:T(8,128)(2,1)S(1)}, u32[]{:S(2)}, u32[]{:S(2)}) collective-permute-start(bf16[128,1280]{1,0:T(8,128)(2,1)} %add_partials.1), channel_id=1, source_target_pairs={{0,16},{8,24},{16,0},{24,8},{1,17},{9,25},{17,1},{25,9},{2,18},{10... | collective-permute-start | bytes 983048 | tf_op jit(solution)/shard_map/ppermute | solution.py:421
  129.6 0.6 reshape.21.rate
  130.2 0.0 collective-permute-done.18.rest_0_
  130.2 7.8 %collective-permute-done.22.rest_1_ = bf16[128,1280]{1,0:T(8,128)(2,1)S(1)} collective-permute-done((bf16[128,1280]{1,0:T(8,128)(2,1)}, bf16[128,1280]{1,0:T(8,128)(2,1)S(1)}, u32[]{:S(2)}, u32[]{:S(2)}) %collective-permute-start.22) | collective-permute-done | bytes 327712 | tf_op jit(solution)/shard_map/ppermute | solution.py:421
  138.0 0.7 copy-done.12
  138.8 2.6 %finish.1 = bf16[128,1280]{1,0:T(8,128)(2,1)} custom-call(f32[128,1280]{1,0:T(8,128)} %copy-done.7, f32[1,1280]{1,0:T(1,128)} %reshape.21.rate, f32[128,1280]{1,0:T(8,128)} %copy-done.8, bf16[128,1280]{1,0:T(8,128)(2,1)} %copy-done.11, bf16[128,1280]{1,0:T(8,128)(2,1)} %copy-done.12), custom_call_target="tpu_custom_call" | custom-call | flops 1638400 | bytes 1966080 | tf_op jit(solution)/shard_map/finish/pallas_call | solution.py:409
  (30 shorter events, 0.1 us)
Async XLA Ops:
  0.7 1.0 copy-start.2
  1.7 17.9 %copy-start.5 = (bf16[1,256,1280]{2,1,0:T(8,128)(2,1)S(1)}, bf16[1,256,1280]{2,1,0:T(8,128)(2,1)}, u32[]{:S(2)}) copy-start(bf16[1,256,1280]{2,1,0:T(8,128)(2,1)} %param.16) | copy-start | bytes 1966084
  1.7 17.9 %copy-start.6 = (bf16[1,256,1280]{2,1,0:T(8,128)(2,1)S(1)}, bf16[1,256,1280]{2,1,0:T(8,128)(2,1)}, u32[]{:S(2)}) copy-start(bf16[1,256,1280]{2,1,0:T(8,128)(2,1)} %param.17) | copy-start | bytes 1966084
  1.7 52.9 %copy-start.9 = (s32[1,16]{1,0:T(1,128)S(1)}, s32[1,16]{1,0:T(1,128)}, u32[]{:S(2)}) copy-start(s32[1,16]{1,0:T(1,128)} %lengths.3) | copy-start | bytes 196
  9.3 20.8 %collective-permute-start = (bf16[960,128]{1,0:T(8,128)(2,1)S(1)}, bf16[960,128]{1,0:T(8,128)(2,1)S(1)}, u32[]{:S(2)}, u32[]{:S(2)}) collective-permute-start(bf16[960,128]{1,0:T(8,128)(2,1)S(1)} %get-tuple-element.32), channel_id=1, source_target_pairs={{0,1},{1,0},{2,3},{3,2},{4,5},{5,4},{6,7},{7,6},{8,9},{9,8},{10,11... | collective-permute-start | bytes 737288 | tf_op jit(solution)/shard_map/ppermute | solution.py:421
  12.3 13.2 %collective-permute-start.10 = (bf16[320,128]{1,0:T(8,128)(2,1)S(1)}, bf16[320,128]{1,0:T(8,128)(2,1)S(1)}, u32[]{:S(2)}, u32[]{:S(2)}) collective-permute-start(bf16[320,128]{1,0:T(8,128)(2,1)S(1)} %get-tuple-element.44), channel_id=1, source_target_pairs={{0,5},{1,4},{2,7},{3,6},{4,1},{5,0},{6,3},{7,2},{8,13},{9,12},{10,... | collective-permute-start | bytes 245768 | tf_op jit(solution)/shard_map/ppermute | solution.py:421
  14.9 10.7 %collective-permute-start.11 = (bf16[320,128]{1,0:T(8,128)(2,1)S(1)}, bf16[320,128]{1,0:T(8,128)(2,1)S(1)}, u32[]{:S(2)}, u32[]{:S(2)}) collective-permute-start(bf16[320,128]{1,0:T(8,128)(2,1)S(1)} %get-tuple-element.45), channel_id=1, source_target_pairs={{0,6},{1,7},{2,4},{3,5},{4,2},{5,3},{6,0},{7,1},{8,14},{9,15},{10,... | collective-permute-start | bytes 245768 | tf_op jit(solution)/shard_map/ppermute | solution.py:421
  16.2 10.6 %collective-permute-start.12 = (bf16[320,128]{1,0:T(8,128)(2,1)S(1)}, bf16[320,128]{1,0:T(8,128)(2,1)S(1)}, u32[]{:S(2)}, u32[]{:S(2)}) collective-permute-start(bf16[320,128]{1,0:T(8,128)(2,1)S(1)} %get-tuple-element.46), channel_id=1, source_target_pairs={{0,7},{1,6},{2,5},{3,4},{4,3},{5,2},{6,1},{7,0},{8,15},{9,14},{10,... | collective-permute-start | bytes 245768 | tf_op jit(solution)/shard_map/ppermute | solution.py:421
  19.6 10.0 %collective-permute-start.9 = (bf16[320,128]{1,0:T(8,128)(2,1)S(1)}, bf16[320,128]{1,0:T(8,128)(2,1)S(1)}, u32[]{:S(2)}, u32[]{:S(2)}) collective-permute-start(bf16[320,128]{1,0:T(8,128)(2,1)S(1)} %get-tuple-element.43), channel_id=1, source_target_pairs={{0,4},{1,5},{2,6},{3,7},{4,0},{5,1},{6,2},{7,3},{8,12},{9,13},{10,... | collective-permute-start | bytes 245768 | tf_op jit(solution)/shard_map/ppermute | solution.py:421
  25.5 29.0 %collective-permute-start.3 = (bf16[640,256]{1,0:T(8,128)(2,1)S(1)}, bf16[640,256]{1,0:T(8,128)(2,1)S(1)}, u32[]{:S(2)}, u32[]{:S(2)}) collective-permute-start(bf16[640,256]{1,0:T(8,128)(2,1)S(1)} %get-tuple-element.36), channel_id=1, source_target_pairs={{0,1},{1,0},{2,3},{3,2},{4,5},{5,4},{6,7},{7,6},{8,9},{9,8},{10,11... | collective-permute-start | bytes 983048 | tf_op jit(solution)/shard_map/ppermute | solution.py:421
  25.5 29.0 %collective-permute-start.4 = (bf16[640,256]{1,0:T(8,128)(2,1)S(1)}, bf16[640,256]{1,0:T(8,128)(2,1)S(1)}, u32[]{:S(2)}, u32[]{:S(2)}) collective-permute-start(bf16[640,256]{1,0:T(8,128)(2,1)S(1)} %get-tuple-element.37), channel_id=1, source_target_pairs={{0,2},{1,3},{2,0},{3,1},{4,6},{5,7},{6,4},{7,5},{8,10},{9,11},{10,... | collective-permute-start | bytes 983048 | tf_op jit(solution)/shard_map/ppermute | solution.py:421
  26.8 27.7 %collective-permute-start.5 = (bf16[640,256]{1,0:T(8,128)(2,1)S(1)}, bf16[640,256]{1,0:T(8,128)(2,1)S(1)}, u32[]{:S(2)}, u32[]{:S(2)}) collective-permute-start(bf16[640,256]{1,0:T(8,128)(2,1)S(1)} %get-tuple-element.38), channel_id=1, source_target_pairs={{0,3},{1,2},{2,1},{3,0},{4,7},{5,6},{6,5},{7,4},{8,11},{9,10},{10,... | collective-permute-start | bytes 983048 | tf_op jit(solution)/shard_map/ppermute | solution.py:421
  29.6 19.4 %collective-permute-start.1 = (bf16[960,128]{1,0:T(8,128)(2,1)S(1)}, bf16[960,128]{1,0:T(8,128)(2,1)S(1)}, u32[]{:S(2)}, u32[]{:S(2)}) collective-permute-start(bf16[960,128]{1,0:T(8,128)(2,1)S(1)} %get-tuple-element.33), channel_id=1, source_target_pairs={{0,2},{1,3},{2,0},{3,1},{4,6},{5,7},{6,4},{7,5},{8,10},{9,11},{10,... | collective-permute-start | bytes 737288 | tf_op jit(solution)/shard_map/ppermute | solution.py:421
  30.1 24.4 %collective-permute-start.2 = (bf16[960,128]{1,0:T(8,128)(2,1)S(1)}, bf16[960,128]{1,0:T(8,128)(2,1)S(1)}, u32[]{:S(2)}, u32[]{:S(2)}) collective-permute-start(bf16[960,128]{1,0:T(8,128)(2,1)S(1)} %get-tuple-element.34), channel_id=1, source_target_pairs={{0,3},{1,2},{2,1},{3,0},{4,7},{5,6},{6,5},{7,4},{8,11},{9,10},{10,... | collective-permute-start | bytes 737288 | tf_op jit(solution)/shard_map/ppermute | solution.py:421
  67.3 24.1 %collective-permute-start.13 = (bf16[352,128]{1,0:T(8,128)(2,1)S(1)}, bf16[352,128]{1,0:T(8,128)(2,1)S(1)}, u32[]{:S(2)}, u32[]{:S(2)}) collective-permute-start(bf16[352,128]{1,0:T(8,128)(2,1)S(1)} %get-tuple-element.47), channel_id=1, source_target_pairs={{0,4},{1,5},{2,6},{3,7},{4,0},{5,1},{6,2},{7,3},{8,12},{9,13},{10,... | collective-permute-start | bytes 270344 | tf_op jit(solution)/shard_map/ppermute | solution.py:421
  68.8 22.5 %collective-permute-start.14 = (bf16[352,128]{1,0:T(8,128)(2,1)S(1)}, bf16[352,128]{1,0:T(8,128)(2,1)S(1)}, u32[]{:S(2)}, u32[]{:S(2)}) collective-permute-start(bf16[352,128]{1,0:T(8,128)(2,1)S(1)} %get-tuple-element.48), channel_id=1, source_target_pairs={{0,5},{1,4},{2,7},{3,6},{4,1},{5,0},{6,3},{7,2},{8,13},{9,12},{10,... | collective-permute-start | bytes 270344 | tf_op jit(solution)/shard_map/ppermute | solution.py:421
  70.3 24.0 %collective-permute-start.15 = (bf16[352,128]{1,0:T(8,128)(2,1)S(1)}, bf16[352,128]{1,0:T(8,128)(2,1)S(1)}, u32[]{:S(2)}, u32[]{:S(2)}) collective-permute-start(bf16[352,128]{1,0:T(8,128)(2,1)S(1)} %get-tuple-element.49), channel_id=1, source_target_pairs={{0,6},{1,7},{2,4},{3,5},{4,2},{5,3},{6,0},{7,1},{8,14},{9,15},{10,... | collective-permute-start | bytes 270344 | tf_op jit(solution)/shard_map/ppermute | solution.py:421
  73.7 20.6 %copy-start.13 = (f32[1280]{0:T(1024)S(1)}, f32[1280]{0:T(1024)}, u32[]{:S(2)}) copy-start(f32[1280]{0:T(1024)} %param.21) | copy-start | bytes 15364
  73.7 24.1 %copy-start.1 = (bf16[1280,1280]{1,0:T(8,128)(2,1)S(1)}, bf16[1280,1280]{1,0:T(8,128)(2,1)}, u32[]{:S(2)}) copy-start(bf16[1280,1280]{1,0:T(8,128)(2,1)} %w_hbm.1) | copy-start | bytes 9830404
  73.7 24.1 %copy-start.3 = (bf16[1,128,1280]{2,1,0:T(8,128)(2,1)S(1)}, bf16[1,128,1280]{2,1,0:T(8,128)(2,1)}, u32[]{:S(2)}) copy-start(bf16[1,128,1280]{2,1,0:T(8,128)(2,1)} %param.14) | copy-start | bytes 983044
  73.7 20.7 %collective-permute-start.16 = (bf16[352,128]{1,0:T(8,128)(2,1)S(1)}, bf16[352,128]{1,0:T(8,128)(2,1)S(1)}, u32[]{:S(2)}, u32[]{:S(2)}) collective-permute-start(bf16[352,128]{1,0:T(8,128)(2,1)S(1)} %get-tuple-element.50), channel_id=1, source_target_pairs={{0,7},{1,6},{2,5},{3,4},{4,3},{5,2},{6,1},{7,0},{8,15},{9,14},{10,... | collective-permute-start | bytes 270344 | tf_op jit(solution)/shard_map/ppermute | solution.py:421
  90.7 16.7 %copy-start.14 = (f32[1280]{0:T(1024)S(1)}, f32[1280]{0:T(1024)}, u32[]{:S(2)}) copy-start(f32[1280]{0:T(1024)} %param.25) | copy-start | bytes 15364
  90.7 16.7 %copy-start.15 = (f32[1280]{0:T(1024)S(1)}, f32[1280]{0:T(1024)}, u32[]{:S(2)}) copy-start(f32[1280]{0:T(1024)} %param.26) | copy-start | bytes 15364
  90.7 18.3 %copy-start = (bf16[1280,1280]{1,0:T(8,128)(2,1)S(1)}, bf16[1280,1280]{1,0:T(8,128)(2,1)}, u32[]{:S(2)}) copy-start(bf16[1280,1280]{1,0:T(8,128)(2,1)} %w_up.3) | copy-start | bytes 9830404
  90.7 5.5 %collective-permute-start.6 = (bf16[352,128]{1,0:T(8,128)(2,1)S(1)}, bf16[352,128]{1,0:T(8,128)(2,1)S(1)}, u32[]{:S(2)}, u32[]{:S(2)}) collective-permute-start(bf16[352,128]{1,0:T(8,128)(2,1)S(1)} %get-tuple-element.40), channel_id=1, source_target_pairs={{0,1},{1,0},{2,3},{3,2},{4,5},{5,4},{6,7},{7,6},{8,9},{9,8},{10,11... | collective-permute-start | bytes 270344 | tf_op jit(solution)/shard_map/ppermute | solution.py:421
  91.4 4.9 %collective-permute-start.7 = (bf16[352,128]{1,0:T(8,128)(2,1)S(1)}, bf16[352,128]{1,0:T(8,128)(2,1)S(1)}, u32[]{:S(2)}, u32[]{:S(2)}) collective-permute-start(bf16[352,128]{1,0:T(8,128)(2,1)S(1)} %get-tuple-element.41), channel_id=1, source_target_pairs={{0,2},{1,3},{2,0},{3,1},{4,6},{5,7},{6,4},{7,5},{8,10},{9,11},{10,... | collective-permute-start | bytes 270344 | tf_op jit(solution)/shard_map/ppermute | solution.py:421
  91.4 6.4 %collective-permute-start.8 = (bf16[352,128]{1,0:T(8,128)(2,1)S(1)}, bf16[352,128]{1,0:T(8,128)(2,1)S(1)}, u32[]{:S(2)}, u32[]{:S(2)}) collective-permute-start(bf16[352,128]{1,0:T(8,128)(2,1)S(1)} %get-tuple-element.42), channel_id=1, source_target_pairs={{0,3},{1,2},{2,1},{3,0},{4,7},{5,6},{6,5},{7,4},{8,11},{9,10},{10,... | collective-permute-start | bytes 270344 | tf_op jit(solution)/shard_map/ppermute | solution.py:421
  99.5 0.8 copy-start.7
  100.3 7.1 %collective-permute-start.19 = (bf16[128,1280]{1,0:T(8,128)(2,1)S(1)}, bf16[128,1280]{1,0:T(8,128)(2,1)S(1)}, u32[]{:S(2)}, u32[]{:S(2)}) collective-permute-start(bf16[128,1280]{1,0:T(8,128)(2,1)S(1)} %get-tuple-element.52.first), channel_id=1, source_target_pairs={{0,16},{8,24},{16,0},{24,8},{1,17},{9,25},{17,1},{25,9},{2,18},{10... | collective-permute-start | bytes 983048 | tf_op jit(solution)/shard_map/ppermute | solution.py:421
  107.4 1.6 %collective-permute-start.20 = (bf16[128,1280]{1,0:T(8,128)(2,1)S(1)}, bf16[128,1280]{1,0:T(8,128)(2,1)S(1)}, u32[]{:S(2)}, u32[]{:S(2)}) collective-permute-start(bf16[128,1280]{1,0:T(8,128)(2,1)S(1)} %collective-permute-done.19.first), channel_id=1, source_target_pairs={{0,8},{8,0},{16,24},{24,16},{1,9},{9,1},{17,25},{25,17},{2,10},{10... | collective-permute-start | bytes 983048 | tf_op jit(solution)/shard_map/ppermute | solution.py:421
  107.4 9.6 %collective-permute-start.17 = (bf16[128,1280]{1,0:T(8,128)(2,1)S(1)}, bf16[128,1280]{1,0:T(8,128)(2,1)S(1)}, u32[]{:S(2)}, u32[]{:S(2)}) collective-permute-start(bf16[128,1280]{1,0:T(8,128)(2,1)S(1)} %get-tuple-element.52.first), channel_id=1, source_target_pairs={{0,8},{8,0},{16,24},{24,16},{1,9},{9,1},{17,25},{25,17},{2,10},{10... | collective-permute-start | bytes 983048 | tf_op jit(solution)/shard_map/ppermute | solution.py:421
  116.1 0.8 copy-start.4
  116.9 12.7 %copy-start.16 = (f32[1280]{0:T(1024)S(1)}, f32[1280]{0:T(1024)}, u32[]{:S(2)}) copy-start(f32[1280]{0:T(1024)} %param.27) | copy-start | bytes 15364
  116.9 8.4 %collective-permute-start.21 = (bf16[128,1280]{1,0:T(8,128)(2,1)S(1)}, bf16[128,1280]{1,0:T(8,128)(2,1)S(1)}, u32[]{:S(2)}, u32[]{:S(2)}) collective-permute-start(bf16[128,1280]{1,0:T(8,128)(2,1)S(1)} %get-tuple-element.56), channel_id=1, source_target_pairs={{0,8},{8,0},{16,24},{24,16},{1,9},{9,1},{17,25},{25,17},{2,10},{10... | collective-permute-start | bytes 983048 | tf_op jit(solution)/shard_map/ppermute | solution.py:421
  124.1 0.9 copy-start.8
  125.0 5.2 %collective-permute-start.18 = (bf16[128,1280]{1,0:T(8,128)(2,1)S(1)}, bf16[128,1280]{1,0:T(8,128)(2,1)S(1)}, u32[]{:S(2)}, u32[]{:S(2)}) collective-permute-start(bf16[128,1280]{1,0:T(8,128)(2,1)S(1)} %get-tuple-element.54), channel_id=1, source_target_pairs={{0,8},{8,0},{16,24},{24,16},{1,9},{9,1},{17,25},{25,17},{2,10},{10... | collective-permute-start | bytes 983048 | tf_op jit(solution)/shard_map/ppermute | solution.py:421
  125.4 0.7 copy-start.10
  128.1 10.0 %collective-permute-start.22 = (bf16[128,1280]{1,0:T(8,128)(2,1)}, bf16[128,1280]{1,0:T(8,128)(2,1)S(1)}, u32[]{:S(2)}, u32[]{:S(2)}) collective-permute-start(bf16[128,1280]{1,0:T(8,128)(2,1)} %add_partials.1), channel_id=1, source_target_pairs={{0,16},{8,24},{16,0},{24,8},{1,17},{9,25},{17,1},{25,9},{2,18},{10... | collective-permute-start | bytes 983048 | tf_op jit(solution)/shard_map/ppermute | solution.py:421
  130.2 7.8 %copy-start.11 = (bf16[128,1280]{1,0:T(8,128)(2,1)}, bf16[128,1280]{1,0:T(8,128)(2,1)S(1)}, u32[]{:S(2)}) copy-start(bf16[128,1280]{1,0:T(8,128)(2,1)S(1)} %collective-permute-done.18.rest_0_) | copy-start | bytes 983044
  138.0 0.7 copy-start.12

commit v2 on v0

v2 whole, which is shorter than its diff:
```python
import functools
import math

import jax
import jax.numpy as jnp
from jax import lax
from jax.experimental import pallas as pl
from jax.experimental.pallas import tpu as pltpu
from jax.sharding import PartitionSpec as P

D = 1280
HEADS = 20
HEAD = 64
EPS = 1e-06
SQ = 4
HQ = HEADS // SQ
QD = HQ * HEAD
LSE = 16
NEG = -1e30
MIB = 1 << 20

f32 = jnp.float32
bf16 = jnp.bfloat16


def unit(vector):
    return vector * lax.rsqrt(jnp.sum(vector * vector, axis=-1, keepdims=True) + EPS)


def head_unit_t(block, scale):
    dims, rows = block.shape
    per_head = block.reshape(dims // HEAD, HEAD, rows)
    total = jnp.sum(per_head * per_head, axis=1, keepdims=True)
    return (per_head * lax.rsqrt(total + EPS)).reshape(dims, rows) * scale


def params(limit):
    return pltpu.CompilerParams(vmem_limit_bytes=limit * MIB)


def vmem():
    return pl.BlockSpec(memory_space=pltpu.VMEM)


def hbm():
    return pl.BlockSpec(memory_space=pltpu.HBM)


def fetch(sources, targets, sems):
    copies = [
        pltpu.make_async_copy(a, b, sems.at[n]) for n, (a, b) in enumerate(zip(sources, targets))
    ]
    for copy in copies:
        copy.start()
    return copies


def wait(copies):
    for copy in copies:
        copy.wait()


def fetched(*arrays):
    return [pltpu.VMEM(a.shape, a.dtype) for a in arrays] + [
        pltpu.SemaphoreType.DMA((len(arrays),))
    ]


def over_rows(vector, rows):
    tiles = [
        jnp.broadcast_to(vector[c * 128 : (c + 1) * 128], (rows, 128))
        for c in range(vector.shape[0] // 128)
    ]
    return jnp.concatenate(tiles, axis=1)


def smem():
    return pl.BlockSpec(memory_space=pltpu.SMEM)


def cost(flops, nbytes, trans=0):
    return pl.CostEstimate(flops=int(flops), bytes_accessed=int(nbytes), transcendentals=int(trans))


def prefix_kernel(place, *rest):
    outs, rest, sources = rest[4 : 4 + SQ], rest[4 + SQ :], rest[:4]
    hidden, columns, parts, scale, keys, values, tokens, sems = rest
    copies = fetch(sources, (scale, keys, values, tokens), sems)
    rows = keys.shape[0]
    wait(copies[:2])
    for c in range(D // 128):
        cols = slice(c * 128, (c + 1) * 128)
        columns[c] = jnp.broadcast_to(scale[cols], (128, 128)).T
        scale_t = jnp.concatenate([columns[c]] * (rows // 128), axis=1)
        split(parts, 0, c, head_unit_t(keys[:, cols].T.astype(f32), scale_t).astype(bf16))
    wait(copies[2:])
    for c in range(D // 128):
        split(parts, QD, c, values[:, c * 128 : (c + 1) * 128].T)
    i = lax.rem(place[0], SQ)
    for m in range(SQ):
        outs[m][...] = parts[jnp.bitwise_xor(i, m)]
    hidden[...] = unit(tokens[...].astype(f32)).astype(bf16)


def split(out, base, c, block):
    for part in range(0, 128, HEAD):
        row = c * 128 + part
        at = base + row % QD
        out[row // QD, at : at + HEAD, :] = block[part : part + HEAD, :]


def prefix_call(place, scale, keys, values, tokens):
    rows = keys.shape[0]
    return pl.pallas_call(
        prefix_kernel,
        out_shape=[jax.ShapeDtypeStruct((2 * QD, rows), bf16)] * SQ
        + [
            jax.ShapeDtypeStruct(tokens.shape, bf16),
            jax.ShapeDtypeStruct((D // 128, 128, 128), f32),
        ],
        in_specs=[smem()] + [hbm()] * 4,
        out_specs=[vmem()] * (SQ + 2),
        scratch_shapes=[pltpu.VMEM((SQ, 2 * QD, rows), bf16)]
        + fetched(scale, keys, values, tokens),
        compiler_params=params(6),
        cost_estimate=cost(5e10, 4 * rows * D * 2),
        name="prefix_prep",
    )(place, scale, keys, values, tokens)


def qkv_kernel(squares, place, hidden, columns, w_hbm, queries, *rest):
    outs, (parts, weights, w_sems) = rest[:SQ], rest[SQ:]
    spans = [pl.ds(p * D, D) for p in range(3)]
    copies = fetch([w_hbm.at[:, p] for p in spans], [weights.at[:, p] for p in spans], w_sems)
    rows = hidden.shape[0]
    for part in range(3):
        copies[part].wait()
        out = jnp.dot(hidden[...], weights[:, part * D : (part + 1) * D], preferred_element_type=f32)
        for c in range(D // 128):
            block = out[:, c * 128 : (c + 1) * 128].T
            if part < 2:
                block = head_unit_t(block, columns[c, :, :rows])
            if part == 0:
                block = (block * math.sqrt(HEAD)).astype(bf16)
                for s in range(squares):
                    queries[s * D + c * 128 : s * D + (c + 1) * 128, :] = block
            else:
                split(parts, (part - 1) * QD, c, block.astype(bf16))
    i = lax.rem(place[0], SQ)
    for m in range(SQ):
        outs[m][...] = parts[jnp.bitwise_xor(i, m)]


def qkv_call(squares, place, hidden, columns, weights):
    rows = hidden.shape[0]
    pair = jax.ShapeDtypeStruct((2 * QD, rows), bf16)
    return pl.pallas_call(
        functools.partial(qkv_kernel, squares),
        out_shape=[jax.ShapeDtypeStruct((squares * D, rows), bf16)] + [pair] * SQ,
        in_specs=[smem(), vmem(), vmem(), hbm()],
        out_specs=[vmem()] * (1 + SQ),
        scratch_shapes=[
            pltpu.VMEM((SQ, 2 * QD, rows), bf16),
            pltpu.VMEM((D, 3 * D), bf16),
            pltpu.SemaphoreType.DMA((3,)),
        ],
        compiler_params=params(14),
        cost_estimate=cost(5e10, 3 * D * D * 2),
        name="qkv",
    )(place, hidden, columns, weights)


def pack_kernel(*refs):
    parts, (keys, values) = refs[:SQ], refs[SQ:]
    span = parts[0].shape[1]
    for n, part in enumerate(parts):
        at = slice(n * span, (n + 1) * span)
        for h in range(HQ):
            keys[h, at, :] = part[h * HEAD : (h + 1) * HEAD, :].T
        values[:, at] = part[QD:, :]


PACK_COST = 20e9


def pack_call(parts):
    span = parts[0].shape[1]
    return pl.pallas_call(
        pack_kernel,
        out_shape=[
            jax.ShapeDtypeStruct((HQ, SQ * span, HEAD), bf16),
            jax.ShapeDtypeStruct((QD, SQ * span), bf16),
        ],
        in_specs=[vmem()] * SQ,
        out_specs=[vmem()] * 2,
        compiler_params=params(2),
        cost_estimate=cost(PACK_COST, 0),
        name="pack",
    )(*parts)


def cached_kernel(query_all, keys, values, accum, stats, query):
    extent, _, rows = query_all.shape
    for s in range(extent // SQ):
        for j in range(SQ):
            query[:, j * rows : (j + 1) * rows] = query_all[s * SQ + j]
        for h in range(HQ):
            head = slice(h * HEAD, (h + 1) * HEAD)
            score = jnp.dot(keys[h], query[head, :], preferred_element_type=f32)
            top = jnp.max(score, axis=0, keepdims=True)
            weights = jnp.exp(score - top)
            total = jnp.sum(weights, axis=0, keepdims=True)
            blended = jnp.dot(values[head, :], weights.astype(bf16), preferred_element_type=f32)
            accum[s, head, :] = blended
            stats[s, h : h + 1, :] = top
            stats[s, 8 + h : 9 + h, :] = total


def cached_call(queries, keys, values):
    extent, _, rows = queries.shape
    pairs = extent * rows * keys.shape[1] * HQ
    return pl.pallas_call(
        cached_kernel,
        out_shape=[
            jax.ShapeDtypeStruct((extent // SQ, QD, SQ * rows), f32),
            jax.ShapeDtypeStruct((extent // SQ, 16, SQ * rows), f32),
        ],
        in_specs=[vmem()] * 3,
        out_specs=[vmem()] * 2,
        scratch_shapes=[pltpu.VMEM((QD, SQ * rows), bf16)],
        compiler_params=params(12),
        cost_estimate=cost(CACHED_COST, 0, 0),
        name="attend_cached",
    )(queries, keys, values)


CACHED_COST = 1e9


def widen(part, lanes, width, fill):
    rows = part.shape[0]
    pieces = []
    if lanes.start:
        pieces.append(jnp.full((rows, lanes.start), fill, f32))
    pieces.append(part)
    if lanes.stop < width:
        pieces.append(jnp.full((rows, width - lanes.stop), fill, f32))
    return jnp.concatenate(pieces, axis=1)


def suffix_kernel(place, lengths, query_all, accum, stats, *rest):
    suffix, (w_hbm, outs, w_out, pairs, lse, sems) = rest[:SQ], rest[SQ:]
    copies = fetch([w_hbm], [w_out], sems)
    extent, _, rows = query_all.shape
    i = lax.rem(place[0], SQ)
    square = lax.div(place[0], SQ)
    width = SQ * rows
    for m in range(SQ):
        pairs[jnp.bitwise_xor(i, m)] = suffix[m][...]
    lse[...] = jnp.zeros_like(lse)
    for shift in range(extent // SQ):
        query_square = jnp.bitwise_xor(square, shift)
        position = query_square * width + lax.broadcasted_iota(jnp.int32, (1, width), 1)
        first = jnp.zeros((1, width), jnp.int32)
        bound = jnp.int32(0)
        for r in range(lengths.shape[1]):
            bound = bound + lengths[0, r]
            first = jnp.where(position >= bound, bound, first)
        windows = [(SQ - 2, 0, 1), (SQ - 1, 0, 2)]
        if not shift:
            windows = [(j, j, min(SQ, j + 3)) for j in range(SQ)]
        masks = []
        for block, begin, end in windows:
            lanes = slice(begin * rows, end * rows)
            key_at = (square * SQ + block) * rows + lax.broadcasted_iota(
                jnp.int32, (rows, lanes.stop - lanes.start), 0
            )
            masks.append((key_at >= first[:, lanes]) & (key_at <= position[:, lanes]))
        for h in range(HQ):
            head = slice(h * HEAD, (h + 1) * HEAD)
            head_v = slice(QD + h * HEAD, QD + (h + 1) * HEAD)
            query = [query_all[query_square * SQ + j, head, :] for j in range(windows[-1][2])]
            cached_top = stats[query_square, h : h + 1, :]
            top = cached_top
            pieces = []
            for (block, begin, end), mask in zip(windows, masks):
                lanes = slice(begin * rows, end * rows)
                score = jnp.dot(
                    pairs[block, head, :].T,
                    jnp.concatenate(query[begin:end], axis=1),
                    preferred_element_type=f32,
                )
                score = jnp.where(mask, score, NEG)
                level = jnp.max(score, axis=0, keepdims=True)
                top = jnp.maximum(top, widen(level, lanes, width, NEG))
                pieces.append((score, block, lanes))
            shrink = jnp.exp(cached_top - top)
            total = stats[query_square, 8 + h : 9 + h, :] * shrink
            mixed = accum[query_square, head, :] * shrink
            for score, block, lanes in pieces:
                weights = jnp.exp(score - top[:, lanes])
                total = total + widen(jnp.sum(weights, axis=0, keepdims=True), lanes, width, 0.0)
                blended = jnp.dot(
                    pairs[block, head_v, :], weights.astype(bf16), preferred_element_type=f32
                )
                mixed = mixed + widen(blended, lanes, width, 0.0)
            out = (mixed * (1.0 / total)).astype(bf16)
            for j in range(SQ):
                outs[query_square * SQ + j, head, :] = out[:, j * rows : (j + 1) * rows]
            level = top + jnp.log(total)
            high = level.astype(bf16).astype(f32)
            middle = (level - high).astype(bf16).astype(f32)
            for n, piece in enumerate((high, middle, level - high - middle)):
                lse[n * HQ + h : n * HQ + h + 1, :] = piece
        for j in range(SQ):
            outs[query_square * SQ + j, QD:, :] = lse[:, j * rows : (j + 1) * rows].astype(bf16)
    wait(copies)


def suffix_call(place, lengths, queries, accum, stats, suffix, w_out):
    extent, _, rows = queries.shape
    return pl.pallas_call(
        suffix_kernel,
        out_shape=[
            jax.ShapeDtypeStruct((extent, QD + LSE, rows), bf16),
            jax.ShapeDtypeStruct(w_out.shape, bf16),
        ],
        in_specs=[smem(), smem()] + [vmem()] * (3 + SQ) + [hbm()],
        out_specs=[vmem()] * 2,
        scratch_shapes=[
            pltpu.VMEM((SQ, 2 * QD, rows), bf16),
            pltpu.VMEM((LSE, SQ * rows), f32),
            pltpu.SemaphoreType.DMA((1,)),
        ],
        compiler_params=params(8),
        cost_estimate=cost(2e10, 8 * MIB, 0),
        name="attend_suffix",
    )(place, lengths, queries, accum, stats, *suffix, w_out)


def project_kernel(tokens_hbm, rate_hbm, w_out, parts, hidden_out, flat_out, mix, *rest):
    tokens, rate, sems = rest
    copies = fetch((tokens_hbm, rate_hbm), (tokens, rate), sems)
    squares = parts.shape[0] // SQ
    for j in range(SQ):
        group = [parts.at[s * SQ + j] for s in range(squares)]
        levels = []
        for part in group:
            pieces = part[QD:, :].astype(f32)
            levels.append(pieces[:HQ] + pieces[HQ : 2 * HQ] + pieces[2 * HQ : 3 * HQ])
        top = functools.reduce(jnp.maximum, levels)
        weights = [jnp.exp(v - top) for v in levels]
        inverse = 1.0 / functools.reduce(jnp.add, weights)
        weights = [w * inverse for w in weights]
        for h in range(HQ):
            head = slice(h * HEAD, (h + 1) * HEAD)
            mixed = functools.reduce(
                jnp.add, [w[h : h + 1, :] * p[head, :].astype(f32) for w, p in zip(weights, group)]
            )
            at = j * QD + h * HEAD
            mix[at : at + HEAD, :] = mixed.astype(bf16)
    wait(copies)
    hidden = unit(tokens[...].astype(f32))
    attn = jnp.concatenate(
        [mix[c * 128 : (c + 1) * 128, :].astype(f32).T.astype(bf16) for c in range(D // 128)], axis=1
    )
    attended = unit(jnp.dot(attn, w_out[...], preferred_element_type=f32))
    hidden = unit(hidden + over_rows(rate, hidden.shape[0]) * (attended - hidden))
    hidden_out[...] = hidden
    flat_out[...] = hidden.astype(bf16)


def project_call(tokens, rate, w_out, parts):
    rows = tokens.shape[0]
    return pl.pallas_call(
        project_kernel,
        out_shape=[jax.ShapeDtypeStruct((rows, D), f32), jax.ShapeDtypeStruct((rows, D), bf16)],
        in_specs=[hbm(), hbm(), vmem(), vmem()],
        out_specs=[vmem()] * 2,
        scratch_shapes=[pltpu.VMEM((D, rows), bf16)] + fetched(tokens, rate),
        compiler_params=params(8),
        cost_estimate=cost(2 * rows * D * D, D * D * 2),
        name="project",
    )(tokens, rate, w_out, parts)


def feed(first, second, w_up, w_gate, w_down, up_scale, gate_scale, keep, send):
    rows = first.shape[0]
    data = jnp.concatenate([first[...], second[...]], axis=0)
    up = jnp.dot(data, w_up(), preferred_element_type=f32) * over_rows(up_scale, 2 * rows)
    gate = jnp.dot(data, w_gate(), preferred_element_type=f32)
    gate = gate * (over_rows(gate_scale, 2 * rows) * math.sqrt(D))
    act = (up * (gate / (1.0 + jnp.exp(-gate)))).astype(bf16)
    part = jnp.dot(act, w_down(), preferred_element_type=f32)
    keep[...] = part[:rows, :]
    send[...] = part[rows:, :].astype(bf16)


def mlp_first_kernel(first, second, *rest):
    sources, (keep, send), held, sems = rest[:5], rest[5:7], rest[7:12], rest[12]
    copies = fetch(sources, held, sems)

    def ready(n):
        def get():
            copies[n].wait()
            return held[n][...]

        return get

    wait(copies[3:])
    feed(first, second, ready(0), ready(1), ready(2), held[3], held[4], keep, send)


def mlp_next_kernel(first, second, w_up, w_gate, w_down, up_scale, gate_scale, keep, send):
    feed(
        first,
        second,
        lambda: w_up[...],
        lambda: w_gate[...],
        lambda: w_down[...],
        up_scale,
        gate_scale,
        keep,
        send,
    )


def mlp_call(first, second, weights, held=False):
    rows = first.shape[0]
    units = weights[0].shape[1]
    out_shape = [jax.ShapeDtypeStruct((rows, D), f32), jax.ShapeDtypeStruct((rows, D), bf16)]
    if not held:
        out_shape += [jax.ShapeDtypeStruct(w.shape, w.dtype) for w in weights]
    return pl.pallas_call(
        mlp_next_kernel if held else mlp_first_kernel,
        out_shape=out_shape,
        in_specs=[vmem()] * 2 + [vmem() if held else hbm()] * 5,
        out_specs=[vmem()] * len(out_shape),
        scratch_shapes=[] if held else [pltpu.SemaphoreType.DMA((5,))],
        compiler_params=params(16),
        cost_estimate=cost(2 * 2 * rows * D * units * 3, 3 * D * units * 2, 2 * rows * units),
        name="mlp_held" if held else "mlp",
    )(first, second, *weights)


def add_kernel(kept, arrived, out):
    out[...] = (kept[...] + arrived[...].astype(f32)).astype(bf16)


def add_call(kept, arrived):
    return pl.pallas_call(
        add_kernel,
        out_shape=jax.ShapeDtypeStruct(kept.shape, bf16),
        in_specs=[vmem()] * 2,
        out_specs=vmem(),
        compiler_params=params(8),
        cost_estimate=cost(kept.size, kept.size * 8),
        name="add_partials",
    )(kept, arrived)


def final_kernel(hidden, rate_hbm, kept, *rest):
    arrived, (out, rate, sems) = rest[:-3], rest[-3:]
    copies = fetch([rate_hbm], [rate], sems)
    total = kept[...]
    for part in arrived:
        total = total + part[...].astype(f32)
    state = hidden[...]
    wait(copies)
    state = unit(state + over_rows(rate, state.shape[0]) * (unit(total) - state))
    out[...] = (math.sqrt(D) * state).astype(bf16)


def final_call(hidden, rate, kept, arrived):
    return pl.pallas_call(
        final_kernel,
        out_shape=jax.ShapeDtypeStruct(hidden.shape, bf16),
        in_specs=[vmem(), hbm()] + [vmem()] * (1 + len(arrived)),
        out_specs=pl.BlockSpec(hidden.shape, lambda: (0, 0)),
        scratch_shapes=fetched(rate),
        compiler_params=params(8),
        cost_estimate=cost(hidden.size * 10, hidden.size * 12),
        name="finish",
    )(hidden, rate, kept, *arrived)


def swap(shard, axis, mask):
    length = lax.axis_size(axis)
    return lax.ppermute(shard, axis, [(j, j ^ mask) for j in range(length)])


def body(
    tokens,
    seg_lengths,
    prefix_keys,
    prefix_values,
    w_qkv,
    w_out,
    qk_scale,
    attn_rate,
    w_up,
    w_gate,
    w_down,
    up_scale,
    gate_scale,
    mlp_rate,
):
    extent = lax.axis_size("tok")
    squares = extent // SQ
    place = lax.axis_index("tok").astype(jnp.int32).reshape(1)
    own = tokens[0]
    rows = own.shape[0]

    *cached, hidden, columns = prefix_call(
        place, qk_scale, prefix_keys[0], prefix_values[0], own
    )
    prefix = [cached[0]] + [swap(cached[m], "tok", m) for m in range(1, SQ)]
    queries, *sent = qkv_call(squares, place, hidden, columns, w_qkv)
    suffix = [sent[0]] + [swap(sent[m], "tok", m) for m in range(1, SQ)]
    queries = lax.all_to_all(queries.reshape(extent, QD, rows), "tok", 0, 0)
    accum, stats = cached_call(queries, *pack_call(prefix))
    parts, w_out = suffix_call(place, seg_lengths, queries, accum, stats, suffix, w_out)
    parts = lax.all_to_all(parts, "tok", 0, 0)
    hidden, flat = project_call(own, attn_rate, w_out, parts)

    weights = (w_up, w_gate, w_down, up_scale, gate_scale)
    chips = lax.axis_size("grp") // 2
    remote = [swap(flat, "grp", 2 * c) for c in range(1, chips)]
    keep, send, *weights = mlp_call(flat, swap(flat, "grp", 1), weights)
    arrived = [swap(send, "grp", 1)]
    for c in range(1, chips):
        data, keep = lax.optimization_barrier((remote[c - 1], keep))
        kept, send = mlp_call(data, swap(data, "grp", 1), weights, held=True)
        arrived.append(swap(add_call(kept, swap(send, "grp", 1)), "grp", 2 * c))
    return final_call(hidden, mlp_rate, keep, arrived)[None]


def solution(mesh):
    in_specs = (
        P("grp", "tok", None),
        P("grp", None),
        P("grp", "tok", None),
        P("grp", "tok", None),
        P(),
        P(),
        P(),
        P(),
        P(None, "grp"),
        P(None, "grp"),
        P("grp", None),
        P("grp"),
        P("grp"),
        P(),
    )
    out_specs = P("grp", "tok", None)
    return jax.shard_map(body, mesh=mesh, in_specs=in_specs, out_specs=out_specs, check_vma=False)
```

time: 318 us -> 105 us (0.33)
  waiting for transfers between devices: 186 us -> 25.6 us
  matrix products: 46.8 us -> 0 us
  Pallas kernels: 0 us -> 29.4 us
  local copies, waits for them, and re-layouts: 32.3 us -> 10.1 us
  other arithmetic: 21.4 us -> 0 us
  blocking collectives: 0 us -> 20.6 us
  between operations: 13.3 us -> 0.43 us
    all_gather x3 -> x0, waiting for transfers between devices: 154 us -> none  [the longest x1 85.2 us: body(): lax.all_gather(cached_values, 'tok', axis=0, tiled=True)]
    dot_general x14 -> x0, matrix products: 46.8 us -> none  [the longest x5 13.4 us: block_state(): jnp.einsum('rhk,khd->rhd', weights.astype(jnp.bfloat16), values, preferre...]
    pallas_call x0 -> x10, Pallas kernels: none -> 29.4 us  [the longest x1 9.65 us: cached_call(): pl.pallas_call(cached_kernel, out_shape=[jax.ShapeDtypeStruct((extent //...]
    reduce_scatter x1 -> x0, waiting for transfers between devices: 26.7 us -> none  [body(): lax.psum_scatter(partials.astype(jnp.bfloat16), 'grp', scatter_dimension=...]
    all_to_all x0 -> x1, blocking collectives: none -> 20.6 us  [body(): parts = lax.all_to_all(parts, 'tok', 0, 0)]
    ppermute x4 -> x12, waiting for transfers between devices: 4.94 us -> 20.1 us  [swap(): return lax.ppermute(shard, axis, [(j, j ^ mask) for j in range(length)])]
    reduce_sum x14 -> x0, other arithmetic: 12.1 us -> none  [the longest x7 7.62 us: unit(): jnp.sum(vector * vector, axis=-1, keepdims=True) + EPS]
    reshape x2 -> x0, local copies, waits for them, and re-layouts: 11.3 us -> none  [the longest x1 5.64 us: body(): pieces[0].reshape(piece_rows // block_rows, block_rows, HEADS, HEAD)]
  transfers between devices with their start and end apart: 8 -> 13, of which waited for: 5 -> 6; matrix products, arithmetic and copies ran while one was open for 11% -> 0% of each run, Pallas kernels for 0% -> 17%
where the time goes in v2:
time: 105 us; the launch traced here: 104 us
  Pallas kernels  29.4 us (28%)
  waiting for transfers between devices  25.6 us (24%)
  blocking collectives  20.6 us (20%)
  starting transfers between devices  18.1 us (17%)
  local copies, waits for them, and re-layouts  10.1 us (10%)
    all_to_all x1, blocking collectives, body(): parts = lax.all_to_all(parts, 'tok', 0, 0)  20.6 us
    ppermute x12, waiting for transfers between devices, swap(): return lax.ppermute(shard, axis, [(j, j ^ mask) for j in range(length)])  20.1 us
    ppermute x12, starting transfers between devices, swap(): return lax.ppermute(shard, axis, [(j, j ^ mask) for j in range(length)])  11.9 us
    unnamed x46, local copies, waits for them, and re-layouts  10.1 us
    pallas_call x1, Pallas kernels, cached_call(): pl.pallas_call(cached_kernel, out_shape=[jax.ShapeDtypeStruct((extent //...  9.65 us
    pallas_call x2, Pallas kernels, mlp_call(): pl.pallas_call(mlp_next_kernel if held else mlp_first_kernel, out_shape=o...  7.67 us
    all_to_all x1, starting transfers between devices, body(): queries = lax.all_to_all(queries.reshape(extent, QD, rows), 'tok', 0, 0)  6.23 us
    all_to_all x1, waiting for transfers between devices, body(): queries = lax.all_to_all(queries.reshape(extent, QD, rows), 'tok', 0, 0)  5.45 us
  transfers between devices with their start and end apart: 13, of which 6 were waited for; matrix products, arithmetic and copies ran while one was open for 0% of the time, Pallas kernels for 17%

profile of v2, /device:TPU:0, one launch (start us, length us, event | category | flops | bytes accessed | tf_op | source)
XLA Modules:
  0.0 104.2 jit_solution(18263236894103427838)
XLA Ops:
  0.0 1.0 copy-done.3
  1.0 1.1 %copy-done.11 = bf16[1,256,1280]{2,1,0:T(8,128)(2,1)S(1)} copy-done((bf16[1,256,1280]{2,1,0:T(8,128)(2,1)S(1)}, bf16[1,256,1280]{2,1,0:T(8,128)(2,1)}, u32[]{:S(2)}) %copy-start.11) | copy-done | bytes 655384
  2.1 1.1 %copy-done.12 = bf16[1,256,1280]{2,1,0:T(8,128)(2,1)S(1)} copy-done((bf16[1,256,1280]{2,1,0:T(8,128)(2,1)S(1)}, bf16[1,256,1280]{2,1,0:T(8,128)(2,1)}, u32[]{:S(2)}) %copy-start.12) | copy-done | bytes 655384
  3.2 0.7 copy-done.13
  3.8 1.4 %prefix_prep.1 = (bf16[640,256]{1,0:T(8,128)(2,1)S(1)}, bf16[640,256]{1,0:T(8,128)(2,1)S(1)}, bf16[640,256]{1,0:T(8,128)(2,1)S(1)}, bf16[640,256]{1,0:T(8,128)(2...) custom-call(s32[1]{0:T(128)} %bitcast.1.place, f32[1280]{0:T(1024)S(1)} %copy-done.13, ...), custom_call_target="tpu_custom_call" | custom-call | flops 49999998976 | bytes 2621440 | tf_op jit(solution)/shard_map/prefix_prep/pallas_call | solution.py:114
  5.2 0.0 copy-start.19
  5.2 0.7 copy-done.19
  5.9 2.9 %collective-permute-start = (bf16[640,256]{1,0:T(8,128)(2,1)S(1)}, bf16[640,256]{1,0:T(8,128)(2,1)S(1)}, u32[]{:S(2)}, u32[]{:S(2)}) collective-permute-start(bf16[640,256]{1,0:T(8,128)(2,1)S(1)} %get-tuple-element.39), channel_id=1, source_target_pairs={{0,1},{1,0},{2,3},{3,2},{4,5},{5,4},{6,7},{7,6},{8,9},{9,8},{10,11... | collective-permute-start | bytes 983048 | tf_op jit(solution)/shard_map/ppermute | solution.py:489
  8.9 1.6 %collective-permute-start.1 = (bf16[640,256]{1,0:T(8,128)(2,1)S(1)}, bf16[640,256]{1,0:T(8,128)(2,1)S(1)}, u32[]{:S(2)}, u32[]{:S(2)}) collective-permute-start(bf16[640,256]{1,0:T(8,128)(2,1)S(1)} %get-tuple-element.40), channel_id=1, source_target_pairs={{0,2},{1,3},{2,0},{3,1},{4,6},{5,7},{6,4},{7,5},{8,10},{9,11},{10,... | collective-permute-start | bytes 983048 | tf_op jit(solution)/shard_map/ppermute | solution.py:489
  10.5 0.0 collective-permute-start.2
  10.5 0.0 copy-done.9
  10.5 3.1 %qkv.1 = (bf16[2560,128]{1,0:T(8,128)(2,1)}, bf16[640,128]{1,0:T(8,128)(2,1)S(1)}, bf16[640,128]{1,0:T(8,128)(2,1)S(1)}, bf16[640,128]{1,0:T(8,128)(2,1)S(1)}, bf16[640,128]{1,0:T(8,128)(2,1)S(1)}) custom-call(s32[1]{0:T(128)} %bitcast.1.place, bf16[128,1280]{1,0:T(8,128)(2,1)S(1)} %get-tuple-element.35.hidden, ...), custom_call_target="tpu_custom_call" | custom-call | flops 49999998976 | bytes 9830400 | tf_op jit(solution)/shard_map/qkv/pallas_call | solution.py:157
  13.5 0.0 copy-start.21
  13.6 6.2 %all-to-all-start = ((bf16[8,320,128]{2,1,0:T(8,128)(2,1)}), bf16[8,320,128]{2,1,0:T(8,128)(2,1)S(1)}, u32[]{:S(2)}, u32[]{:S(2)}) async-start(bf16[8,320,128]{2,1,0:T(8,128)(2,1)} %bitcast.4), calls=%async_computation | async-start | bytes 1310720 | tf_op jit(solution)/shard_map/all_to_all | solution.py:520
  19.8 0.0 copy-done.21
  19.8 2.0 %collective-permute-start.3 = (bf16[640,128]{1,0:T(8,128)(2,1)S(1)}, bf16[640,128]{1,0:T(8,128)(2,1)S(1)}, u32[]{:S(2)}, u32[]{:S(2)}) collective-permute-start(bf16[640,128]{1,0:T(8,128)(2,1)S(1)} %get-tuple-element.47), channel_id=1, source_target_pairs={{0,1},{1,0},{2,3},{3,2},{4,5},{5,4},{6,7},{7,6},{8,9},{9,8},{10,11... | collective-permute-start | bytes 491528 | tf_op jit(solution)/shard_map/ppermute | solution.py:489
  21.8 1.5 %collective-permute-start.4 = (bf16[640,128]{1,0:T(8,128)(2,1)S(1)}, bf16[640,128]{1,0:T(8,128)(2,1)S(1)}, u32[]{:S(2)}, u32[]{:S(2)}) collective-permute-start(bf16[640,128]{1,0:T(8,128)(2,1)S(1)} %get-tuple-element.48), channel_id=1, source_target_pairs={{0,2},{1,3},{2,0},{3,1},{4,6},{5,7},{6,4},{7,5},{8,10},{9,11},{10,... | collective-permute-start | bytes 491528 | tf_op jit(solution)/shard_map/ppermute | solution.py:489
  23.3 0.0 collective-permute-done.refs_1_
  23.3 0.1 collective-permute-start.5
  23.3 0.0 collective-permute-done.1.refs_2_
  23.4 5.3 %collective-permute-done.2.refs_3_ = bf16[640,256]{1,0:T(8,128)(2,1)S(1)} collective-permute-done((bf16[640,256]{1,0:T(8,128)(2,1)S(1)}, bf16[640,256]{1,0:T(8,128)(2,1)S(1)}, u32[]{:S(2)}, u32[]{:S(2)}) %collective-permute-start.2) | collective-permute-done | bytes 327712 | tf_op jit(solution)/shard_map/ppermute | solution.py:489
  28.7 1.0 copy-done.20
  29.6 0.5 pack.1
  30.1 0.0 copy-start.15
  30.1 1.1 %copy-done.15 = bf16[5,1024,64]{2,1,0:T(8,128)(2,1)} copy-done((bf16[5,1024,64]{2,1,0:T(8,128)(2,1)}, bf16[5,1024,64]{2,1,0:T(8,128)(2,1)S(1)}, u32[]{:S(2)}) %copy-start.15) | copy-done | bytes 655384
  31.2 0.8 copy-done.17
  32.0 5.4 %all-to-all-done.query_all = bf16[8,320,128]{2,1,0:T(8,128)(2,1)S(1)} async-done(((bf16[8,320,128]{2,1,0:T(8,128)(2,1)}), bf16[8,320,128]{2,1,0:T(8,128)(2,1)S(1)}, u32[]{:S(2)}, u32[]{:S(2)}) %all-to-all-start) | async-done | bytes 655392 | tf_op jit(solution)/shard_map/all_to_all | solution.py:520
  37.5 1.5 %copy-done.16 = bf16[5,1024,64]{2,1,0:T(8,128)(2,1)S(1)} copy-done((bf16[5,1024,64]{2,1,0:T(8,128)(2,1)S(1)}, bf16[5,1024,64]{2,1,0:T(8,128)(2,1)}, u32[]{:S(2)}) %copy-start.16) | copy-done | bytes 655384
  39.0 1.1 %copy-done.18 = bf16[320,1024]{1,0:T(8,128)(2,1)S(1)} copy-done((bf16[320,1024]{1,0:T(8,128)(2,1)S(1)}, bf16[320,1024]{1,0:T(8,128)(2,1)}, u32[]{:S(2)}) %copy-start.18) | copy-done | bytes 655384
  40.1 9.7 %attend_cached.1 = (f32[2,320,512]{2,1,0:T(8,128)S(1)}, f32[2,16,512]{2,1,0:T(8,128)S(1)}) custom-call(bf16[8,320,128]{2,1,0:T(8,128)(2,1)S(1)} %all-to-all-done.query_all, bf16[5,1024,64]{2,1,0:T(8,128)(2,1)S(1)} %copy-done.16, bf16[320,1024]{1,0:T(8,128)(2,1)S(1)} %copy-done.18), custom_call_target="tpu_custom_call" | custom-call | flops 1000000000 | tf_op jit(solution)/shard_map/attend_cached/pallas_call | solution.py:222
  49.7 0.0 collective-permute-done.3.rest_1_
  49.7 0.0 collective-permute-done.4.rest_2_
  49.7 0.0 collective-permute-done.5.rest_3_
  49.7 0.0 copy-done.22
  49.8 0.0 copy-done.14
  49.8 0.0 copy-done.10
  49.8 0.0 copy-start.4
  49.8 0.0 copy-start.5
  49.8 0.0 copy-start.1
  49.8 0.0 copy-start.2
  49.8 4.6 %attend_suffix.1 = (bf16[8,336,128]{2,1,0:T(8,128)(2,1)S(1)}, bf16[1280,1280]{1,0:T(8,128)(2,1)S(1)}) custom-call(s32[1]{0:T(128)} %bitcast.1.place, s32[1,16]{1,0:T(1,128)S(1)} %copy-done.14, bf16[8,320,128]{2,1,0:T(8,128)(2,1)S(1)} %all-to-all-done.query_all, f32[2,320,512]{2,1,0:T(8,128)S(1)} %get-tuple-element.44.accum, ...), custom_call_target="tpu_custom_call" | custom-call | flops 20000000000 | bytes 8388608 | tf_op jit(solution)/shard_map/attend_suffix/pallas_call | solution.py:322
  54.5 0.0 copy-start
  54.5 0.0 copy-start.6
  54.5 0.0 copy-start.7
  54.5 20.6 %all_to_all.10.parts = bf16[8,336,128]{2,1,0:T(8,128)(2,1)S(1)} all-to-all(bf16[8,336,128]{2,1,0:T(8,128)(2,1)S(1)} %get-tuple-element.51), channel_id=1, replica_groups=mesh['grp'=4,'tok'=8] {'tok'}, dimensions={0} | all-to-all | bytes 1376256 | tf_op jit(solution)/shard_map/all_to_all | solution.py:523
  75.1 1.2 %project.1 = (f32[128,1280]{1,0:T(8,128)S(1)}, bf16[128,1280]{1,0:T(8,128)(2,1)S(1)}) custom-call(bf16[128,1280]{1,0:T(8,128)(2,1)S(1)} %bitcast.7, f32[1280]{0:T(1024)S(1)} %copy-done.5, bf16[1280,1280]{1,0:T(8,128)(2,1)S(1)} %get-tuple-element.50.w_out, bf16[8,336,128]{2,1,0:T(8,128)(2,1)S(1)} %all_to_all.10.parts), custom_call_target="tpu_custom_call" | custom-call | flops 419430400 | bytes 3276800 | tf_op jit(solution)/shard_map/project/pallas_call | solution.py:375
  76.4 0.1 collective-permute-start.7
  76.4 1.6 %collective-permute-start.6 = (bf16[128,1280]{1,0:T(8,128)(2,1)S(1)}, bf16[128,1280]{1,0:T(8,128)(2,1)S(1)}, u32[]{:S(2)}, u32[]{:S(2)}) collective-permute-start(bf16[128,1280]{1,0:T(8,128)(2,1)S(1)} %get-tuple-element.53.first), channel_id=1, source_target_pairs={{0,16},{8,24},{16,0},{24,8},{1,17},{9,25},{17,1},{25,9},{2,18},{10... | collective-permute-start | bytes 983048 | tf_op jit(solution)/shard_map/ppermute | solution.py:489
  78.0 0.0 collective-permute-done.7.second
  78.1 0.0 copy-done.2
  78.1 4.7 %mlp.1 = (f32[128,1280]{1,0:T(8,128)S(1)}, bf16[128,1280]{1,0:T(8,128)(2,1)S(1)}, bf16[1280,1280]{1,0:T(8,128)(2,1)S(1)}, bf16[1280,1280]{1,0:T(8,128)(2,1)S(1)}...) custom-call(bf16[128,1280]{1,0:T(8,128)(2,1)S(1)} %get-tuple-element.53.first, ...), custom_call_target="tpu_custom_call" | custom-call | flops 2516582400 | bytes 9830400 | tf_op jit(solution)/shard_map/mlp/pallas_call | solution.py:434
  82.8 3.8 %collective-permute-done.6.first = bf16[128,1280]{1,0:T(8,128)(2,1)S(1)} collective-permute-done((bf16[128,1280]{1,0:T(8,128)(2,1)S(1)}, bf16[128,1280]{1,0:T(8,128)(2,1)S(1)}, u32[]{:S(2)}, u32[]{:S(2)}) %collective-permute-start.6) | collective-permute-done | bytes 327712 | tf_op jit(solution)/shard_map/ppermute | solution.py:489
  86.6 0.0 collective-permute-start.9
  86.6 1.6 %collective-permute-done.9.second = bf16[128,1280]{1,0:T(8,128)(2,1)S(1)} collective-permute-done((bf16[128,1280]{1,0:T(8,128)(2,1)S(1)}, bf16[128,1280]{1,0:T(8,128)(2,1)S(1)}, u32[]{:S(2)}, u32[]{:S(2)}) %collective-permute-start.9) | collective-permute-done | bytes 327712 | tf_op jit(solution)/shard_map/ppermute | solution.py:489
  88.2 3.0 %mlp_held.1 = (f32[128,1280]{1,0:T(8,128)S(1)}, bf16[128,1280]{1,0:T(8,128)(2,1)S(1)}) custom-call(bf16[128,1280]{1,0:T(8,128)(2,1)S(1)} %collective-permute-done.6.first, bf16[128,1280]{1,0:T(8,128)(2,1)S(1)} %collective-permute-done.9.second, bf16[1280,1280]{1,0:T(8,128)(2,1)S(1)} %get-tuple-element.58.w_up, ...), custom_call_target="tpu_custom_call" | custom-call | flops 2516582400 | bytes 9830400 | tf_op jit(solution)/shard_map/mlp_held/pallas_call | solution.py:434
  91.2 0.2 collective-permute-start.10
  91.4 0.4 collective-permute-start.8
  91.8 1.1 %collective-permute-done.10.arrived = bf16[128,1280]{1,0:T(8,128)(2,1)S(1)} collective-permute-done((bf16[128,1280]{1,0:T(8,128)(2,1)S(1)}, bf16[128,1280]{1,0:T(8,128)(2,1)S(1)}, u32[]{:S(2)}, u32[]{:S(2)}) %collective-permute-start.10) | collective-permute-done | bytes 327712 | tf_op jit(solution)/shard_map/ppermute | solution.py:489
  92.9 0.1 add_partials.1
  92.9 1.6 %collective-permute-start.11 = (bf16[128,1280]{1,0:T(8,128)(2,1)S(1)}, bf16[128,1280]{1,0:T(8,128)(2,1)S(1)}, u32[]{:S(2)}, u32[]{:S(2)}) collective-permute-start(bf16[128,1280]{1,0:T(8,128)(2,1)S(1)} %add_partials.1), channel_id=1, source_target_pairs={{0,16},{8,24},{16,0},{24,8},{1,17},{9,25},{17,1},{25,9},{2,18},{10... | collective-permute-start | bytes 983048 | tf_op jit(solution)/shard_map/ppermute | solution.py:489
  94.5 0.0 collective-permute-done.8.rest_0_
  94.5 8.2 %collective-permute-done.11.rest_1_ = bf16[128,1280]{1,0:T(8,128)(2,1)S(1)} collective-permute-done((bf16[128,1280]{1,0:T(8,128)(2,1)S(1)}, bf16[128,1280]{1,0:T(8,128)(2,1)S(1)}, u32[]{:S(2)}, u32[]{:S(2)}) %collective-permute-start.11) | collective-permute-done | bytes 327712 | tf_op jit(solution)/shard_map/ppermute | solution.py:489
  102.8 0.0 copy-done.8
  102.8 1.3 %finish.1 = bf16[128,1280]{1,0:T(8,128)(2,1)} custom-call(f32[128,1280]{1,0:T(8,128)S(1)} %get-tuple-element.52.hidden, f32[1280]{0:T(1024)S(1)} %copy-done.8, f32[128,1280]{1,0:T(8,128)S(1)} %get-tuple-element.55.kept, bf16[128,1280]{1,0:T(8,128)(2,1)S(1)} %collective-permute-done.8.rest_0_, bf16[128,1280]{1,0:T(8,128)(2,1)S(1)} %collective-permute-done.11.rest_1_), custom_call_target="tpu_custom_call" | custom-call | flops 1638400 | bytes 1966080 | tf_op jit(solution)/shard_map/finish/pallas_call | solution.py:475
  (19 shorter events, 0.0 us)
Async XLA Ops:
  0.0 1.0 copy-start.3
  1.0 1.1 %copy-start.11 = (bf16[1,256,1280]{2,1,0:T(8,128)(2,1)S(1)}, bf16[1,256,1280]{2,1,0:T(8,128)(2,1)}, u32[]{:S(2)}) copy-start(bf16[1,256,1280]{2,1,0:T(8,128)(2,1)} %param.16) | copy-start | bytes 1966084
  2.1 1.1 %copy-start.12 = (bf16[1,256,1280]{2,1,0:T(8,128)(2,1)S(1)}, bf16[1,256,1280]{2,1,0:T(8,128)(2,1)}, u32[]{:S(2)}) copy-start(bf16[1,256,1280]{2,1,0:T(8,128)(2,1)} %param.17) | copy-start | bytes 1966084
  3.1 0.7 copy-start.13
  3.8 6.6 %copy-start.9 = (bf16[1280,3840]{1,0:T(8,128)(2,1)S(1)}, bf16[1280,3840]{1,0:T(8,128)(2,1)}, u32[]{:S(2)}) copy-start(bf16[1280,3840]{1,0:T(8,128)(2,1)} %w_hbm.1) | copy-start | bytes 29491204
  5.2 0.7 copy-start.19
  5.9 17.3 %collective-permute-start = (bf16[640,256]{1,0:T(8,128)(2,1)S(1)}, bf16[640,256]{1,0:T(8,128)(2,1)S(1)}, u32[]{:S(2)}, u32[]{:S(2)}) collective-permute-start(bf16[640,256]{1,0:T(8,128)(2,1)S(1)} %get-tuple-element.39), channel_id=1, source_target_pairs={{0,1},{1,0},{2,3},{3,2},{4,5},{5,4},{6,7},{7,6},{8,9},{9,8},{10,11... | collective-permute-start | bytes 983048 | tf_op jit(solution)/shard_map/ppermute | solution.py:489
  8.9 14.5 %collective-permute-start.1 = (bf16[640,256]{1,0:T(8,128)(2,1)S(1)}, bf16[640,256]{1,0:T(8,128)(2,1)S(1)}, u32[]{:S(2)}, u32[]{:S(2)}) collective-permute-start(bf16[640,256]{1,0:T(8,128)(2,1)S(1)} %get-tuple-element.40), channel_id=1, source_target_pairs={{0,2},{1,3},{2,0},{3,1},{4,6},{5,7},{6,4},{7,5},{8,10},{9,11},{10,... | collective-permute-start | bytes 983048 | tf_op jit(solution)/shard_map/ppermute | solution.py:489
  10.5 18.2 %collective-permute-start.2 = (bf16[640,256]{1,0:T(8,128)(2,1)S(1)}, bf16[640,256]{1,0:T(8,128)(2,1)S(1)}, u32[]{:S(2)}, u32[]{:S(2)}) collective-permute-start(bf16[640,256]{1,0:T(8,128)(2,1)S(1)} %get-tuple-element.41), channel_id=1, source_target_pairs={{0,3},{1,2},{2,1},{3,0},{4,7},{5,6},{6,5},{7,4},{8,11},{9,10},{10,... | collective-permute-start | bytes 983048 | tf_op jit(solution)/shard_map/ppermute | solution.py:489
  13.5 6.2 %copy-start.21 = (bf16[640,128]{1,0:T(8,128)(2,1)}, bf16[640,128]{1,0:T(8,128)(2,1)S(1)}, u32[]{:S(2)}) copy-start(bf16[640,128]{1,0:T(8,128)(2,1)S(1)} %get-tuple-element.46.rest_0_) | copy-start | bytes 491524
  13.6 23.9 %all-to-all-start = ((bf16[8,320,128]{2,1,0:T(8,128)(2,1)}), bf16[8,320,128]{2,1,0:T(8,128)(2,1)S(1)}, u32[]{:S(2)}, u32[]{:S(2)}) async-start(bf16[8,320,128]{2,1,0:T(8,128)(2,1)} %bitcast.4), calls=%async_computation | async-start | bytes 1310720 | tf_op jit(solution)/shard_map/all_to_all | solution.py:520
  19.8 29.9 %collective-permute-start.3 = (bf16[640,128]{1,0:T(8,128)(2,1)S(1)}, bf16[640,128]{1,0:T(8,128)(2,1)S(1)}, u32[]{:S(2)}, u32[]{:S(2)}) collective-permute-start(bf16[640,128]{1,0:T(8,128)(2,1)S(1)} %get-tuple-element.47), channel_id=1, source_target_pairs={{0,1},{1,0},{2,3},{3,2},{4,5},{5,4},{6,7},{7,6},{8,9},{9,8},{10,11... | collective-permute-start | bytes 491528 | tf_op jit(solution)/shard_map/ppermute | solution.py:489
  21.8 27.9 %collective-permute-start.4 = (bf16[640,128]{1,0:T(8,128)(2,1)S(1)}, bf16[640,128]{1,0:T(8,128)(2,1)S(1)}, u32[]{:S(2)}, u32[]{:S(2)}) collective-permute-start(bf16[640,128]{1,0:T(8,128)(2,1)S(1)} %get-tuple-element.48), channel_id=1, source_target_pairs={{0,2},{1,3},{2,0},{3,1},{4,6},{5,7},{6,4},{7,5},{8,10},{9,11},{10,... | collective-permute-start | bytes 491528 | tf_op jit(solution)/shard_map/ppermute | solution.py:489
  23.3 26.5 %collective-permute-start.5 = (bf16[640,128]{1,0:T(8,128)(2,1)S(1)}, bf16[640,128]{1,0:T(8,128)(2,1)S(1)}, u32[]{:S(2)}, u32[]{:S(2)}) collective-permute-start(bf16[640,128]{1,0:T(8,128)(2,1)S(1)} %get-tuple-element.49), channel_id=1, source_target_pairs={{0,3},{1,2},{2,1},{3,0},{4,7},{5,6},{6,5},{7,4},{8,11},{9,10},{10,... | collective-permute-start | bytes 491528 | tf_op jit(solution)/shard_map/ppermute | solution.py:489
  28.7 1.0 copy-start.20
  29.6 20.1 %copy-start.22 = (bf16[640,128]{1,0:T(8,128)(2,1)S(1)}, bf16[640,128]{1,0:T(8,128)(2,1)}, u32[]{:S(2)}) copy-start(bf16[640,128]{1,0:T(8,128)(2,1)} %copy-done.21) | copy-start | bytes 491524
  30.1 1.1 %copy-start.15 = (bf16[5,1024,64]{2,1,0:T(8,128)(2,1)}, bf16[5,1024,64]{2,1,0:T(8,128)(2,1)S(1)}, u32[]{:S(2)}) copy-start(bf16[5,1024,64]{2,1,0:T(8,128)(2,1)S(1)} %get-tuple-element.42.keys) | copy-start | bytes 1966084
  31.2 0.8 copy-start.17
  32.0 17.7 %copy-start.14 = (s32[1,16]{1,0:T(1,128)S(1)}, s32[1,16]{1,0:T(1,128)}, u32[]{:S(2)}) copy-start(s32[1,16]{1,0:T(1,128)} %lengths.1) | copy-start | bytes 196
  37.5 12.3 %copy-start.10 = (bf16[1280,1280]{1,0:T(8,128)(2,1)S(1)}, bf16[1280,1280]{1,0:T(8,128)(2,1)}, u32[]{:S(2)}) copy-start(bf16[1280,1280]{1,0:T(8,128)(2,1)} %rest_4_.2) | copy-start | bytes 9830404
  37.5 1.5 %copy-start.16 = (bf16[5,1024,64]{2,1,0:T(8,128)(2,1)S(1)}, bf16[5,1024,64]{2,1,0:T(8,128)(2,1)}, u32[]{:S(2)}) copy-start(bf16[5,1024,64]{2,1,0:T(8,128)(2,1)} %copy-done.15) | copy-start | bytes 1966084
  39.0 1.1 %copy-start.18 = (bf16[320,1024]{1,0:T(8,128)(2,1)S(1)}, bf16[320,1024]{1,0:T(8,128)(2,1)}, u32[]{:S(2)}) copy-start(bf16[320,1024]{1,0:T(8,128)(2,1)} %copy-done.17) | copy-start | bytes 1966084
  49.8 25.3 %copy-start.4 = (bf16[1,128,1280]{2,1,0:T(8,128)(2,1)S(1)}, bf16[1,128,1280]{2,1,0:T(8,128)(2,1)}, u32[]{:S(2)}) copy-start(bf16[1,128,1280]{2,1,0:T(8,128)(2,1)} %param.14) | copy-start | bytes 983044
  49.8 25.3 %copy-start.5 = (f32[1280]{0:T(1024)S(1)}, f32[1280]{0:T(1024)}, u32[]{:S(2)}) copy-start(f32[1280]{0:T(1024)} %rate_hbm.2) | copy-start | bytes 15364
  49.8 28.3 %copy-start.1 = (bf16[1280,1280]{1,0:T(8,128)(2,1)S(1)}, bf16[1280,1280]{1,0:T(8,128)(2,1)}, u32[]{:S(2)}) copy-start(bf16[1280,1280]{1,0:T(8,128)(2,1)} %rest_1_.1) | copy-start | bytes 9830404
  49.8 28.2 %copy-start.2 = (bf16[1280,1280]{1,0:T(8,128)(2,1)S(1)}, bf16[1280,1280]{1,0:T(8,128)(2,1)}, u32[]{:S(2)}) copy-start(bf16[1280,1280]{1,0:T(8,128)(2,1)} %rest_2_.1) | copy-start | bytes 9830404
  54.5 23.6 %copy-start = (bf16[1280,1280]{1,0:T(8,128)(2,1)S(1)}, bf16[1280,1280]{1,0:T(8,128)(2,1)}, u32[]{:S(2)}) copy-start(bf16[1280,1280]{1,0:T(8,128)(2,1)} %rest_0_.3) | copy-start | bytes 9830404
  54.5 23.6 %copy-start.6 = (f32[1280]{0:T(1024)S(1)}, f32[1280]{0:T(1024)}, u32[]{:S(2)}) copy-start(f32[1280]{0:T(1024)} %rest_3_.1) | copy-start | bytes 15364
  54.5 23.6 %copy-start.7 = (f32[1280]{0:T(1024)S(1)}, f32[1280]{0:T(1024)}, u32[]{:S(2)}) copy-start(f32[1280]{0:T(1024)} %rest_4_.3) | copy-start | bytes 15364
  76.4 1.7 %collective-permute-start.7 = (bf16[128,1280]{1,0:T(8,128)(2,1)S(1)}, bf16[128,1280]{1,0:T(8,128)(2,1)S(1)}, u32[]{:S(2)}, u32[]{:S(2)}) collective-permute-start(bf16[128,1280]{1,0:T(8,128)(2,1)S(1)} %get-tuple-element.53.first), channel_id=1, source_target_pairs={{0,8},{8,0},{16,24},{24,16},{1,9},{9,1},{17,25},{25,17},{2,10},{10... | collective-permute-start | bytes 983048 | tf_op jit(solution)/shard_map/ppermute | solution.py:489
  76.4 10.1 %collective-permute-start.6 = (bf16[128,1280]{1,0:T(8,128)(2,1)S(1)}, bf16[128,1280]{1,0:T(8,128)(2,1)S(1)}, u32[]{:S(2)}, u32[]{:S(2)}) collective-permute-start(bf16[128,1280]{1,0:T(8,128)(2,1)S(1)} %get-tuple-element.53.first), channel_id=1, source_target_pairs={{0,16},{8,24},{16,0},{24,8},{1,17},{9,25},{17,1},{25,9},{2,18},{10... | collective-permute-start | bytes 983048 | tf_op jit(solution)/shard_map/ppermute | solution.py:489
  86.6 1.6 %collective-permute-start.9 = (bf16[128,1280]{1,0:T(8,128)(2,1)S(1)}, bf16[128,1280]{1,0:T(8,128)(2,1)S(1)}, u32[]{:S(2)}, u32[]{:S(2)}) collective-permute-start(bf16[128,1280]{1,0:T(8,128)(2,1)S(1)} %collective-permute-done.6.first), channel_id=1, source_target_pairs={{0,8},{8,0},{16,24},{24,16},{1,9},{9,1},{17,25},{25,17},{2,10},{10... | collective-permute-start | bytes 983048 | tf_op jit(solution)/shard_map/ppermute | solution.py:489
  88.2 14.6 %copy-start.8 = (f32[1280]{0:T(1024)S(1)}, f32[1280]{0:T(1024)}, u32[]{:S(2)}) copy-start(f32[1280]{0:T(1024)} %rate_hbm.3) | copy-start | bytes 15364
  91.2 1.7 %collective-permute-start.10 = (bf16[128,1280]{1,0:T(8,128)(2,1)S(1)}, bf16[128,1280]{1,0:T(8,128)(2,1)S(1)}, u32[]{:S(2)}, u32[]{:S(2)}) collective-permute-start(bf16[128,1280]{1,0:T(8,128)(2,1)S(1)} %get-tuple-element.64), channel_id=1, source_target_pairs={{0,8},{8,0},{16,24},{24,16},{1,9},{9,1},{17,25},{25,17},{2,10},{10... | collective-permute-start | bytes 983048 | tf_op jit(solution)/shard_map/ppermute | solution.py:489
  91.4 3.1 %collective-permute-start.8 = (bf16[128,1280]{1,0:T(8,128)(2,1)S(1)}, bf16[128,1280]{1,0:T(8,128)(2,1)S(1)}, u32[]{:S(2)}, u32[]{:S(2)}) collective-permute-start(bf16[128,1280]{1,0:T(8,128)(2,1)S(1)} %get-tuple-element.56), channel_id=1, source_target_pairs={{0,8},{8,0},{16,24},{24,16},{1,9},{9,1},{17,25},{25,17},{2,10},{10... | collective-permute-start | bytes 983048 | tf_op jit(solution)/shard_map/ppermute | solution.py:489
  92.9 9.8 %collective-permute-start.11 = (bf16[128,1280]{1,0:T(8,128)(2,1)S(1)}, bf16[128,1280]{1,0:T(8,128)(2,1)S(1)}, u32[]{:S(2)}, u32[]{:S(2)}) collective-permute-start(bf16[128,1280]{1,0:T(8,128)(2,1)S(1)} %add_partials.1), channel_id=1, source_target_pairs={{0,16},{8,24},{16,0},{24,8},{1,17},{9,25},{17,1},{25,9},{2,18},{10... | collective-permute-start | bytes 983048 | tf_op jit(solution)/shard_map/ppermute | solution.py:489

commit v3 on v2

--- a/solution.py
+++ b/solution.py
@@ -17,6 +17,8 @@
 QD = HQ * HEAD
 LSE = 16
 NEG = -1e30
+PREFIX_LIMIT = 61
+QKV_LIMIT = 50
 MIB = 1 << 20
 
 f32 = jnp.float32
@@ -82,16 +84,18 @@
     return pl.CostEstimate(flops=int(flops), bytes_accessed=int(nbytes), transcendentals=int(trans))
 
 
+def column(scale, c):
+    return jnp.broadcast_to(scale[c * 128 : (c + 1) * 128], (128, 128)).T
+
+
 def prefix_kernel(place, *rest):
-    outs, rest, sources = rest[4 : 4 + SQ], rest[4 + SQ :], rest[:4]
-    hidden, columns, parts, scale, keys, values, tokens, sems = rest
-    copies = fetch(sources, (scale, keys, values, tokens), sems)
+    sources, outs, (parts, scale, keys, values, sems) = rest[:3], rest[3 : 3 + SQ], rest[3 + SQ :]
+    copies = fetch(sources, (scale, keys, values), sems)
     rows = keys.shape[0]
     wait(copies[:2])
     for c in range(D // 128):
         cols = slice(c * 128, (c + 1) * 128)
-        columns[c] = jnp.broadcast_to(scale[cols], (128, 128)).T
-        scale_t = jnp.concatenate([columns[c]] * (rows // 128), axis=1)
+        scale_t = jnp.concatenate([column(scale, c)] * (rows // 128), axis=1)
         split(parts, 0, c, head_unit_t(keys[:, cols].T.astype(f32), scale_t).astype(bf16))
     wait(copies[2:])
     for c in range(D // 128):
@@ -99,7 +103,6 @@
     i = lax.rem(place[0], SQ)
     for m in range(SQ):
         outs[m][...] = parts[jnp.bitwise_xor(i, m)]
-    hidden[...] = unit(tokens[...].astype(f32)).astype(bf16)
 
 
 def split(out, base, c, block):
@@ -109,37 +112,36 @@
         out[row // QD, at : at + HEAD, :] = block[part : part + HEAD, :]
 
 
-def prefix_call(place, scale, keys, values, tokens):
+def prefix_call(place, scale, keys, values):
     rows = keys.shape[0]
     return pl.pallas_call(
         prefix_kernel,
-        out_shape=[jax.ShapeDtypeStruct((2 * QD, rows), bf16)] * SQ
-        + [
-            jax.ShapeDtypeStruct(tokens.shape, bf16),
-            jax.ShapeDtypeStruct((D // 128, 128, 128), f32),
-        ],
-        in_specs=[smem()] + [hbm()] * 4,
-        out_specs=[vmem()] * (SQ + 2),
-        scratch_shapes=[pltpu.VMEM((SQ, 2 * QD, rows), bf16)]
-        + fetched(scale, keys, values, tokens),
-        compiler_params=params(6),
+        out_shape=[jax.ShapeDtypeStruct((2 * QD, rows), bf16)] * SQ,
+        in_specs=[smem()] + [hbm()] * 3,
+        out_specs=[vmem()] * SQ,
+        scratch_shapes=[pltpu.VMEM((SQ, 2 * QD, rows), bf16)] + fetched(scale, keys, values),
+        compiler_params=params(PREFIX_LIMIT),
         cost_estimate=cost(5e10, 4 * rows * D * 2),
         name="prefix_prep",
-    )(place, scale, keys, values, tokens)
-
-
-def qkv_kernel(squares, place, hidden, columns, w_hbm, queries, *rest):
-    outs, (parts, weights, w_sems) = rest[:SQ], rest[SQ:]
+    )(place, scale, keys, values)
+
+
+def qkv_kernel(squares, place, tokens_hbm, scale_hbm, w_hbm, queries, *rest):
+    outs, (parts, tokens, scale, sems, weights, w_sems) = rest[:SQ], rest[SQ:]
+    small = fetch((tokens_hbm, scale_hbm), (tokens, scale), sems)
     spans = [pl.ds(p * D, D) for p in range(3)]
     copies = fetch([w_hbm.at[:, p] for p in spans], [weights.at[:, p] for p in spans], w_sems)
-    rows = hidden.shape[0]
+    wait(small)
+    rows = tokens.shape[0]
+    hidden = unit(tokens[...].astype(f32)).astype(bf16)
+    columns = [column(scale, c)[:, :rows] for c in range(D // 128)]
     for part in range(3):
         copies[part].wait()
-        out = jnp.dot(hidden[...], weights[:, part * D : (part + 1) * D], preferred_element_type=f32)
+        out = jnp.dot(hidden, weights[:, part * D : (part + 1) * D], preferred_element_type=f32)
         for c in range(D // 128):
             block = out[:, c * 128 : (c + 1) * 128].T
             if part < 2:
-                block = head_unit_t(block, columns[c, :, :rows])
+                block = head_unit_t(block, columns[c])
             if part == 0:
                 block = (block * math.sqrt(HEAD)).astype(bf16)
                 for s in range(squares):
@@ -151,56 +153,55 @@
         outs[m][...] = parts[jnp.bitwise_xor(i, m)]
 
 
-def qkv_call(squares, place, hidden, columns, weights):
-    rows = hidden.shape[0]
+def qkv_call(squares, place, tokens, scale, weights):
+    rows = tokens.shape[0]
     pair = jax.ShapeDtypeStruct((2 * QD, rows), bf16)
     return pl.pallas_call(
         functools.partial(qkv_kernel, squares),
         out_shape=[jax.ShapeDtypeStruct((squares * D, rows), bf16)] + [pair] * SQ,
-        in_specs=[smem(), vmem(), vmem(), hbm()],
+        in_specs=[smem()] + [hbm()] * 3,
         out_specs=[vmem()] * (1 + SQ),
         scratch_shapes=[
             pltpu.VMEM((SQ, 2 * QD, rows), bf16),
+            *fetched(tokens, scale),
             pltpu.VMEM((D, 3 * D), bf16),
             pltpu.SemaphoreType.DMA((3,)),
         ],
-        compiler_params=params(14),
+        compiler_params=params(QKV_LIMIT),
         cost_estimate=cost(5e10, 3 * D * D * 2),
         name="qkv",
-    )(place, hidden, columns, weights)
-
-
-def pack_kernel(*refs):
-    parts, (keys, values) = refs[:SQ], refs[SQ:]
-    span = parts[0].shape[1]
-    for n, part in enumerate(parts):
+    )(place, tokens, scale, weights)
+
+
+def arrive_kernel(*refs):
+    parts, out = refs[:-1], refs[-1]
+    out[...] = functools.reduce(jnp.add, [p[:16, :128].astype(f32) for p in parts])
+
+
+ARRIVE_COST = 20e9
+
+
+def arrive_call(parts):
+    return pl.pallas_call(
+        arrive_kernel,
+        out_shape=jax.ShapeDtypeStruct((16, 128), f32),
+        in_specs=[vmem()] * len(parts),
+        out_specs=vmem(),
+        compiler_params=params(2),
+        cost_estimate=cost(ARRIVE_COST, 0),
+        name="arrive",
+    )(*parts)
+
+
+def cached_kernel(query_all, _, *rest):
+    prefix, (accum, stats, query, keys, values) = rest[:SQ], rest[SQ:]
+    extent, _, rows = query_all.shape
+    span = prefix[0].shape[1]
+    for n, part in enumerate(prefix):
         at = slice(n * span, (n + 1) * span)
         for h in range(HQ):
             keys[h, at, :] = part[h * HEAD : (h + 1) * HEAD, :].T
         values[:, at] = part[QD:, :]
-
-
-PACK_COST = 20e9
-
-
-def pack_call(parts):
-    span = parts[0].shape[1]
-    return pl.pallas_call(
-        pack_kernel,
-        out_shape=[
-            jax.ShapeDtypeStruct((HQ, SQ * span, HEAD), bf16),
-            jax.ShapeDtypeStruct((QD, SQ * span), bf16),
-        ],
-        in_specs=[vmem()] * SQ,
-        out_specs=[vmem()] * 2,
-        compiler_params=params(2),
-        cost_estimate=cost(PACK_COST, 0),
-        name="pack",
-    )(*parts)
-
-
-def cached_kernel(query_all, keys, values, accum, stats, query):
-    extent, _, rows = query_all.shape
     for s in range(extent // SQ):
         for j in range(SQ):
             query[:, j * rows : (j + 1) * rows] = query_all[s * SQ + j]
@@ -216,22 +217,26 @@
             stats[s, 8 + h : 9 + h, :] = total
 
 
-def cached_call(queries, keys, values):
+def cached_call(queries, arrived, prefix):
     extent, _, rows = queries.shape
-    pairs = extent * rows * keys.shape[1] * HQ
+    span = prefix[0].shape[1]
     return pl.pallas_call(
         cached_kernel,
         out_shape=[
             jax.ShapeDtypeStruct((extent // SQ, QD, SQ * rows), f32),
             jax.ShapeDtypeStruct((extent // SQ, 16, SQ * rows), f32),
         ],
-        in_specs=[vmem()] * 3,
+        in_specs=[vmem()] * (2 + SQ),
         out_specs=[vmem()] * 2,
-        scratch_shapes=[pltpu.VMEM((QD, SQ * rows), bf16)],
+        scratch_shapes=[
+            pltpu.VMEM((QD, SQ * rows), bf16),
+            pltpu.VMEM((HQ, SQ * span, HEAD), bf16),
+            pltpu.VMEM((QD, SQ * span), bf16),
+        ],
         compiler_params=params(12),
         cost_estimate=cost(CACHED_COST, 0, 0),
         name="attend_cached",
-    )(queries, keys, values)
+    )(queries, arrived, *prefix)
 
 
 CACHED_COST = 1e9
@@ -276,33 +281,42 @@
                 jnp.int32, (rows, lanes.stop - lanes.start), 0
             )
             masks.append((key_at >= first[:, lanes]) & (key_at <= position[:, lanes]))
+        scores = []
         for h in range(HQ):
             head = slice(h * HEAD, (h + 1) * HEAD)
-            head_v = slice(QD + h * HEAD, QD + (h + 1) * HEAD)
             query = [query_all[query_square * SQ + j, head, :] for j in range(windows[-1][2])]
-            cached_top = stats[query_square, h : h + 1, :]
-            top = cached_top
-            pieces = []
             for (block, begin, end), mask in zip(windows, masks):
-                lanes = slice(begin * rows, end * rows)
                 score = jnp.dot(
                     pairs[block, head, :].T,
                     jnp.concatenate(query[begin:end], axis=1),
                     preferred_element_type=f32,
                 )
-                score = jnp.where(mask, score, NEG)
+                scores.append(jnp.where(mask, score, NEG))
+        states = []
+        for h in range(HQ):
+            cached_top = stats[query_square, h : h + 1, :]
+            top = cached_top
+            part = scores[h * len(windows) : (h + 1) * len(windows)]
+            for score, (block, begin, end) in zip(part, windows):
+                lanes = slice(begin * rows, end * rows)
                 level = jnp.max(score, axis=0, keepdims=True)
                 top = jnp.maximum(top, widen(level, lanes, width, NEG))
-                pieces.append((score, block, lanes))
             shrink = jnp.exp(cached_top - top)
             total = stats[query_square, 8 + h : 9 + h, :] * shrink
+            weights = []
+            for score, (block, begin, end) in zip(part, windows):
+                lanes = slice(begin * rows, end * rows)
+                weight = jnp.exp(score - top[:, lanes])
+                total = total + widen(jnp.sum(weight, axis=0, keepdims=True), lanes, width, 0.0)
+                weights.append(weight.astype(bf16))
+            states.append((top, shrink, total, weights))
+        for h, (top, shrink, total, weights) in enumerate(states):
+            head = slice(h * HEAD, (h + 1) * HEAD)
+            head_v = slice(QD + h * HEAD, QD + (h + 1) * HEAD)
             mixed = accum[query_square, head, :] * shrink
-            for score, block, lanes in pieces:
-                weights = jnp.exp(score - top[:, lanes])
-                total = total + widen(jnp.sum(weights, axis=0, keepdims=True), lanes, width, 0.0)
-                blended = jnp.dot(
-                    pairs[block, head_v, :], weights.astype(bf16), preferred_element_type=f32
-                )
+            for weight, (block, begin, end) in zip(weights, windows):
+                lanes = slice(begin * rows, end * rows)
+                blended = jnp.dot(pairs[block, head_v, :], weight, preferred_element_type=f32)
                 mixed = mixed + widen(blended, lanes, width, 0.0)
             out = (mixed * (1.0 / total)).astype(bf16)
             for j in range(SQ):
@@ -384,62 +398,29 @@
     )(tokens, rate, w_out, parts)
 
 
-def feed(first, second, w_up, w_gate, w_down, up_scale, gate_scale, keep, send):
+def mlp_kernel(first, second, w_up, w_gate, w_down, up_scale, gate_scale, keep, send):
     rows = first.shape[0]
     data = jnp.concatenate([first[...], second[...]], axis=0)
-    up = jnp.dot(data, w_up(), preferred_element_type=f32) * over_rows(up_scale, 2 * rows)
-    gate = jnp.dot(data, w_gate(), preferred_element_type=f32)
+    up = jnp.dot(data, w_up[...], preferred_element_type=f32) * over_rows(up_scale, 2 * rows)
+    gate = jnp.dot(data, w_gate[...], preferred_element_type=f32)
     gate = gate * (over_rows(gate_scale, 2 * rows) * math.sqrt(D))
     act = (up * (gate / (1.0 + jnp.exp(-gate)))).astype(bf16)
-    part = jnp.dot(act, w_down(), preferred_element_type=f32)
+    part = jnp.dot(act, w_down[...], preferred_element_type=f32)
     keep[...] = part[:rows, :]
     send[...] = part[rows:, :].astype(bf16)
 
 
-def mlp_first_kernel(first, second, *rest):
-    sources, (keep, send), held, sems = rest[:5], rest[5:7], rest[7:12], rest[12]
-    copies = fetch(sources, held, sems)
-
-    def ready(n):
-        def get():
-            copies[n].wait()
-            return held[n][...]
-
-        return get
-
-    wait(copies[3:])
-    feed(first, second, ready(0), ready(1), ready(2), held[3], held[4], keep, send)
-
-
-def mlp_next_kernel(first, second, w_up, w_gate, w_down, up_scale, gate_scale, keep, send):
-    feed(
-        first,
-        second,
-        lambda: w_up[...],
-        lambda: w_gate[...],
-        lambda: w_down[...],
-        up_scale,
-        gate_scale,
-        keep,
-        send,
-    )
-
-
-def mlp_call(first, second, weights, held=False):
+def mlp_call(first, second, weights):
     rows = first.shape[0]
     units = weights[0].shape[1]
-    out_shape = [jax.ShapeDtypeStruct((rows, D), f32), jax.ShapeDtypeStruct((rows, D), bf16)]
-    if not held:
-        out_shape += [jax.ShapeDtypeStruct(w.shape, w.dtype) for w in weights]
-    return pl.pallas_call(
-        mlp_next_kernel if held else mlp_first_kernel,
-        out_shape=out_shape,
-        in_specs=[vmem()] * 2 + [vmem() if held else hbm()] * 5,
-        out_specs=[vmem()] * len(out_shape),
-        scratch_shapes=[] if held else [pltpu.SemaphoreType.DMA((5,))],
-        compiler_params=params(16),
+    return pl.pallas_call(
+        mlp_kernel,
+        out_shape=[jax.ShapeDtypeStruct((rows, D), f32), jax.ShapeDtypeStruct((rows, D), bf16)],
+        in_specs=[vmem()] * 7,
+        out_specs=[vmem()] * 2,
+        compiler_params=params(12),
         cost_estimate=cost(2 * 2 * rows * D * units * 3, 3 * D * units * 2, 2 * rows * units),
-        name="mlp_held" if held else "mlp",
+        name="mlp",
     )(first, second, *weights)
 
 
@@ -511,14 +492,12 @@
     own = tokens[0]
     rows = own.shape[0]
 
-    *cached, hidden, columns = prefix_call(
-        place, qk_scale, prefix_keys[0], prefix_values[0], own
-    )
+    cached = prefix_call(place, qk_scale, prefix_keys[0], prefix_values[0])
     prefix = [cached[0]] + [swap(cached[m], "tok", m) for m in range(1, SQ)]
-    queries, *sent = qkv_call(squares, place, hidden, columns, w_qkv)
+    queries, *sent = qkv_call(squares, place, own, qk_scale, w_qkv)
     suffix = [sent[0]] + [swap(sent[m], "tok", m) for m in range(1, SQ)]
     queries = lax.all_to_all(queries.reshape(extent, QD, rows), "tok", 0, 0)
-    accum, stats = cached_call(queries, *pack_call(prefix))
+    accum, stats = cached_call(queries, arrive_call(prefix), prefix)
     parts, w_out = suffix_call(place, seg_lengths, queries, accum, stats, suffix, w_out)
     parts = lax.all_to_all(parts, "tok", 0, 0)
     hidden, flat = project_call(own, attn_rate, w_out, parts)
@@ -526,11 +505,11 @@
     weights = (w_up, w_gate, w_down, up_scale, gate_scale)
     chips = lax.axis_size("grp") // 2
     remote = [swap(flat, "grp", 2 * c) for c in range(1, chips)]
-    keep, send, *weights = mlp_call(flat, swap(flat, "grp", 1), weights)
+    keep, send = mlp_call(flat, swap(flat, "grp", 1), weights)
     arrived = [swap(send, "grp", 1)]
     for c in range(1, chips):
         data, keep = lax.optimization_barrier((remote[c - 1], keep))
-        kept, send = mlp_call(data, swap(data, "grp", 1), weights, held=True)
+        kept, send = mlp_call(data, swap(data, "grp", 1), weights)
         arrived.append(swap(add_call(kept, swap(send, "grp", 1)), "grp", 2 * c))
     return final_call(hidden, mlp_rate, keep, arrived)[None]
 

time: 105 us -> 97.3 us (0.927)
  local copies, waits for them, and re-layouts: 10.1 us -> 0.07 us
  waiting for transfers between devices: 25.6 us -> 29 us
    unnamed x46 -> x24, local copies, waits for them, and re-layouts: 10.1 us -> 0.07 us
    all_to_all x1, waiting for transfers between devices: 5.45 us -> 10.6 us  [body(): queries = lax.all_to_all(queries.reshape(extent, QD, rows), 'tok', 0, 0)]
    pallas_call x3, Pallas kernels: 8.13 us -> 5.97 us  [the longest x2 5.96 us: mlp_call(): pl.pallas_call(mlp_kernel, out_shape=[jax.ShapeDtypeStruct((rows, D), f32...]
    pallas_call x1, Pallas kernels: 3.06 us -> 4.9 us  [qkv_call(): pl.pallas_call(functools.partial(qkv_kernel, squares), out_shape=[jax.Sha...]
    ppermute x12, waiting for transfers between devices: 20.1 us -> 18.3 us  [swap(): return lax.ppermute(shard, axis, [(j, j ^ mask) for j in range(length)])]
    pallas_call x1, Pallas kernels: 1.36 us -> 2.91 us  [prefix_call(): pl.pallas_call(prefix_kernel, out_shape=[jax.ShapeDtypeStruct((2 * QD, ro...]
    pallas_call x1, Pallas kernels: 4.64 us -> 3.2 us  [suffix_call(): pl.pallas_call(suffix_kernel, out_shape=[jax.ShapeDtypeStruct((extent, QD...]
  transfers between devices with their start and end apart: 13 -> 13, of which waited for: 6 -> 6; matrix products, arithmetic and copies ran while one was open for 0% -> 0% of each run, Pallas kernels for 17% -> 18%
where the time goes in v3:
time: 97.3 us; the launch traced here: 97.1 us
  Pallas kernels  29.3 us (30%)
  waiting for transfers between devices  29 us (30%)
  blocking collectives  20.2 us (21%)
  starting transfers between devices  18.1 us (19%)
    all_to_all x1, blocking collectives, body(): parts = lax.all_to_all(parts, 'tok', 0, 0)  20.2 us
    ppermute x12, waiting for transfers between devices, swap(): return lax.ppermute(shard, axis, [(j, j ^ mask) for j in range(length)])  18.3 us
    ppermute x12, starting transfers between devices, swap(): return lax.ppermute(shard, axis, [(j, j ^ mask) for j in range(length)])  11.9 us
    all_to_all x1, waiting for transfers between devices, body(): queries = lax.all_to_all(queries.reshape(extent, QD, rows), 'tok', 0, 0)  10.6 us
    pallas_call x1, Pallas kernels, cached_call(): pl.pallas_call(cached_kernel, out_shape=[jax.ShapeDtypeStruct((extent //...  9.73 us
    all_to_all x1, starting transfers between devices, body(): queries = lax.all_to_all(queries.reshape(extent, QD, rows), 'tok', 0, 0)  6.21 us
    pallas_call x2, Pallas kernels, mlp_call(): pl.pallas_call(mlp_kernel, out_shape=[jax.ShapeDtypeStruct((rows, D), f32...  5.96 us
    pallas_call x1, Pallas kernels, qkv_call(): pl.pallas_call(functools.partial(qkv_kernel, squares), out_shape=[jax.Sha...  4.9 us
  transfers between devices with their start and end apart: 13, of which 6 were waited for; matrix products, arithmetic and copies ran while one was open for 0% of the time, Pallas kernels for 18%

profile of v3, /device:TPU:0, one launch (start us, length us, event | category | flops | bytes accessed | tf_op | source)
XLA Modules:
  0.0 97.1 jit_solution(5627847714624016791)
XLA Ops:
  0.0 0.0 copy-start.3
  0.0 0.0 copy-start.9
  0.0 2.9 %prefix_prep.1 = (bf16[640,256]{1,0:T(8,128)(2,1)}, bf16[640,256]{1,0:T(8,128)(2,1)}, bf16[640,256]{1,0:T(8,128)(2,1)}, bf16[640,256]{1,0:T(8,128)(2,1)}) custom-call(s32[1]{0:T(128)} %bitcast.1.place, f32[1280]{0:T(1024)} %rest_0_.1, bf16[256,1280]{1,0:T(8,128)(2,1)} %bitcast.8, bf16[256,1280]{1,0:T(8,128)(2,1)} %bitcast.9), custom_call_target="tpu_custom_call" | custom-call | flops 49999998976 | bytes 2621440 | tf_op jit(solution)/shard_map/prefix_prep/pallas_call | solution.py:117
  2.9 3.0 %collective-permute-start = (bf16[640,256]{1,0:T(8,128)(2,1)}, bf16[640,256]{1,0:T(8,128)(2,1)S(1)}, u32[]{:S(2)}, u32[]{:S(2)}) collective-permute-start(bf16[640,256]{1,0:T(8,128)(2,1)} %get-tuple-element.28), channel_id=1, source_target_pairs={{0,1},{1,0},{2,3},{3,2},{4,5},{5,4},{6,7},{7,6},{8,9},{9,8},{10,11... | collective-permute-start | bytes 983048 | tf_op jit(solution)/shard_map/ppermute | solution.py:470
  5.9 1.6 %collective-permute-start.1 = (bf16[640,256]{1,0:T(8,128)(2,1)}, bf16[640,256]{1,0:T(8,128)(2,1)S(1)}, u32[]{:S(2)}, u32[]{:S(2)}) collective-permute-start(bf16[640,256]{1,0:T(8,128)(2,1)} %get-tuple-element.29), channel_id=1, source_target_pairs={{0,2},{1,3},{2,0},{3,1},{4,6},{5,7},{6,4},{7,5},{8,10},{9,11},{10,... | collective-permute-start | bytes 983048 | tf_op jit(solution)/shard_map/ppermute | solution.py:470
  7.5 0.0 collective-permute-start.2
  7.5 0.0 copy-done.3
  7.5 0.0 copy-done.9
  7.5 0.0 copy-start.11
  7.5 4.9 %qkv.1 = (bf16[2560,128]{1,0:T(8,128)(2,1)}, bf16[640,128]{1,0:T(8,128)(2,1)S(1)}, bf16[640,128]{1,0:T(8,128)(2,1)S(1)}, bf16[640,128]{1,0:T(8,128)(2,1)S(1)}, bf16[640,128]{1,0:T(8,128)(2,1)S(1)}) custom-call(s32[1]{0:T(128)} %bitcast.1.place, bf16[128,1280]{1,0:T(8,128)(2,1)S(1)} %bitcast.6, f32[1280]{0:T(1024)S(1)} %copy-done.9, bf16[1280,3840]{1,0:T(8,128)(2,1)} %w_hbm.1), custom_call_target="tpu_custom_call" | custom-call | flops 49999998976 | bytes 9830400 | tf_op jit(solution)/shard_map/qkv/pallas_call | solution.py:159
  12.5 6.2 %all-to-all-start = ((bf16[8,320,128]{2,1,0:T(8,128)(2,1)}), bf16[8,320,128]{2,1,0:T(8,128)(2,1)S(1)}, u32[]{:S(2)}, u32[]{:S(2)}) async-start(bf16[8,320,128]{2,1,0:T(8,128)(2,1)} %bitcast.2), calls=%async_computation | async-start | bytes 1310720 | tf_op jit(solution)/shard_map/all_to_all | solution.py:499
  18.7 2.0 %collective-permute-start.3 = (bf16[640,128]{1,0:T(8,128)(2,1)S(1)}, bf16[640,128]{1,0:T(8,128)(2,1)S(1)}, u32[]{:S(2)}, u32[]{:S(2)}) collective-permute-start(bf16[640,128]{1,0:T(8,128)(2,1)S(1)} %get-tuple-element.34), channel_id=1, source_target_pairs={{0,1},{1,0},{2,3},{3,2},{4,5},{5,4},{6,7},{7,6},{8,9},{9,8},{10,11... | collective-permute-start | bytes 491528 | tf_op jit(solution)/shard_map/ppermute | solution.py:470
  20.7 1.5 %collective-permute-start.4 = (bf16[640,128]{1,0:T(8,128)(2,1)S(1)}, bf16[640,128]{1,0:T(8,128)(2,1)S(1)}, u32[]{:S(2)}, u32[]{:S(2)}) collective-permute-start(bf16[640,128]{1,0:T(8,128)(2,1)S(1)} %get-tuple-element.35), channel_id=1, source_target_pairs={{0,2},{1,3},{2,0},{3,1},{4,6},{5,7},{6,4},{7,5},{8,10},{9,11},{10,... | collective-permute-start | bytes 491528 | tf_op jit(solution)/shard_map/ppermute | solution.py:470
  22.2 0.0 collective-permute-done.refs_1_.rest_1_
  22.2 0.0 collective-permute-start.5
  22.2 0.0 collective-permute-done.1.refs_2_.rest_2_
  22.2 1.8 %collective-permute-done.2.refs_3_.rest_3_ = bf16[640,256]{1,0:T(8,128)(2,1)S(1)} collective-permute-done((bf16[640,256]{1,0:T(8,128)(2,1)}, bf16[640,256]{1,0:T(8,128)(2,1)S(1)}, u32[]{:S(2)}, u32[]{:S(2)}) %collective-permute-start.2) | collective-permute-done | bytes 327712 | tf_op jit(solution)/shard_map/ppermute | solution.py:470
  24.0 0.0 copy-done.11
  24.0 0.0 copy-start.10
  24.0 10.6 %all-to-all-done.query_all = bf16[8,320,128]{2,1,0:T(8,128)(2,1)S(1)} async-done(((bf16[8,320,128]{2,1,0:T(8,128)(2,1)}), bf16[8,320,128]{2,1,0:T(8,128)(2,1)S(1)}, u32[]{:S(2)}, u32[]{:S(2)}) %all-to-all-start) | async-done | bytes 655392 | tf_op jit(solution)/shard_map/all_to_all | solution.py:499
  34.7 0.0 copy-start.8
  34.7 9.7 %attend_cached.1 = (f32[2,320,512]{2,1,0:T(8,128)S(1)}, f32[2,16,512]{2,1,0:T(8,128)S(1)}) custom-call(bf16[8,320,128]{2,1,0:T(8,128)(2,1)S(1)} %all-to-all-done.query_all, f32[16,128]{1,0:T(8,128)S(1)} %arrive.1._, bf16[640,256]{1,0:T(8,128)(2,1)S(1)} %copy-done.11, bf16[640,256]{1,0:T(8,128)(2,1)S(1)} %collective-permute-done.refs_1_.rest_1_, ...), custom_call_target="tpu_custom_call" | custom-call | flops 1000000000 | tf_op jit(solution)/shard_map/attend_cached/pallas_call | solution.py:223
  44.4 0.0 collective-permute-done.3.rest_1_
  44.4 0.0 collective-permute-done.4.rest_2_
  44.4 0.0 collective-permute-done.5.rest_3_
  44.4 0.0 copy-done.10
  44.5 0.0 copy-done.8
  44.5 0.0 copy-start.6
  44.5 0.0 copy-start.1
  44.5 0.0 copy-start.2
  44.5 3.2 %attend_suffix.1 = (bf16[8,336,128]{2,1,0:T(8,128)(2,1)S(1)}, bf16[1280,1280]{1,0:T(8,128)(2,1)S(1)}) custom-call(s32[1]{0:T(128)} %bitcast.1.place, s32[1,16]{1,0:T(1,128)S(1)} %copy-done.10, bf16[8,320,128]{2,1,0:T(8,128)(2,1)S(1)} %all-to-all-done.query_all, f32[2,320,512]{2,1,0:T(8,128)S(1)} %get-tuple-element.31.accum, ...), custom_call_target="tpu_custom_call" | custom-call | flops 20000000000 | bytes 8388608 | tf_op jit(solution)/shard_map/attend_suffix/pallas_call | solution.py:336
  47.7 0.0 copy-start
  47.7 0.0 copy-start.4
  47.7 0.0 copy-start.5
  47.7 20.2 %all_to_all.10.parts = bf16[8,336,128]{2,1,0:T(8,128)(2,1)S(1)} all-to-all(bf16[8,336,128]{2,1,0:T(8,128)(2,1)S(1)} %get-tuple-element.38), channel_id=1, replica_groups=mesh['grp'=4,'tok'=8] {'tok'}, dimensions={0} | all-to-all | bytes 1376256 | tf_op jit(solution)/shard_map/all_to_all | solution.py:502
  68.0 0.0 copy-done.6
  68.0 1.3 %project.1 = (f32[128,1280]{1,0:T(8,128)S(1)}, bf16[128,1280]{1,0:T(8,128)(2,1)S(1)}) custom-call(bf16[128,1280]{1,0:T(8,128)(2,1)S(1)} %bitcast.7, f32[1280]{0:T(1024)S(1)} %copy-done.6, bf16[1280,1280]{1,0:T(8,128)(2,1)S(1)} %get-tuple-element.37.w_out, bf16[8,336,128]{2,1,0:T(8,128)(2,1)S(1)} %all_to_all.10.parts), custom_call_target="tpu_custom_call" | custom-call | flops 419430400 | bytes 3276800 | tf_op jit(solution)/shard_map/project/pallas_call | solution.py:389
  69.2 0.1 collective-permute-start.7
  69.3 1.6 %collective-permute-start.6 = (bf16[128,1280]{1,0:T(8,128)(2,1)S(1)}, bf16[128,1280]{1,0:T(8,128)(2,1)S(1)}, u32[]{:S(2)}, u32[]{:S(2)}) collective-permute-start(bf16[128,1280]{1,0:T(8,128)(2,1)S(1)} %get-tuple-element.40.first), channel_id=1, source_target_pairs={{0,16},{8,24},{16,0},{24,8},{1,17},{9,25},{17,1},{25,9},{2,18},{10... | collective-permute-start | bytes 983048 | tf_op jit(solution)/shard_map/ppermute | solution.py:470
  70.9 0.0 collective-permute-done.7.second
  70.9 0.0 copy-done.1
  70.9 0.0 copy-done.2
  70.9 0.0 copy-done
  70.9 0.0 copy-done.4
  71.0 0.0 copy-done.5
  71.0 3.0 %mlp.2 = (f32[128,1280]{1,0:T(8,128)S(1)}, bf16[128,1280]{1,0:T(8,128)(2,1)S(1)}) custom-call(bf16[128,1280]{1,0:T(8,128)(2,1)S(1)} %get-tuple-element.40.first, bf16[128,1280]{1,0:T(8,128)(2,1)S(1)} %collective-permute-done.7.second, bf16[1280,1280]{1,0:T(8,128)(2,1)S(1)} %copy-done, bf16[1280,1280]{1,0:T(8,128)(2,1)S(1)} %copy-done.1, ...), custom_call_target="tpu_custom_call" | custom-call | flops 2516582400 | bytes 9830400 | tf_op jit(solution)/shard_map/mlp/pallas_call | solution.py:416
  74.0 5.5 %collective-permute-done.6.first = bf16[128,1280]{1,0:T(8,128)(2,1)S(1)} collective-permute-done((bf16[128,1280]{1,0:T(8,128)(2,1)S(1)}, bf16[128,1280]{1,0:T(8,128)(2,1)S(1)}, u32[]{:S(2)}, u32[]{:S(2)}) %collective-permute-start.6) | collective-permute-done | bytes 327712 | tf_op jit(solution)/shard_map/ppermute | solution.py:470
  79.4 0.0 copy-start.7
  79.5 0.0 collective-permute-start.9
  79.5 1.6 %collective-permute-done.9.second = bf16[128,1280]{1,0:T(8,128)(2,1)S(1)} collective-permute-done((bf16[128,1280]{1,0:T(8,128)(2,1)S(1)}, bf16[128,1280]{1,0:T(8,128)(2,1)S(1)}, u32[]{:S(2)}, u32[]{:S(2)}) %collective-permute-start.9) | collective-permute-done | bytes 327712 | tf_op jit(solution)/shard_map/ppermute | solution.py:470
  81.1 3.0 %mlp.3 = (f32[128,1280]{1,0:T(8,128)S(1)}, bf16[128,1280]{1,0:T(8,128)(2,1)S(1)}) custom-call(bf16[128,1280]{1,0:T(8,128)(2,1)S(1)} %collective-permute-done.6.first, bf16[128,1280]{1,0:T(8,128)(2,1)S(1)} %collective-permute-done.9.second, bf16[1280,1280]{1,0:T(8,128)(2,1)S(1)} %copy-done, bf16[1280,1280]{1,0:T(8,128)(2,1)S(1)} %copy-done.1, ...), custom_call_target="tpu_custom_call" | custom-call | flops 2516582400 | bytes 9830400 | tf_op jit(solution)/shard_map/mlp/pallas_call | solution.py:416
  84.1 0.2 collective-permute-start.10
  84.3 0.4 collective-permute-start.8
  84.6 1.1 %collective-permute-done.10.arrived = bf16[128,1280]{1,0:T(8,128)(2,1)S(1)} collective-permute-done((bf16[128,1280]{1,0:T(8,128)(2,1)S(1)}, bf16[128,1280]{1,0:T(8,128)(2,1)S(1)}, u32[]{:S(2)}, u32[]{:S(2)}) %collective-permute-start.10) | collective-permute-done | bytes 327712 | tf_op jit(solution)/shard_map/ppermute | solution.py:470
  85.8 0.1 add_partials.1
  85.8 1.6 %collective-permute-start.11 = (bf16[128,1280]{1,0:T(8,128)(2,1)S(1)}, bf16[128,1280]{1,0:T(8,128)(2,1)S(1)}, u32[]{:S(2)}, u32[]{:S(2)}) collective-permute-start(bf16[128,1280]{1,0:T(8,128)(2,1)S(1)} %add_partials.1), channel_id=1, source_target_pairs={{0,16},{8,24},{16,0},{24,8},{1,17},{9,25},{17,1},{25,9},{2,18},{10... | collective-permute-start | bytes 983048 | tf_op jit(solution)/shard_map/ppermute | solution.py:470
  87.4 0.0 collective-permute-done.8.rest_0_
  87.4 8.2 %collective-permute-done.11.rest_1_ = bf16[128,1280]{1,0:T(8,128)(2,1)S(1)} collective-permute-done((bf16[128,1280]{1,0:T(8,128)(2,1)S(1)}, bf16[128,1280]{1,0:T(8,128)(2,1)S(1)}, u32[]{:S(2)}, u32[]{:S(2)}) %collective-permute-start.11) | collective-permute-done | bytes 327712 | tf_op jit(solution)/shard_map/ppermute | solution.py:470
  95.6 0.0 copy-done.7
  95.6 1.3 %finish.1 = bf16[128,1280]{1,0:T(8,128)(2,1)} custom-call(f32[128,1280]{1,0:T(8,128)S(1)} %get-tuple-element.39.hidden, f32[1280]{0:T(1024)S(1)} %copy-done.7, f32[128,1280]{1,0:T(8,128)S(1)} %get-tuple-element.42.kept, bf16[128,1280]{1,0:T(8,128)(2,1)S(1)} %collective-permute-done.8.rest_0_, bf16[128,1280]{1,0:T(8,128)(2,1)S(1)} %collective-permute-done.11.rest_1_), custom_call_target="tpu_custom_call" | custom-call | flops 1638400 | bytes 1966080 | tf_op jit(solution)/shard_map/finish/pallas_call | solution.py:456
  (1 shorter events, 0.0 us)
Async XLA Ops:
  0.0 7.5 %copy-start.3 = (bf16[1,128,1280]{2,1,0:T(8,128)(2,1)S(1)}, bf16[1,128,1280]{2,1,0:T(8,128)(2,1)}, u32[]{:S(2)}) copy-start(bf16[1,128,1280]{2,1,0:T(8,128)(2,1)} %param.14) | copy-start | bytes 983044
  0.0 7.5 %copy-start.9 = (f32[1280]{0:T(1024)S(1)}, f32[1280]{0:T(1024)}, u32[]{:S(2)}) copy-start(f32[1280]{0:T(1024)} %rest_0_.1) | copy-start | bytes 15364
  2.9 19.2 %collective-permute-start = (bf16[640,256]{1,0:T(8,128)(2,1)}, bf16[640,256]{1,0:T(8,128)(2,1)S(1)}, u32[]{:S(2)}, u32[]{:S(2)}) collective-permute-start(bf16[640,256]{1,0:T(8,128)(2,1)} %get-tuple-element.28), channel_id=1, source_target_pairs={{0,1},{1,0},{2,3},{3,2},{4,5},{5,4},{6,7},{7,6},{8,9},{9,8},{10,11... | collective-permute-start | bytes 983048 | tf_op jit(solution)/shard_map/ppermute | solution.py:470
  5.9 16.3 %collective-permute-start.1 = (bf16[640,256]{1,0:T(8,128)(2,1)}, bf16[640,256]{1,0:T(8,128)(2,1)S(1)}, u32[]{:S(2)}, u32[]{:S(2)}) collective-permute-start(bf16[640,256]{1,0:T(8,128)(2,1)} %get-tuple-element.29), channel_id=1, source_target_pairs={{0,2},{1,3},{2,0},{3,1},{4,6},{5,7},{6,4},{7,5},{8,10},{9,11},{10,... | collective-permute-start | bytes 983048 | tf_op jit(solution)/shard_map/ppermute | solution.py:470
  7.5 16.5 %collective-permute-start.2 = (bf16[640,256]{1,0:T(8,128)(2,1)}, bf16[640,256]{1,0:T(8,128)(2,1)S(1)}, u32[]{:S(2)}, u32[]{:S(2)}) collective-permute-start(bf16[640,256]{1,0:T(8,128)(2,1)} %get-tuple-element.30), channel_id=1, source_target_pairs={{0,3},{1,2},{2,1},{3,0},{4,7},{5,6},{6,5},{7,4},{8,11},{9,10},{10,... | collective-permute-start | bytes 983048 | tf_op jit(solution)/shard_map/ppermute | solution.py:470
  7.5 16.5 %copy-start.11 = (bf16[640,256]{1,0:T(8,128)(2,1)S(1)}, bf16[640,256]{1,0:T(8,128)(2,1)}, u32[]{:S(2)}) copy-start(bf16[640,256]{1,0:T(8,128)(2,1)} %get-tuple-element.27.refs_0_.rest_0_) | copy-start | bytes 983044
  12.5 22.2 %all-to-all-start = ((bf16[8,320,128]{2,1,0:T(8,128)(2,1)}), bf16[8,320,128]{2,1,0:T(8,128)(2,1)S(1)}, u32[]{:S(2)}, u32[]{:S(2)}) async-start(bf16[8,320,128]{2,1,0:T(8,128)(2,1)} %bitcast.2), calls=%async_computation | async-start | bytes 1310720 | tf_op jit(solution)/shard_map/all_to_all | solution.py:499
  18.7 25.7 %collective-permute-start.3 = (bf16[640,128]{1,0:T(8,128)(2,1)S(1)}, bf16[640,128]{1,0:T(8,128)(2,1)S(1)}, u32[]{:S(2)}, u32[]{:S(2)}) collective-permute-start(bf16[640,128]{1,0:T(8,128)(2,1)S(1)} %get-tuple-element.34), channel_id=1, source_target_pairs={{0,1},{1,0},{2,3},{3,2},{4,5},{5,4},{6,7},{7,6},{8,9},{9,8},{10,11... | collective-permute-start | bytes 491528 | tf_op jit(solution)/shard_map/ppermute | solution.py:470
  20.7 23.7 %collective-permute-start.4 = (bf16[640,128]{1,0:T(8,128)(2,1)S(1)}, bf16[640,128]{1,0:T(8,128)(2,1)S(1)}, u32[]{:S(2)}, u32[]{:S(2)}) collective-permute-start(bf16[640,128]{1,0:T(8,128)(2,1)S(1)} %get-tuple-element.35), channel_id=1, source_target_pairs={{0,2},{1,3},{2,0},{3,1},{4,6},{5,7},{6,4},{7,5},{8,10},{9,11},{10,... | collective-permute-start | bytes 491528 | tf_op jit(solution)/shard_map/ppermute | solution.py:470
  22.2 22.3 %collective-permute-start.5 = (bf16[640,128]{1,0:T(8,128)(2,1)S(1)}, bf16[640,128]{1,0:T(8,128)(2,1)S(1)}, u32[]{:S(2)}, u32[]{:S(2)}) collective-permute-start(bf16[640,128]{1,0:T(8,128)(2,1)S(1)} %get-tuple-element.36), channel_id=1, source_target_pairs={{0,3},{1,2},{2,1},{3,0},{4,7},{5,6},{6,5},{7,4},{8,11},{9,10},{10,... | collective-permute-start | bytes 491528 | tf_op jit(solution)/shard_map/ppermute | solution.py:470
  24.0 20.4 %copy-start.10 = (s32[1,16]{1,0:T(1,128)S(1)}, s32[1,16]{1,0:T(1,128)}, u32[]{:S(2)}) copy-start(s32[1,16]{1,0:T(1,128)} %lengths.1) | copy-start | bytes 196
  34.7 9.8 %copy-start.8 = (bf16[1280,1280]{1,0:T(8,128)(2,1)S(1)}, bf16[1280,1280]{1,0:T(8,128)(2,1)}, u32[]{:S(2)}) copy-start(bf16[1280,1280]{1,0:T(8,128)(2,1)} %rest_4_.1) | copy-start | bytes 9830404
  44.5 23.5 %copy-start.6 = (f32[1280]{0:T(1024)S(1)}, f32[1280]{0:T(1024)}, u32[]{:S(2)}) copy-start(f32[1280]{0:T(1024)} %rate_hbm.2) | copy-start | bytes 15364
  44.5 26.5 %copy-start.1 = (bf16[1280,1280]{1,0:T(8,128)(2,1)S(1)}, bf16[1280,1280]{1,0:T(8,128)(2,1)}, u32[]{:S(2)}) copy-start(bf16[1280,1280]{1,0:T(8,128)(2,1)} %w_gate.3) | copy-start | bytes 9830404
  44.5 26.5 %copy-start.2 = (bf16[1280,1280]{1,0:T(8,128)(2,1)S(1)}, bf16[1280,1280]{1,0:T(8,128)(2,1)}, u32[]{:S(2)}) copy-start(bf16[1280,1280]{1,0:T(8,128)(2,1)} %w_down.3) | copy-start | bytes 9830404
  47.7 23.2 %copy-start = (bf16[1280,1280]{1,0:T(8,128)(2,1)S(1)}, bf16[1280,1280]{1,0:T(8,128)(2,1)}, u32[]{:S(2)}) copy-start(bf16[1280,1280]{1,0:T(8,128)(2,1)} %w_up.3) | copy-start | bytes 9830404
  47.7 23.2 %copy-start.4 = (f32[1280]{0:T(1024)S(1)}, f32[1280]{0:T(1024)}, u32[]{:S(2)}) copy-start(f32[1280]{0:T(1024)} %up_scale.3) | copy-start | bytes 15364
  47.7 23.2 %copy-start.5 = (f32[1280]{0:T(1024)S(1)}, f32[1280]{0:T(1024)}, u32[]{:S(2)}) copy-start(f32[1280]{0:T(1024)} %gate_scale.3) | copy-start | bytes 15364
  69.2 1.7 %collective-permute-start.7 = (bf16[128,1280]{1,0:T(8,128)(2,1)S(1)}, bf16[128,1280]{1,0:T(8,128)(2,1)S(1)}, u32[]{:S(2)}, u32[]{:S(2)}) collective-permute-start(bf16[128,1280]{1,0:T(8,128)(2,1)S(1)} %get-tuple-element.40.first), channel_id=1, source_target_pairs={{0,8},{8,0},{16,24},{24,16},{1,9},{9,1},{17,25},{25,17},{2,10},{10... | collective-permute-start | bytes 983048 | tf_op jit(solution)/shard_map/ppermute | solution.py:470
  69.3 10.1 %collective-permute-start.6 = (bf16[128,1280]{1,0:T(8,128)(2,1)S(1)}, bf16[128,1280]{1,0:T(8,128)(2,1)S(1)}, u32[]{:S(2)}, u32[]{:S(2)}) collective-permute-start(bf16[128,1280]{1,0:T(8,128)(2,1)S(1)} %get-tuple-element.40.first), channel_id=1, source_target_pairs={{0,16},{8,24},{16,0},{24,8},{1,17},{9,25},{17,1},{25,9},{2,18},{10... | collective-permute-start | bytes 983048 | tf_op jit(solution)/shard_map/ppermute | solution.py:470
  79.4 16.2 %copy-start.7 = (f32[1280]{0:T(1024)S(1)}, f32[1280]{0:T(1024)}, u32[]{:S(2)}) copy-start(f32[1280]{0:T(1024)} %rate_hbm.3) | copy-start | bytes 15364
  79.5 1.6 %collective-permute-start.9 = (bf16[128,1280]{1,0:T(8,128)(2,1)S(1)}, bf16[128,1280]{1,0:T(8,128)(2,1)S(1)}, u32[]{:S(2)}, u32[]{:S(2)}) collective-permute-start(bf16[128,1280]{1,0:T(8,128)(2,1)S(1)} %collective-permute-done.6.first), channel_id=1, source_target_pairs={{0,8},{8,0},{16,24},{24,16},{1,9},{9,1},{17,25},{25,17},{2,10},{10... | collective-permute-start | bytes 983048 | tf_op jit(solution)/shard_map/ppermute | solution.py:470
  84.1 1.7 %collective-permute-start.10 = (bf16[128,1280]{1,0:T(8,128)(2,1)S(1)}, bf16[128,1280]{1,0:T(8,128)(2,1)S(1)}, u32[]{:S(2)}, u32[]{:S(2)}) collective-permute-start(bf16[128,1280]{1,0:T(8,128)(2,1)S(1)} %get-tuple-element.46), channel_id=1, source_target_pairs={{0,8},{8,0},{16,24},{24,16},{1,9},{9,1},{17,25},{25,17},{2,10},{10... | collective-permute-start | bytes 983048 | tf_op jit(solution)/shard_map/ppermute | solution.py:470
  84.3 3.1 %collective-permute-start.8 = (bf16[128,1280]{1,0:T(8,128)(2,1)S(1)}, bf16[128,1280]{1,0:T(8,128)(2,1)S(1)}, u32[]{:S(2)}, u32[]{:S(2)}) collective-permute-start(bf16[128,1280]{1,0:T(8,128)(2,1)S(1)} %get-tuple-element.43), channel_id=1, source_target_pairs={{0,8},{8,0},{16,24},{24,16},{1,9},{9,1},{17,25},{25,17},{2,10},{10... | collective-permute-start | bytes 983048 | tf_op jit(solution)/shard_map/ppermute | solution.py:470
  85.8 9.8 %collective-permute-start.11 = (bf16[128,1280]{1,0:T(8,128)(2,1)S(1)}, bf16[128,1280]{1,0:T(8,128)(2,1)S(1)}, u32[]{:S(2)}, u32[]{:S(2)}) collective-permute-start(bf16[128,1280]{1,0:T(8,128)(2,1)S(1)} %add_partials.1), channel_id=1, source_target_pairs={{0,16},{8,24},{16,0},{24,8},{1,17},{9,25},{17,1},{25,9},{2,18},{10... | collective-permute-start | bytes 983048 | tf_op jit(solution)/shard_map/ppermute | solution.py:470

commit v4 on v3

--- a/solution.py
+++ b/solution.py
@@ -194,7 +194,7 @@
 
 
 def cached_kernel(query_all, _, *rest):
-    prefix, (accum, stats, query, keys, values) = rest[:SQ], rest[SQ:]
+    prefix, (accum, stats, keys, values) = rest[:SQ], rest[SQ:]
     extent, _, rows = query_all.shape
     span = prefix[0].shape[1]
     for n, part in enumerate(prefix):
@@ -202,19 +202,37 @@
         for h in range(HQ):
             keys[h, at, :] = part[h * HEAD : (h + 1) * HEAD, :].T
         values[:, at] = part[QD:, :]
-    for s in range(extent // SQ):
-        for j in range(SQ):
-            query[:, j * rows : (j + 1) * rows] = query_all[s * SQ + j]
-        for h in range(HQ):
-            head = slice(h * HEAD, (h + 1) * HEAD)
-            score = jnp.dot(keys[h], query[head, :], preferred_element_type=f32)
-            top = jnp.max(score, axis=0, keepdims=True)
+    steps = [(s, h) for s in range(extent // SQ) for h in range(HQ)]
+    cuts = [slice(k, k + 2 * span) for k in range(0, SQ * span, 2 * span)]
+
+    def queries(s, h):
+        head = slice(h * HEAD, (h + 1) * HEAD)
+        return jnp.concatenate([query_all[s * SQ + j, head, :] for j in range(SQ)], axis=1)
+
+    def part_scores(h, cut, query):
+        return jnp.dot(keys[h, cut, :], query, preferred_element_type=f32)
+
+    query = queries(0, 0)
+    scores = [part_scores(0, cut, query) for cut in cuts]
+    for n, (s, h) in enumerate(steps):
+        head = slice(h * HEAD, (h + 1) * HEAD)
+        top = functools.reduce(jnp.maximum, [jnp.max(x, axis=0, keepdims=True) for x in scores])
+        following = steps[n + 1] if n + 1 < len(steps) else None
+        if following:
+            query = queries(*following)
+        ahead, total, blended = [], 0.0, 0.0
+        for cut, score in zip(cuts, scores):
+            if following:
+                ahead.append(part_scores(following[1], cut, query))
             weights = jnp.exp(score - top)
-            total = jnp.sum(weights, axis=0, keepdims=True)
-            blended = jnp.dot(values[head, :], weights.astype(bf16), preferred_element_type=f32)
-            accum[s, head, :] = blended
-            stats[s, h : h + 1, :] = top
-            stats[s, 8 + h : 9 + h, :] = total
+            total = total + jnp.sum(weights, axis=0, keepdims=True)
+            blended = blended + jnp.dot(
+                values[head, cut], weights.astype(bf16), preferred_element_type=f32
+            )
+        accum[s, head, :] = blended
+        stats[s, h : h + 1, :] = top
+        stats[s, 8 + h : 9 + h, :] = total
+        scores = ahead
 
 
 def cached_call(queries, arrived, prefix):
@@ -229,11 +247,10 @@
         in_specs=[vmem()] * (2 + SQ),
         out_specs=[vmem()] * 2,
         scratch_shapes=[
-            pltpu.VMEM((QD, SQ * rows), bf16),
             pltpu.VMEM((HQ, SQ * span, HEAD), bf16),
             pltpu.VMEM((QD, SQ * span), bf16),
         ],
-        compiler_params=params(12),
+        compiler_params=params(16),
         cost_estimate=cost(CACHED_COST, 0, 0),
         name="attend_cached",
     )(queries, arrived, *prefix)
@@ -253,8 +270,9 @@
     return jnp.concatenate(pieces, axis=1)
 
 
-def suffix_kernel(place, lengths, query_all, accum, stats, *rest):
-    suffix, (w_hbm, outs, w_out, pairs, lse, sems) = rest[:SQ], rest[SQ:]
+def suffix_kernel(count, place, lengths, query_all, accum, stats, *rest):
+    suffix, w_hbm, rest = rest[:SQ], rest[SQ], rest[SQ + 1 :]
+    outs, (w_out, pairs, mixes, sems) = rest[:count], rest[count:]
     copies = fetch([w_hbm], [w_out], sems)
     extent, _, rows = query_all.shape
     i = lax.rem(place[0], SQ)
@@ -262,7 +280,6 @@
     width = SQ * rows
     for m in range(SQ):
         pairs[jnp.bitwise_xor(i, m)] = suffix[m][...]
-    lse[...] = jnp.zeros_like(lse)
     for shift in range(extent // SQ):
         query_square = jnp.bitwise_xor(square, shift)
         position = query_square * width + lax.broadcasted_iota(jnp.int32, (1, width), 1)
@@ -318,32 +335,31 @@
                 lanes = slice(begin * rows, end * rows)
                 blended = jnp.dot(pairs[block, head_v, :], weight, preferred_element_type=f32)
                 mixed = mixed + widen(blended, lanes, width, 0.0)
-            out = (mixed * (1.0 / total)).astype(bf16)
-            for j in range(SQ):
-                outs[query_square * SQ + j, head, :] = out[:, j * rows : (j + 1) * rows]
+            mixes[head, :] = mixed * (1.0 / total)
             level = top + jnp.log(total)
             high = level.astype(bf16).astype(f32)
             middle = (level - high).astype(bf16).astype(f32)
             for n, piece in enumerate((high, middle, level - high - middle)):
-                lse[n * HQ + h : n * HQ + h + 1, :] = piece
-        for j in range(SQ):
-            outs[query_square * SQ + j, QD:, :] = lse[:, j * rows : (j + 1) * rows].astype(bf16)
+                row = QD + n * HQ + h
+                mixes[row : row + 1, :] = piece
+        mixes[QD + LSE - 1 :, :] = jnp.zeros((1, width), f32)
+        for m in range(SQ):
+            lanes = pl.ds(pl.multiple_of(jnp.bitwise_xor(i, m) * rows, rows), rows)
+            outs[shift * SQ + m][...] = mixes[:, lanes].astype(bf16)
     wait(copies)
 
 
 def suffix_call(place, lengths, queries, accum, stats, suffix, w_out):
     extent, _, rows = queries.shape
     return pl.pallas_call(
-        suffix_kernel,
-        out_shape=[
-            jax.ShapeDtypeStruct((extent, QD + LSE, rows), bf16),
-            jax.ShapeDtypeStruct(w_out.shape, bf16),
-        ],
+        functools.partial(suffix_kernel, extent),
+        out_shape=[jax.ShapeDtypeStruct((QD + LSE, rows), bf16)] * extent
+        + [jax.ShapeDtypeStruct(w_out.shape, bf16)],
         in_specs=[smem(), smem()] + [vmem()] * (3 + SQ) + [hbm()],
-        out_specs=[vmem()] * 2,
+        out_specs=[vmem()] * (extent + 1),
         scratch_shapes=[
             pltpu.VMEM((SQ, 2 * QD, rows), bf16),
-            pltpu.VMEM((LSE, SQ * rows), f32),
+            pltpu.VMEM((QD + LSE, SQ * rows), f32),
             pltpu.SemaphoreType.DMA((1,)),
         ],
         compiler_params=params(8),
@@ -352,10 +368,14 @@
     )(place, lengths, queries, accum, stats, *suffix, w_out)
 
 
-def project_kernel(tokens_hbm, rate_hbm, w_out, parts, hidden_out, flat_out, mix, *rest):
-    tokens, rate, sems = rest
+def project_kernel(count, place, tokens_hbm, rate_hbm, w_out, *rest):
+    arrived, rest = rest[:count], rest[count:]
+    hidden_out, flat_out, mix, parts, tokens, rate, sems = rest
     copies = fetch((tokens_hbm, rate_hbm), (tokens, rate), sems)
-    squares = parts.shape[0] // SQ
+    squares = count // SQ
+    i = lax.rem(place[0], SQ)
+    for m, part in enumerate(arrived):
+        parts[m // SQ * SQ + jnp.bitwise_xor(i, m % SQ)] = part[...]
     for j in range(SQ):
         group = [parts.at[s * SQ + j] for s in range(squares)]
         levels = []
@@ -384,18 +404,22 @@
     flat_out[...] = hidden.astype(bf16)
 
 
-def project_call(tokens, rate, w_out, parts):
+def project_call(place, tokens, rate, w_out, parts):
     rows = tokens.shape[0]
     return pl.pallas_call(
-        project_kernel,
+        functools.partial(project_kernel, len(parts)),
         out_shape=[jax.ShapeDtypeStruct((rows, D), f32), jax.ShapeDtypeStruct((rows, D), bf16)],
-        in_specs=[hbm(), hbm(), vmem(), vmem()],
+        in_specs=[smem(), hbm(), hbm()] + [vmem()] * (1 + len(parts)),
         out_specs=[vmem()] * 2,
-        scratch_shapes=[pltpu.VMEM((D, rows), bf16)] + fetched(tokens, rate),
+        scratch_shapes=[
+            pltpu.VMEM((D, rows), bf16),
+            pltpu.VMEM((len(parts), *parts[0].shape), bf16),
+            *fetched(tokens, rate),
+        ],
         compiler_params=params(8),
         cost_estimate=cost(2 * rows * D * D, D * D * 2),
         name="project",
-    )(tokens, rate, w_out, parts)
+    )(place, tokens, rate, w_out, *parts)
 
 
 def mlp_kernel(first, second, w_up, w_gate, w_down, up_scale, gate_scale, keep, send):
@@ -498,9 +522,9 @@
     suffix = [sent[0]] + [swap(sent[m], "tok", m) for m in range(1, SQ)]
     queries = lax.all_to_all(queries.reshape(extent, QD, rows), "tok", 0, 0)
     accum, stats = cached_call(queries, arrive_call(prefix), prefix)
-    parts, w_out = suffix_call(place, seg_lengths, queries, accum, stats, suffix, w_out)
-    parts = lax.all_to_all(parts, "tok", 0, 0)
-    hidden, flat = project_call(own, attn_rate, w_out, parts)
+    *parts, w_out = suffix_call(place, seg_lengths, queries, accum, stats, suffix, w_out)
+    parts = parts[:1] + [swap(parts[m], "tok", m) for m in range(1, extent)]
+    hidden, flat = project_call(place, own, attn_rate, w_out, parts)
 
     weights = (w_up, w_gate, w_down, up_scale, gate_scale)
     chips = lax.axis_size("grp") // 2

time: 97.3 us -> 93 us (0.956)
  blocking collectives: 20.2 us -> 0 us
  starting transfers between devices: 18.1 us -> 30.8 us
  waiting for transfers between devices: 29 us -> 34.6 us
  Pallas kernels: 29.3 us -> 27 us
    all_to_all x1 -> x0, blocking collectives: 20.2 us -> none  [body(): parts = lax.all_to_all(parts, 'tok', 0, 0)]
    ppermute x12 -> x19, starting transfers between devices: 11.9 us -> 24.6 us  [swap(): return lax.ppermute(shard, axis, [(j, j ^ mask) for j in range(length)])]
    ppermute x12 -> x19, waiting for transfers between devices: 18.3 us -> 24 us  [swap(): return lax.ppermute(shard, axis, [(j, j ^ mask) for j in range(length)])]
    pallas_call x1, Pallas kernels: 9.73 us -> 6.99 us  [cached_call(): pl.pallas_call(cached_kernel, out_shape=[jax.ShapeDtypeStruct((extent //...]
  transfers between devices with their start and end apart: 13 -> 20, of which waited for: 6 -> 8; matrix products, arithmetic and copies ran while one was open for 0% -> 0% of each run, Pallas kernels for 18% -> 16%
where the time goes in v4:
time: 93 us; the launch traced here: 92.8 us
  waiting for transfers between devices  34.6 us (37%)
  starting transfers between devices  30.8 us (33%)
  Pallas kernels  27 us (29%)
    ppermute x19, starting transfers between devices, swap(): return lax.ppermute(shard, axis, [(j, j ^ mask) for j in range(length)])  24.6 us
    ppermute x19, waiting for transfers between devices, swap(): return lax.ppermute(shard, axis, [(j, j ^ mask) for j in range(length)])  24 us
    all_to_all x1, waiting for transfers between devices, body(): queries = lax.all_to_all(queries.reshape(extent, QD, rows), 'tok', 0, 0)  10.6 us
    pallas_call x1, Pallas kernels, cached_call(): pl.pallas_call(cached_kernel, out_shape=[jax.ShapeDtypeStruct((extent //...  6.99 us
    all_to_all x1, starting transfers between devices, body(): queries = lax.all_to_all(queries.reshape(extent, QD, rows), 'tok', 0, 0)  6.21 us
    pallas_call x2, Pallas kernels, mlp_call(): pl.pallas_call(mlp_kernel, out_shape=[jax.ShapeDtypeStruct((rows, D), f32...  5.98 us
    pallas_call x1, Pallas kernels, qkv_call(): pl.pallas_call(functools.partial(qkv_kernel, squares), out_shape=[jax.Sha...  4.92 us
    pallas_call x1, Pallas kernels, suffix_call(): pl.pallas_call(functools.partial(suffix_kernel, extent), out_shape=[jax.S...  3.32 us
  transfers between devices with their start and end apart: 20, of which 8 were waited for; matrix products, arithmetic and copies ran while one was open for 0% of the time, Pallas kernels for 16%

profile of v4, /device:TPU:0, one launch (start us, length us, event | category | flops | bytes accessed | tf_op | source)
XLA Modules:
  0.0 92.8 jit_solution(5033400153262137728)
XLA Ops:
  0.0 2.9 %prefix_prep.1 = (bf16[640,256]{1,0:T(8,128)(2,1)}, bf16[640,256]{1,0:T(8,128)(2,1)}, bf16[640,256]{1,0:T(8,128)(2,1)}, bf16[640,256]{1,0:T(8,128)(2,1)}) custom-call(s32[1]{0:T(128)} %bitcast.place, f32[1280]{0:T(1024)} %rest_0_.1, bf16[256,1280]{1,0:T(8,128)(2,1)} %bitcast.8, bf16[256,1280]{1,0:T(8,128)(2,1)} %bitcast.9), custom_call_target="tpu_custom_call" | custom-call | flops 49999998976 | bytes 2621440 | tf_op jit(solution)/shard_map/prefix_prep/pallas_call | solution.py:117
  2.9 3.0 %collective-permute-start = (bf16[640,256]{1,0:T(8,128)(2,1)}, bf16[640,256]{1,0:T(8,128)(2,1)S(1)}, u32[]{:S(2)}, u32[]{:S(2)}) collective-permute-start(bf16[640,256]{1,0:T(8,128)(2,1)} %get-tuple-element.35), channel_id=1, source_target_pairs={{0,1},{1,0},{2,3},{3,2},{4,5},{5,4},{6,7},{7,6},{8,9},{9,8},{10,11... | collective-permute-start | bytes 983048 | tf_op jit(solution)/shard_map/ppermute | solution.py:494
  5.9 1.6 %collective-permute-start.1 = (bf16[640,256]{1,0:T(8,128)(2,1)}, bf16[640,256]{1,0:T(8,128)(2,1)S(1)}, u32[]{:S(2)}, u32[]{:S(2)}) collective-permute-start(bf16[640,256]{1,0:T(8,128)(2,1)} %get-tuple-element.36), channel_id=1, source_target_pairs={{0,2},{1,3},{2,0},{3,1},{4,6},{5,7},{6,4},{7,5},{8,10},{9,11},{10,... | collective-permute-start | bytes 983048 | tf_op jit(solution)/shard_map/ppermute | solution.py:494
  7.5 0.0 collective-permute-start.2
  7.5 0.0 copy-done.3
  7.5 0.0 copy-done.9
  7.5 0.0 copy-start.11
  7.6 4.9 %qkv.1 = (bf16[2560,128]{1,0:T(8,128)(2,1)}, bf16[640,128]{1,0:T(8,128)(2,1)S(1)}, bf16[640,128]{1,0:T(8,128)(2,1)S(1)}, bf16[640,128]{1,0:T(8,128)(2,1)S(1)}, bf16[640,128]{1,0:T(8,128)(2,1)S(1)}) custom-call(s32[1]{0:T(128)} %bitcast.place, bf16[128,1280]{1,0:T(8,128)(2,1)S(1)} %bitcast.6, f32[1280]{0:T(1024)S(1)} %copy-done.9, bf16[1280,3840]{1,0:T(8,128)(2,1)} %w_hbm.1), custom_call_target="tpu_custom_call" | custom-call | flops 49999998976 | bytes 9830400 | tf_op jit(solution)/shard_map/qkv/pallas_call | solution.py:159
  12.5 6.2 %all-to-all-start = ((bf16[8,320,128]{2,1,0:T(8,128)(2,1)}), bf16[8,320,128]{2,1,0:T(8,128)(2,1)S(1)}, u32[]{:S(2)}, u32[]{:S(2)}) async-start(bf16[8,320,128]{2,1,0:T(8,128)(2,1)} %bitcast.2), calls=%async_computation | async-start | bytes 1310720 | tf_op jit(solution)/shard_map/all_to_all | solution.py:523
  18.7 2.0 %collective-permute-start.3 = (bf16[640,128]{1,0:T(8,128)(2,1)S(1)}, bf16[640,128]{1,0:T(8,128)(2,1)S(1)}, u32[]{:S(2)}, u32[]{:S(2)}) collective-permute-start(bf16[640,128]{1,0:T(8,128)(2,1)S(1)} %get-tuple-element.41), channel_id=1, source_target_pairs={{0,1},{1,0},{2,3},{3,2},{4,5},{5,4},{6,7},{7,6},{8,9},{9,8},{10,11... | collective-permute-start | bytes 491528 | tf_op jit(solution)/shard_map/ppermute | solution.py:494
  20.7 1.5 %collective-permute-start.4 = (bf16[640,128]{1,0:T(8,128)(2,1)S(1)}, bf16[640,128]{1,0:T(8,128)(2,1)S(1)}, u32[]{:S(2)}, u32[]{:S(2)}) collective-permute-start(bf16[640,128]{1,0:T(8,128)(2,1)S(1)} %get-tuple-element.42), channel_id=1, source_target_pairs={{0,2},{1,3},{2,0},{3,1},{4,6},{5,7},{6,4},{7,5},{8,10},{9,11},{10,... | collective-permute-start | bytes 491528 | tf_op jit(solution)/shard_map/ppermute | solution.py:494
  22.2 0.0 collective-permute-done.refs_1_.rest_1_
  22.2 0.0 collective-permute-start.5
  22.2 0.0 collective-permute-done.1.refs_2_.rest_2_
  22.2 1.8 %collective-permute-done.2.refs_3_.rest_3_ = bf16[640,256]{1,0:T(8,128)(2,1)S(1)} collective-permute-done((bf16[640,256]{1,0:T(8,128)(2,1)}, bf16[640,256]{1,0:T(8,128)(2,1)S(1)}, u32[]{:S(2)}, u32[]{:S(2)}) %collective-permute-start.2) | collective-permute-done | bytes 327712 | tf_op jit(solution)/shard_map/ppermute | solution.py:494
  24.0 0.0 copy-done.11
  24.0 0.0 copy-start.10
  24.0 10.6 %all-to-all-done.query_all = bf16[8,320,128]{2,1,0:T(8,128)(2,1)S(1)} async-done(((bf16[8,320,128]{2,1,0:T(8,128)(2,1)}), bf16[8,320,128]{2,1,0:T(8,128)(2,1)S(1)}, u32[]{:S(2)}, u32[]{:S(2)}) %all-to-all-start) | async-done | bytes 655392 | tf_op jit(solution)/shard_map/all_to_all | solution.py:523
  34.7 7.0 %attend_cached.1 = (f32[2,320,512]{2,1,0:T(8,128)S(1)}, f32[2,16,512]{2,1,0:T(8,128)S(1)}) custom-call(bf16[8,320,128]{2,1,0:T(8,128)(2,1)S(1)} %all-to-all-done.query_all, f32[16,128]{1,0:T(8,128)S(1)} %arrive.1._, bf16[640,256]{1,0:T(8,128)(2,1)S(1)} %copy-done.11, bf16[640,256]{1,0:T(8,128)(2,1)S(1)} %collective-permute-done.refs_1_.rest_1_, ...), custom_call_target="tpu_custom_call" | custom-call | flops 1000000000 | tf_op jit(solution)/shard_map/attend_cached/pallas_call | solution.py:241
  41.7 0.0 collective-permute-done.3.rest_1_
  41.7 0.0 collective-permute-done.4.rest_2_
  41.7 0.0 collective-permute-done.5.rest_3_
  41.7 0.0 copy-done.10
  41.7 0.0 copy-done.8
  41.7 0.0 copy-start.6
  41.7 0.0 copy-start.1
  41.7 0.0 copy-start.2
  41.8 3.3 %attend_suffix.1 = (bf16[336,128]{1,0:T(8,128)(2,1)S(1)}, bf16[336,128]{1,0:T(8,128)(2,1)S(1)}, bf16[336,128]{1,0:T(8,128)(2,1)S(1)}, bf16[336,128]{1,0:T(8,128)...) custom-call(s32[1]{0:T(128)} %bitcast.place, ...), custom_call_target="tpu_custom_call" | custom-call | flops 20000000000 | bytes 8388608 | tf_op jit(solution)/shard_map/attend_suffix/pallas_call | solution.py:354
  45.1 0.0 copy-start
  45.1 0.0 copy-start.4
  45.1 0.0 copy-start.5
  45.1 1.7 %collective-permute-start.6 = (bf16[336,128]{1,0:T(8,128)(2,1)S(1)}, bf16[336,128]{1,0:T(8,128)(2,1)S(1)}, u32[]{:S(2)}, u32[]{:S(2)}) collective-permute-start(bf16[336,128]{1,0:T(8,128)(2,1)S(1)} %get-tuple-element.46), channel_id=1, source_target_pairs={{0,1},{1,0},{2,3},{3,2},{4,5},{5,4},{6,7},{7,6},{8,9},{9,8},{10,11... | collective-permute-start | bytes 258056 | tf_op jit(solution)/shard_map/ppermute | solution.py:494
  46.8 1.9 %collective-permute-start.7 = (bf16[336,128]{1,0:T(8,128)(2,1)S(1)}, bf16[336,128]{1,0:T(8,128)(2,1)S(1)}, u32[]{:S(2)}, u32[]{:S(2)}) collective-permute-start(bf16[336,128]{1,0:T(8,128)(2,1)S(1)} %get-tuple-element.47), channel_id=1, source_target_pairs={{0,2},{1,3},{2,0},{3,1},{4,6},{5,7},{6,4},{7,5},{8,10},{9,11},{10,... | collective-permute-start | bytes 258056 | tf_op jit(solution)/shard_map/ppermute | solution.py:494
  48.7 1.4 %collective-permute-start.8 = (bf16[336,128]{1,0:T(8,128)(2,1)S(1)}, bf16[336,128]{1,0:T(8,128)(2,1)S(1)}, u32[]{:S(2)}, u32[]{:S(2)}) collective-permute-start(bf16[336,128]{1,0:T(8,128)(2,1)S(1)} %get-tuple-element.48), channel_id=1, source_target_pairs={{0,3},{1,2},{2,1},{3,0},{4,7},{5,6},{6,5},{7,4},{8,11},{9,10},{10,... | collective-permute-start | bytes 258056 | tf_op jit(solution)/shard_map/ppermute | solution.py:494
  50.1 1.1 %collective-permute-start.9 = (bf16[336,128]{1,0:T(8,128)(2,1)S(1)}, bf16[336,128]{1,0:T(8,128)(2,1)S(1)}, u32[]{:S(2)}, u32[]{:S(2)}) collective-permute-start(bf16[336,128]{1,0:T(8,128)(2,1)S(1)} %get-tuple-element.49), channel_id=1, source_target_pairs={{0,4},{1,5},{2,6},{3,7},{4,0},{5,1},{6,2},{7,3},{8,12},{9,13},{10,... | collective-permute-start | bytes 258056 | tf_op jit(solution)/shard_map/ppermute | solution.py:494
  51.2 1.8 %collective-permute-start.10 = (bf16[336,128]{1,0:T(8,128)(2,1)S(1)}, bf16[336,128]{1,0:T(8,128)(2,1)S(1)}, u32[]{:S(2)}, u32[]{:S(2)}) collective-permute-start(bf16[336,128]{1,0:T(8,128)(2,1)S(1)} %get-tuple-element.50), channel_id=1, source_target_pairs={{0,5},{1,4},{2,7},{3,6},{4,1},{5,0},{6,3},{7,2},{8,13},{9,12},{10,... | collective-permute-start | bytes 258056 | tf_op jit(solution)/shard_map/ppermute | solution.py:494
  53.0 0.0 collective-permute-done.6.rest_1_
  53.0 1.5 %collective-permute-start.11 = (bf16[336,128]{1,0:T(8,128)(2,1)S(1)}, bf16[336,128]{1,0:T(8,128)(2,1)S(1)}, u32[]{:S(2)}, u32[]{:S(2)}) collective-permute-start(bf16[336,128]{1,0:T(8,128)(2,1)S(1)} %get-tuple-element.51), channel_id=1, source_target_pairs={{0,6},{1,7},{2,4},{3,5},{4,2},{5,3},{6,0},{7,1},{8,14},{9,15},{10,... | collective-permute-start | bytes 258056 | tf_op jit(solution)/shard_map/ppermute | solution.py:494
  54.5 0.0 collective-permute-done.7.rest_2_
  54.5 3.3 %collective-permute-start.12 = (bf16[336,128]{1,0:T(8,128)(2,1)S(1)}, bf16[336,128]{1,0:T(8,128)(2,1)S(1)}, u32[]{:S(2)}, u32[]{:S(2)}) collective-permute-start(bf16[336,128]{1,0:T(8,128)(2,1)S(1)} %get-tuple-element.52), channel_id=1, source_target_pairs={{0,7},{1,6},{2,5},{3,4},{4,3},{5,2},{6,1},{7,0},{8,15},{9,14},{10,... | collective-permute-start | bytes 258056 | tf_op jit(solution)/shard_map/ppermute | solution.py:494
  57.8 0.0 collective-permute-done.8.rest_3_
  57.8 3.1 %collective-permute-done.9.rest_4_ = bf16[336,128]{1,0:T(8,128)(2,1)S(1)} collective-permute-done((bf16[336,128]{1,0:T(8,128)(2,1)S(1)}, bf16[336,128]{1,0:T(8,128)(2,1)S(1)}, u32[]{:S(2)}, u32[]{:S(2)}) %collective-permute-start.9) | collective-permute-done | bytes 86048 | tf_op jit(solution)/shard_map/ppermute | solution.py:494
  60.9 2.6 %collective-permute-done.10.rest_5_ = bf16[336,128]{1,0:T(8,128)(2,1)S(1)} collective-permute-done((bf16[336,128]{1,0:T(8,128)(2,1)S(1)}, bf16[336,128]{1,0:T(8,128)(2,1)S(1)}, u32[]{:S(2)}, u32[]{:S(2)}) %collective-permute-start.10) | collective-permute-done | bytes 86048 | tf_op jit(solution)/shard_map/ppermute | solution.py:494
  63.4 0.0 collective-permute-done.11.rest_6_
  63.4 0.0 collective-permute-done.12.rest_7_
  63.4 1.5 %project.1 = (f32[128,1280]{1,0:T(8,128)S(1)}, bf16[128,1280]{1,0:T(8,128)(2,1)S(1)}) custom-call(s32[1]{0:T(128)} %bitcast.place, bf16[128,1280]{1,0:T(8,128)(2,1)S(1)} %bitcast.7, f32[1280]{0:T(1024)S(1)} %copy-done.6, bf16[1280,1280]{1,0:T(8,128)(2,1)S(1)} %get-tuple-element.44.w_out, bf16[336,128]{1,0:T(8,128)(2,1)S(1)} %get-tuple-element.45.rest_0_, ...), custom_call_target="tpu_custom_call" | custom-call | flops 419430400 | bytes 3276800 | tf_op jit(solution)/shard_map/project/pallas_call | solution.py:409
  65.0 0.1 collective-permute-start.14
  65.0 1.6 %collective-permute-start.13 = (bf16[128,1280]{1,0:T(8,128)(2,1)S(1)}, bf16[128,1280]{1,0:T(8,128)(2,1)S(1)}, u32[]{:S(2)}, u32[]{:S(2)}) collective-permute-start(bf16[128,1280]{1,0:T(8,128)(2,1)S(1)} %get-tuple-element.54.first), channel_id=1, source_target_pairs={{0,16},{8,24},{16,0},{24,8},{1,17},{9,25},{17,1},{25,9},{2,18},{10... | collective-permute-start | bytes 983048 | tf_op jit(solution)/shard_map/ppermute | solution.py:494
  66.6 0.0 collective-permute-done.14.second
  66.7 0.0 copy-done.4
  66.7 0.0 copy-done.5
  66.7 3.0 %mlp.2 = (f32[128,1280]{1,0:T(8,128)S(1)}, bf16[128,1280]{1,0:T(8,128)(2,1)S(1)}) custom-call(bf16[128,1280]{1,0:T(8,128)(2,1)S(1)} %get-tuple-element.54.first, bf16[128,1280]{1,0:T(8,128)(2,1)S(1)} %collective-permute-done.14.second, bf16[1280,1280]{1,0:T(8,128)(2,1)S(1)} %copy-done, bf16[1280,1280]{1,0:T(8,128)(2,1)S(1)} %copy-done.1, ...), custom_call_target="tpu_custom_call" | custom-call | flops 2516582400 | bytes 9830400 | tf_op jit(solution)/shard_map/mlp/pallas_call | solution.py:440
  69.7 5.5 %collective-permute-done.13.first = bf16[128,1280]{1,0:T(8,128)(2,1)S(1)} collective-permute-done((bf16[128,1280]{1,0:T(8,128)(2,1)S(1)}, bf16[128,1280]{1,0:T(8,128)(2,1)S(1)}, u32[]{:S(2)}, u32[]{:S(2)}) %collective-permute-start.13) | collective-permute-done | bytes 327712 | tf_op jit(solution)/shard_map/ppermute | solution.py:494
  75.2 0.0 collective-permute-start.16
  75.2 1.6 %collective-permute-done.16.second = bf16[128,1280]{1,0:T(8,128)(2,1)S(1)} collective-permute-done((bf16[128,1280]{1,0:T(8,128)(2,1)S(1)}, bf16[128,1280]{1,0:T(8,128)(2,1)S(1)}, u32[]{:S(2)}, u32[]{:S(2)}) %collective-permute-start.16) | collective-permute-done | bytes 327712 | tf_op jit(solution)/shard_map/ppermute | solution.py:494
  76.8 3.0 %mlp.3 = (f32[128,1280]{1,0:T(8,128)S(1)}, bf16[128,1280]{1,0:T(8,128)(2,1)S(1)}) custom-call(bf16[128,1280]{1,0:T(8,128)(2,1)S(1)} %collective-permute-done.13.first, bf16[128,1280]{1,0:T(8,128)(2,1)S(1)} %collective-permute-done.16.second, bf16[1280,1280]{1,0:T(8,128)(2,1)S(1)} %copy-done, bf16[1280,1280]{1,0:T(8,128)(2,1)S(1)} %copy-done.1, ...), custom_call_target="tpu_custom_call" | custom-call | flops 2516582400 | bytes 9830400 | tf_op jit(solution)/shard_map/mlp/pallas_call | solution.py:440
  79.8 0.2 collective-permute-start.17
  80.0 0.4 collective-permute-start.15
  80.4 1.1 %collective-permute-done.17.arrived = bf16[128,1280]{1,0:T(8,128)(2,1)S(1)} collective-permute-done((bf16[128,1280]{1,0:T(8,128)(2,1)S(1)}, bf16[128,1280]{1,0:T(8,128)(2,1)S(1)}, u32[]{:S(2)}, u32[]{:S(2)}) %collective-permute-start.17) | collective-permute-done | bytes 327712 | tf_op jit(solution)/shard_map/ppermute | solution.py:494
  81.5 0.1 add_partials.1
  81.5 1.6 %collective-permute-start.18 = (bf16[128,1280]{1,0:T(8,128)(2,1)S(1)}, bf16[128,1280]{1,0:T(8,128)(2,1)S(1)}, u32[]{:S(2)}, u32[]{:S(2)}) collective-permute-start(bf16[128,1280]{1,0:T(8,128)(2,1)S(1)} %add_partials.1), channel_id=1, source_target_pairs={{0,16},{8,24},{16,0},{24,8},{1,17},{9,25},{17,1},{25,9},{2,18},{10... | collective-permute-start | bytes 983048 | tf_op jit(solution)/shard_map/ppermute | solution.py:494
  83.1 0.0 collective-permute-done.15.rest_0_
  83.1 8.2 %collective-permute-done.18.rest_1_ = bf16[128,1280]{1,0:T(8,128)(2,1)S(1)} collective-permute-done((bf16[128,1280]{1,0:T(8,128)(2,1)S(1)}, bf16[128,1280]{1,0:T(8,128)(2,1)S(1)}, u32[]{:S(2)}, u32[]{:S(2)}) %collective-permute-start.18) | collective-permute-done | bytes 327712 | tf_op jit(solution)/shard_map/ppermute | solution.py:494
  91.4 1.3 %finish.1 = bf16[128,1280]{1,0:T(8,128)(2,1)} custom-call(f32[128,1280]{1,0:T(8,128)S(1)} %get-tuple-element.53.hidden, f32[1280]{0:T(1024)S(1)} %copy-done.7, f32[128,1280]{1,0:T(8,128)S(1)} %get-tuple-element.56.kept, bf16[128,1280]{1,0:T(8,128)(2,1)S(1)} %collective-permute-done.15.rest_0_, bf16[128,1280]{1,0:T(8,128)(2,1)S(1)} %collective-permute-done.18.rest_1_), custom_call_target="tpu_custom_call" | custom-call | flops 1638400 | bytes 1966080 | tf_op jit(solution)/shard_map/finish/pallas_call | solution.py:480
  (10 shorter events, 0.0 us)
Async XLA Ops:
  0.0 7.5 %copy-start.3 = (bf16[1,128,1280]{2,1,0:T(8,128)(2,1)S(1)}, bf16[1,128,1280]{2,1,0:T(8,128)(2,1)}, u32[]{:S(2)}) copy-start(bf16[1,128,1280]{2,1,0:T(8,128)(2,1)} %param.14) | copy-start | bytes 983044
  0.0 7.5 %copy-start.9 = (f32[1280]{0:T(1024)S(1)}, f32[1280]{0:T(1024)}, u32[]{:S(2)}) copy-start(f32[1280]{0:T(1024)} %rest_0_.1) | copy-start | bytes 15364
  2.9 19.2 %collective-permute-start = (bf16[640,256]{1,0:T(8,128)(2,1)}, bf16[640,256]{1,0:T(8,128)(2,1)S(1)}, u32[]{:S(2)}, u32[]{:S(2)}) collective-permute-start(bf16[640,256]{1,0:T(8,128)(2,1)} %get-tuple-element.35), channel_id=1, source_target_pairs={{0,1},{1,0},{2,3},{3,2},{4,5},{5,4},{6,7},{7,6},{8,9},{9,8},{10,11... | collective-permute-start | bytes 983048 | tf_op jit(solution)/shard_map/ppermute | solution.py:494
  5.9 16.3 %collective-permute-start.1 = (bf16[640,256]{1,0:T(8,128)(2,1)}, bf16[640,256]{1,0:T(8,128)(2,1)S(1)}, u32[]{:S(2)}, u32[]{:S(2)}) collective-permute-start(bf16[640,256]{1,0:T(8,128)(2,1)} %get-tuple-element.36), channel_id=1, source_target_pairs={{0,2},{1,3},{2,0},{3,1},{4,6},{5,7},{6,4},{7,5},{8,10},{9,11},{10,... | collective-permute-start | bytes 983048 | tf_op jit(solution)/shard_map/ppermute | solution.py:494
  7.5 16.5 %collective-permute-start.2 = (bf16[640,256]{1,0:T(8,128)(2,1)}, bf16[640,256]{1,0:T(8,128)(2,1)S(1)}, u32[]{:S(2)}, u32[]{:S(2)}) collective-permute-start(bf16[640,256]{1,0:T(8,128)(2,1)} %get-tuple-element.37), channel_id=1, source_target_pairs={{0,3},{1,2},{2,1},{3,0},{4,7},{5,6},{6,5},{7,4},{8,11},{9,10},{10,... | collective-permute-start | bytes 983048 | tf_op jit(solution)/shard_map/ppermute | solution.py:494
  7.5 16.5 %copy-start.11 = (bf16[640,256]{1,0:T(8,128)(2,1)S(1)}, bf16[640,256]{1,0:T(8,128)(2,1)}, u32[]{:S(2)}) copy-start(bf16[640,256]{1,0:T(8,128)(2,1)} %get-tuple-element.34.refs_0_.rest_0_) | copy-start | bytes 983044
  12.5 22.2 %all-to-all-start = ((bf16[8,320,128]{2,1,0:T(8,128)(2,1)}), bf16[8,320,128]{2,1,0:T(8,128)(2,1)S(1)}, u32[]{:S(2)}, u32[]{:S(2)}) async-start(bf16[8,320,128]{2,1,0:T(8,128)(2,1)} %bitcast.2), calls=%async_computation | async-start | bytes 1310720 | tf_op jit(solution)/shard_map/all_to_all | solution.py:523
  18.7 23.0 %collective-permute-start.3 = (bf16[640,128]{1,0:T(8,128)(2,1)S(1)}, bf16[640,128]{1,0:T(8,128)(2,1)S(1)}, u32[]{:S(2)}, u32[]{:S(2)}) collective-permute-start(bf16[640,128]{1,0:T(8,128)(2,1)S(1)} %get-tuple-element.41), channel_id=1, source_target_pairs={{0,1},{1,0},{2,3},{3,2},{4,5},{5,4},{6,7},{7,6},{8,9},{9,8},{10,11... | collective-permute-start | bytes 491528 | tf_op jit(solution)/shard_map/ppermute | solution.py:494
  20.7 21.0 %collective-permute-start.4 = (bf16[640,128]{1,0:T(8,128)(2,1)S(1)}, bf16[640,128]{1,0:T(8,128)(2,1)S(1)}, u32[]{:S(2)}, u32[]{:S(2)}) collective-permute-start(bf16[640,128]{1,0:T(8,128)(2,1)S(1)} %get-tuple-element.42), channel_id=1, source_target_pairs={{0,2},{1,3},{2,0},{3,1},{4,6},{5,7},{6,4},{7,5},{8,10},{9,11},{10,... | collective-permute-start | bytes 491528 | tf_op jit(solution)/shard_map/ppermute | solution.py:494
  22.2 19.5 %collective-permute-start.5 = (bf16[640,128]{1,0:T(8,128)(2,1)S(1)}, bf16[640,128]{1,0:T(8,128)(2,1)S(1)}, u32[]{:S(2)}, u32[]{:S(2)}) collective-permute-start(bf16[640,128]{1,0:T(8,128)(2,1)S(1)} %get-tuple-element.43), channel_id=1, source_target_pairs={{0,3},{1,2},{2,1},{3,0},{4,7},{5,6},{6,5},{7,4},{8,11},{9,10},{10,... | collective-permute-start | bytes 491528 | tf_op jit(solution)/shard_map/ppermute | solution.py:494
  24.0 17.7 %copy-start.10 = (s32[1,16]{1,0:T(1,128)S(1)}, s32[1,16]{1,0:T(1,128)}, u32[]{:S(2)}) copy-start(s32[1,16]{1,0:T(1,128)} %lengths.1) | copy-start | bytes 196
  34.7 7.0 %copy-start.8 = (bf16[1280,1280]{1,0:T(8,128)(2,1)S(1)}, bf16[1280,1280]{1,0:T(8,128)(2,1)}, u32[]{:S(2)}) copy-start(bf16[1280,1280]{1,0:T(8,128)(2,1)} %rest_4_.1) | copy-start | bytes 9830404
  41.7 21.7 %copy-start.6 = (f32[1280]{0:T(1024)S(1)}, f32[1280]{0:T(1024)}, u32[]{:S(2)}) copy-start(f32[1280]{0:T(1024)} %rate_hbm.2) | copy-start | bytes 15364
  41.7 24.9 %copy-start.1 = (bf16[1280,1280]{1,0:T(8,128)(2,1)S(1)}, bf16[1280,1280]{1,0:T(8,128)(2,1)}, u32[]{:S(2)}) copy-start(bf16[1280,1280]{1,0:T(8,128)(2,1)} %w_gate.3) | copy-start | bytes 9830404
  41.7 24.9 %copy-start.2 = (bf16[1280,1280]{1,0:T(8,128)(2,1)S(1)}, bf16[1280,1280]{1,0:T(8,128)(2,1)}, u32[]{:S(2)}) copy-start(bf16[1280,1280]{1,0:T(8,128)(2,1)} %w_down.3) | copy-start | bytes 9830404
  45.1 21.6 %copy-start = (bf16[1280,1280]{1,0:T(8,128)(2,1)S(1)}, bf16[1280,1280]{1,0:T(8,128)(2,1)}, u32[]{:S(2)}) copy-start(bf16[1280,1280]{1,0:T(8,128)(2,1)} %w_up.3) | copy-start | bytes 9830404
  45.1 21.6 %copy-start.4 = (f32[1280]{0:T(1024)S(1)}, f32[1280]{0:T(1024)}, u32[]{:S(2)}) copy-start(f32[1280]{0:T(1024)} %up_scale.3) | copy-start | bytes 15364
  45.1 21.6 %copy-start.5 = (f32[1280]{0:T(1024)S(1)}, f32[1280]{0:T(1024)}, u32[]{:S(2)}) copy-start(f32[1280]{0:T(1024)} %gate_scale.3) | copy-start | bytes 15364
  45.1 7.9 %collective-permute-start.6 = (bf16[336,128]{1,0:T(8,128)(2,1)S(1)}, bf16[336,128]{1,0:T(8,128)(2,1)S(1)}, u32[]{:S(2)}, u32[]{:S(2)}) collective-permute-start(bf16[336,128]{1,0:T(8,128)(2,1)S(1)} %get-tuple-element.46), channel_id=1, source_target_pairs={{0,1},{1,0},{2,3},{3,2},{4,5},{5,4},{6,7},{7,6},{8,9},{9,8},{10,11... | collective-permute-start | bytes 258056 | tf_op jit(solution)/shard_map/ppermute | solution.py:494
  46.8 7.6 %collective-permute-start.7 = (bf16[336,128]{1,0:T(8,128)(2,1)S(1)}, bf16[336,128]{1,0:T(8,128)(2,1)S(1)}, u32[]{:S(2)}, u32[]{:S(2)}) collective-permute-start(bf16[336,128]{1,0:T(8,128)(2,1)S(1)} %get-tuple-element.47), channel_id=1, source_target_pairs={{0,2},{1,3},{2,0},{3,1},{4,6},{5,7},{6,4},{7,5},{8,10},{9,11},{10,... | collective-permute-start | bytes 258056 | tf_op jit(solution)/shard_map/ppermute | solution.py:494
  48.7 9.0 %collective-permute-start.8 = (bf16[336,128]{1,0:T(8,128)(2,1)S(1)}, bf16[336,128]{1,0:T(8,128)(2,1)S(1)}, u32[]{:S(2)}, u32[]{:S(2)}) collective-permute-start(bf16[336,128]{1,0:T(8,128)(2,1)S(1)} %get-tuple-element.48), channel_id=1, source_target_pairs={{0,3},{1,2},{2,1},{3,0},{4,7},{5,6},{6,5},{7,4},{8,11},{9,10},{10,... | collective-permute-start | bytes 258056 | tf_op jit(solution)/shard_map/ppermute | solution.py:494
  50.1 10.8 %collective-permute-start.9 = (bf16[336,128]{1,0:T(8,128)(2,1)S(1)}, bf16[336,128]{1,0:T(8,128)(2,1)S(1)}, u32[]{:S(2)}, u32[]{:S(2)}) collective-permute-start(bf16[336,128]{1,0:T(8,128)(2,1)S(1)} %get-tuple-element.49), channel_id=1, source_target_pairs={{0,4},{1,5},{2,6},{3,7},{4,0},{5,1},{6,2},{7,3},{8,12},{9,13},{10,... | collective-permute-start | bytes 258056 | tf_op jit(solution)/shard_map/ppermute | solution.py:494
  51.2 12.2 %collective-permute-start.10 = (bf16[336,128]{1,0:T(8,128)(2,1)S(1)}, bf16[336,128]{1,0:T(8,128)(2,1)S(1)}, u32[]{:S(2)}, u32[]{:S(2)}) collective-permute-start(bf16[336,128]{1,0:T(8,128)(2,1)S(1)} %get-tuple-element.50), channel_id=1, source_target_pairs={{0,5},{1,4},{2,7},{3,6},{4,1},{5,0},{6,3},{7,2},{8,13},{9,12},{10,... | collective-permute-start | bytes 258056 | tf_op jit(solution)/shard_map/ppermute | solution.py:494
  53.0 10.4 %collective-permute-start.11 = (bf16[336,128]{1,0:T(8,128)(2,1)S(1)}, bf16[336,128]{1,0:T(8,128)(2,1)S(1)}, u32[]{:S(2)}, u32[]{:S(2)}) collective-permute-start(bf16[336,128]{1,0:T(8,128)(2,1)S(1)} %get-tuple-element.51), channel_id=1, source_target_pairs={{0,6},{1,7},{2,4},{3,5},{4,2},{5,3},{6,0},{7,1},{8,14},{9,15},{10,... | collective-permute-start | bytes 258056 | tf_op jit(solution)/shard_map/ppermute | solution.py:494
  54.5 8.9 %collective-permute-start.12 = (bf16[336,128]{1,0:T(8,128)(2,1)S(1)}, bf16[336,128]{1,0:T(8,128)(2,1)S(1)}, u32[]{:S(2)}, u32[]{:S(2)}) collective-permute-start(bf16[336,128]{1,0:T(8,128)(2,1)S(1)} %get-tuple-element.52), channel_id=1, source_target_pairs={{0,7},{1,6},{2,5},{3,4},{4,3},{5,2},{6,1},{7,0},{8,15},{9,14},{10,... | collective-permute-start | bytes 258056 | tf_op jit(solution)/shard_map/ppermute | solution.py:494
  65.0 1.7 %collective-permute-start.14 = (bf16[128,1280]{1,0:T(8,128)(2,1)S(1)}, bf16[128,1280]{1,0:T(8,128)(2,1)S(1)}, u32[]{:S(2)}, u32[]{:S(2)}) collective-permute-start(bf16[128,1280]{1,0:T(8,128)(2,1)S(1)} %get-tuple-element.54.first), channel_id=1, source_target_pairs={{0,8},{8,0},{16,24},{24,16},{1,9},{9,1},{17,25},{25,17},{2,10},{10... | collective-permute-start | bytes 983048 | tf_op jit(solution)/shard_map/ppermute | solution.py:494
  65.0 10.1 %collective-permute-start.13 = (bf16[128,1280]{1,0:T(8,128)(2,1)S(1)}, bf16[128,1280]{1,0:T(8,128)(2,1)S(1)}, u32[]{:S(2)}, u32[]{:S(2)}) collective-permute-start(bf16[128,1280]{1,0:T(8,128)(2,1)S(1)} %get-tuple-element.54.first), channel_id=1, source_target_pairs={{0,16},{8,24},{16,0},{24,8},{1,17},{9,25},{17,1},{25,9},{2,18},{10... | collective-permute-start | bytes 983048 | tf_op jit(solution)/shard_map/ppermute | solution.py:494
  75.2 16.2 %copy-start.7 = (f32[1280]{0:T(1024)S(1)}, f32[1280]{0:T(1024)}, u32[]{:S(2)}) copy-start(f32[1280]{0:T(1024)} %rate_hbm.3) | copy-start | bytes 15364
  75.2 1.6 %collective-permute-start.16 = (bf16[128,1280]{1,0:T(8,128)(2,1)S(1)}, bf16[128,1280]{1,0:T(8,128)(2,1)S(1)}, u32[]{:S(2)}, u32[]{:S(2)}) collective-permute-start(bf16[128,1280]{1,0:T(8,128)(2,1)S(1)} %collective-permute-done.13.first), channel_id=1, source_target_pairs={{0,8},{8,0},{16,24},{24,16},{1,9},{9,1},{17,25},{25,17},{2,10},{10... | collective-permute-start | bytes 983048 | tf_op jit(solution)/shard_map/ppermute | solution.py:494
  79.8 1.7 %collective-permute-start.17 = (bf16[128,1280]{1,0:T(8,128)(2,1)S(1)}, bf16[128,1280]{1,0:T(8,128)(2,1)S(1)}, u32[]{:S(2)}, u32[]{:S(2)}) collective-permute-start(bf16[128,1280]{1,0:T(8,128)(2,1)S(1)} %get-tuple-element.60), channel_id=1, source_target_pairs={{0,8},{8,0},{16,24},{24,16},{1,9},{9,1},{17,25},{25,17},{2,10},{10... | collective-permute-start | bytes 983048 | tf_op jit(solution)/shard_map/ppermute | solution.py:494
  80.0 3.1 %collective-permute-start.15 = (bf16[128,1280]{1,0:T(8,128)(2,1)S(1)}, bf16[128,1280]{1,0:T(8,128)(2,1)S(1)}, u32[]{:S(2)}, u32[]{:S(2)}) collective-permute-start(bf16[128,1280]{1,0:T(8,128)(2,1)S(1)} %get-tuple-element.57), channel_id=1, source_target_pairs={{0,8},{8,0},{16,24},{24,16},{1,9},{9,1},{17,25},{25,17},{2,10},{10... | collective-permute-start | bytes 983048 | tf_op jit(solution)/shard_map/ppermute | solution.py:494
  81.5 9.8 %collective-permute-start.18 = (bf16[128,1280]{1,0:T(8,128)(2,1)S(1)}, bf16[128,1280]{1,0:T(8,128)(2,1)S(1)}, u32[]{:S(2)}, u32[]{:S(2)}) collective-permute-start(bf16[128,1280]{1,0:T(8,128)(2,1)S(1)} %add_partials.1), channel_id=1, source_target_pairs={{0,16},{8,24},{16,0},{24,8},{1,17},{9,25},{17,1},{25,9},{2,18},{10... | collective-permute-start | bytes 983048 | tf_op jit(solution)/shard_map/ppermute | solution.py:494

commit v5 on v4

--- a/solution.py
+++ b/solution.py
@@ -368,13 +368,14 @@
     )(place, lengths, queries, accum, stats, *suffix, w_out)
 
 
-def project_kernel(count, place, tokens_hbm, rate_hbm, w_out, *rest):
+def project_kernel(order, place, tokens_hbm, rate_hbm, w_out, *rest):
+    count = len(order)
     arrived, rest = rest[:count], rest[count:]
     hidden_out, flat_out, mix, parts, tokens, rate, sems = rest
     copies = fetch((tokens_hbm, rate_hbm), (tokens, rate), sems)
     squares = count // SQ
     i = lax.rem(place[0], SQ)
-    for m, part in enumerate(arrived):
+    for m, part in zip(order, arrived):
         parts[m // SQ * SQ + jnp.bitwise_xor(i, m % SQ)] = part[...]
     for j in range(SQ):
         group = [parts.at[s * SQ + j] for s in range(squares)]
@@ -407,7 +408,7 @@
 def project_call(place, tokens, rate, w_out, parts):
     rows = tokens.shape[0]
     return pl.pallas_call(
-        functools.partial(project_kernel, len(parts)),
+        functools.partial(project_kernel, list(parts)),
         out_shape=[jax.ShapeDtypeStruct((rows, D), f32), jax.ShapeDtypeStruct((rows, D), bf16)],
         in_specs=[smem(), hbm(), hbm()] + [vmem()] * (1 + len(parts)),
         out_specs=[vmem()] * 2,
@@ -419,7 +420,7 @@
         compiler_params=params(8),
         cost_estimate=cost(2 * rows * D * D, D * D * 2),
         name="project",
-    )(place, tokens, rate, w_out, *parts)
+    )(place, tokens, rate, w_out, *parts.values())
 
 
 def mlp_kernel(first, second, w_up, w_gate, w_down, up_scale, gate_scale, keep, send):
@@ -523,7 +524,8 @@
     queries = lax.all_to_all(queries.reshape(extent, QD, rows), "tok", 0, 0)
     accum, stats = cached_call(queries, arrive_call(prefix), prefix)
     *parts, w_out = suffix_call(place, seg_lengths, queries, accum, stats, suffix, w_out)
-    parts = parts[:1] + [swap(parts[m], "tok", m) for m in range(1, extent)]
+    order = [1, *range(SQ, extent), *range(SQ - 1, 1, -1)]
+    parts = {m: swap(parts[m], "tok", m) for m in order} | {0: parts[0]}
     hidden, flat = project_call(place, own, attn_rate, w_out, parts)
 
     weights = (w_up, w_gate, w_down, up_scale, gate_scale)

time: 93 us -> 91.4 us (0.983)
  starting transfers between devices: 30.8 us -> 28.9 us
    ppermute x19, starting transfers between devices: 24.6 us -> 22.7 us  [swap(): return lax.ppermute(shard, axis, [(j, j ^ mask) for j in range(length)])]
  transfers between devices with their start and end apart: 20 -> 20, of which waited for: 8 -> 11; matrix products, arithmetic and copies ran while one was open for 0% -> 0% of each run, Pallas kernels for 16% -> 16%
where the time goes in v5:
time: 91.4 us; the launch traced here: 91.2 us
  waiting for transfers between devices  34.8 us (38%)
  starting transfers between devices  28.9 us (32%)
  Pallas kernels  27 us (30%)
    ppermute x19, waiting for transfers between devices, swap(): return lax.ppermute(shard, axis, [(j, j ^ mask) for j in range(length)])  24.2 us
    ppermute x19, starting transfers between devices, swap(): return lax.ppermute(shard, axis, [(j, j ^ mask) for j in range(length)])  22.7 us
    all_to_all x1, waiting for transfers between devices, body(): queries = lax.all_to_all(queries.reshape(extent, QD, rows), 'tok', 0, 0)  10.6 us
    pallas_call x1, Pallas kernels, cached_call(): pl.pallas_call(cached_kernel, out_shape=[jax.ShapeDtypeStruct((extent //...  6.99 us
    all_to_all x1, starting transfers between devices, body(): queries = lax.all_to_all(queries.reshape(extent, QD, rows), 'tok', 0, 0)  6.21 us
    pallas_call x2, Pallas kernels, mlp_call(): pl.pallas_call(mlp_kernel, out_shape=[jax.ShapeDtypeStruct((rows, D), f32...  5.97 us
    pallas_call x1, Pallas kernels, qkv_call(): pl.pallas_call(functools.partial(qkv_kernel, squares), out_shape=[jax.Sha...  4.92 us
    pallas_call x1, Pallas kernels, suffix_call(): pl.pallas_call(functools.partial(suffix_kernel, extent), out_shape=[jax.S...  3.32 us
  transfers between devices with their start and end apart: 20, of which 11 were waited for; matrix products, arithmetic and copies ran while one was open for 0% of the time, Pallas kernels for 16%

profile of v5, /device:TPU:0, one launch (start us, length us, event | category | flops | bytes accessed | tf_op | source)
XLA Modules:
  0.0 91.2 jit_solution(4785592093696217315)
XLA Ops:
  0.0 2.9 %prefix_prep.1 = (bf16[640,256]{1,0:T(8,128)(2,1)}, bf16[640,256]{1,0:T(8,128)(2,1)}, bf16[640,256]{1,0:T(8,128)(2,1)}, bf16[640,256]{1,0:T(8,128)(2,1)}) custom-call(s32[1]{0:T(128)} %bitcast.place, f32[1280]{0:T(1024)} %rest_0_.1, bf16[256,1280]{1,0:T(8,128)(2,1)} %bitcast.8, bf16[256,1280]{1,0:T(8,128)(2,1)} %bitcast.9), custom_call_target="tpu_custom_call" | custom-call | flops 49999998976 | bytes 2621440 | tf_op jit(solution)/shard_map/prefix_prep/pallas_call | solution.py:117
  2.9 3.0 %collective-permute-start = (bf16[640,256]{1,0:T(8,128)(2,1)}, bf16[640,256]{1,0:T(8,128)(2,1)S(1)}, u32[]{:S(2)}, u32[]{:S(2)}) collective-permute-start(bf16[640,256]{1,0:T(8,128)(2,1)} %get-tuple-element.35), channel_id=1, source_target_pairs={{0,1},{1,0},{2,3},{3,2},{4,5},{5,4},{6,7},{7,6},{8,9},{9,8},{10,11... | collective-permute-start | bytes 983048 | tf_op jit(solution)/shard_map/ppermute | solution.py:495
  5.9 1.6 %collective-permute-start.1 = (bf16[640,256]{1,0:T(8,128)(2,1)}, bf16[640,256]{1,0:T(8,128)(2,1)S(1)}, u32[]{:S(2)}, u32[]{:S(2)}) collective-permute-start(bf16[640,256]{1,0:T(8,128)(2,1)} %get-tuple-element.36), channel_id=1, source_target_pairs={{0,2},{1,3},{2,0},{3,1},{4,6},{5,7},{6,4},{7,5},{8,10},{9,11},{10,... | collective-permute-start | bytes 983048 | tf_op jit(solution)/shard_map/ppermute | solution.py:495
  7.5 0.0 collective-permute-start.2
  7.5 0.0 copy-done.3
  7.5 0.0 copy-done.9
  7.5 0.0 copy-start.11
  7.6 4.9 %qkv.1 = (bf16[2560,128]{1,0:T(8,128)(2,1)}, bf16[640,128]{1,0:T(8,128)(2,1)S(1)}, bf16[640,128]{1,0:T(8,128)(2,1)S(1)}, bf16[640,128]{1,0:T(8,128)(2,1)S(1)}, bf16[640,128]{1,0:T(8,128)(2,1)S(1)}) custom-call(s32[1]{0:T(128)} %bitcast.place, bf16[128,1280]{1,0:T(8,128)(2,1)S(1)} %bitcast.6, f32[1280]{0:T(1024)S(1)} %copy-done.9, bf16[1280,3840]{1,0:T(8,128)(2,1)} %w_hbm.1), custom_call_target="tpu_custom_call" | custom-call | flops 49999998976 | bytes 9830400 | tf_op jit(solution)/shard_map/qkv/pallas_call | solution.py:159
  12.5 6.2 %all-to-all-start = ((bf16[8,320,128]{2,1,0:T(8,128)(2,1)}), bf16[8,320,128]{2,1,0:T(8,128)(2,1)S(1)}, u32[]{:S(2)}, u32[]{:S(2)}) async-start(bf16[8,320,128]{2,1,0:T(8,128)(2,1)} %bitcast.2), calls=%async_computation | async-start | bytes 1310720 | tf_op jit(solution)/shard_map/all_to_all | solution.py:524
  18.7 2.0 %collective-permute-start.3 = (bf16[640,128]{1,0:T(8,128)(2,1)S(1)}, bf16[640,128]{1,0:T(8,128)(2,1)S(1)}, u32[]{:S(2)}, u32[]{:S(2)}) collective-permute-start(bf16[640,128]{1,0:T(8,128)(2,1)S(1)} %get-tuple-element.41), channel_id=1, source_target_pairs={{0,1},{1,0},{2,3},{3,2},{4,5},{5,4},{6,7},{7,6},{8,9},{9,8},{10,11... | collective-permute-start | bytes 491528 | tf_op jit(solution)/shard_map/ppermute | solution.py:495
  20.7 1.5 %collective-permute-start.4 = (bf16[640,128]{1,0:T(8,128)(2,1)S(1)}, bf16[640,128]{1,0:T(8,128)(2,1)S(1)}, u32[]{:S(2)}, u32[]{:S(2)}) collective-permute-start(bf16[640,128]{1,0:T(8,128)(2,1)S(1)} %get-tuple-element.42), channel_id=1, source_target_pairs={{0,2},{1,3},{2,0},{3,1},{4,6},{5,7},{6,4},{7,5},{8,10},{9,11},{10,... | collective-permute-start | bytes 491528 | tf_op jit(solution)/shard_map/ppermute | solution.py:495
  22.2 0.0 collective-permute-done.refs_1_.rest_1_
  22.2 0.0 collective-permute-start.5
  22.2 0.0 collective-permute-done.1.refs_2_.rest_2_
  22.2 1.8 %collective-permute-done.2.refs_3_.rest_3_ = bf16[640,256]{1,0:T(8,128)(2,1)S(1)} collective-permute-done((bf16[640,256]{1,0:T(8,128)(2,1)}, bf16[640,256]{1,0:T(8,128)(2,1)S(1)}, u32[]{:S(2)}, u32[]{:S(2)}) %collective-permute-start.2) | collective-permute-done | bytes 327712 | tf_op jit(solution)/shard_map/ppermute | solution.py:495
  24.0 0.0 copy-done.11
  24.0 0.0 copy-start.10
  24.0 10.6 %all-to-all-done.query_all = bf16[8,320,128]{2,1,0:T(8,128)(2,1)S(1)} async-done(((bf16[8,320,128]{2,1,0:T(8,128)(2,1)}), bf16[8,320,128]{2,1,0:T(8,128)(2,1)S(1)}, u32[]{:S(2)}, u32[]{:S(2)}) %all-to-all-start) | async-done | bytes 655392 | tf_op jit(solution)/shard_map/all_to_all | solution.py:524
  34.7 7.0 %attend_cached.1 = (f32[2,320,512]{2,1,0:T(8,128)S(1)}, f32[2,16,512]{2,1,0:T(8,128)S(1)}) custom-call(bf16[8,320,128]{2,1,0:T(8,128)(2,1)S(1)} %all-to-all-done.query_all, f32[16,128]{1,0:T(8,128)S(1)} %arrive.1._, bf16[640,256]{1,0:T(8,128)(2,1)S(1)} %copy-done.11, bf16[640,256]{1,0:T(8,128)(2,1)S(1)} %collective-permute-done.refs_1_.rest_1_, ...), custom_call_target="tpu_custom_call" | custom-call | flops 1000000000 | tf_op jit(solution)/shard_map/attend_cached/pallas_call | solution.py:241
  41.7 0.0 collective-permute-done.3.rest_1_
  41.7 0.0 collective-permute-done.4.rest_2_
  41.7 0.0 collective-permute-done.5.rest_3_
  41.7 0.0 copy-done.10
  41.7 0.0 copy-start.6
  41.7 0.0 copy-start.1
  41.7 0.0 copy-start.2
  41.8 3.3 %attend_suffix.1 = (bf16[336,128]{1,0:T(8,128)(2,1)S(1)}, bf16[336,128]{1,0:T(8,128)(2,1)S(1)}, bf16[336,128]{1,0:T(8,128)(2,1)S(1)}, bf16[336,128]{1,0:T(8,128)...) custom-call(s32[1]{0:T(128)} %bitcast.place, ...), custom_call_target="tpu_custom_call" | custom-call | flops 20000000000 | bytes 8388608 | tf_op jit(solution)/shard_map/attend_suffix/pallas_call | solution.py:354
  45.1 0.0 copy-start
  45.1 0.0 copy-start.4
  45.1 0.0 copy-start.5
  45.1 1.7 %collective-permute-start.6 = (bf16[336,128]{1,0:T(8,128)(2,1)S(1)}, bf16[336,128]{1,0:T(8,128)(2,1)S(1)}, u32[]{:S(2)}, u32[]{:S(2)}) collective-permute-start(bf16[336,128]{1,0:T(8,128)(2,1)S(1)} %get-tuple-element.45), channel_id=1, source_target_pairs={{0,1},{1,0},{2,3},{3,2},{4,5},{5,4},{6,7},{7,6},{8,9},{9,8},{10,11... | collective-permute-start | bytes 258056 | tf_op jit(solution)/shard_map/ppermute | solution.py:495
  46.8 1.8 %collective-permute-start.7 = (bf16[336,128]{1,0:T(8,128)(2,1)S(1)}, bf16[336,128]{1,0:T(8,128)(2,1)S(1)}, u32[]{:S(2)}, u32[]{:S(2)}) collective-permute-start(bf16[336,128]{1,0:T(8,128)(2,1)S(1)} %get-tuple-element.46), channel_id=1, source_target_pairs={{0,4},{1,5},{2,6},{3,7},{4,0},{5,1},{6,2},{7,3},{8,12},{9,13},{10,... | collective-permute-start | bytes 258056 | tf_op jit(solution)/shard_map/ppermute | solution.py:495
  48.6 1.0 %collective-permute-start.8 = (bf16[336,128]{1,0:T(8,128)(2,1)S(1)}, bf16[336,128]{1,0:T(8,128)(2,1)S(1)}, u32[]{:S(2)}, u32[]{:S(2)}) collective-permute-start(bf16[336,128]{1,0:T(8,128)(2,1)S(1)} %get-tuple-element.47), channel_id=1, source_target_pairs={{0,5},{1,4},{2,7},{3,6},{4,1},{5,0},{6,3},{7,2},{8,13},{9,12},{10,... | collective-permute-start | bytes 258056 | tf_op jit(solution)/shard_map/ppermute | solution.py:495
  49.6 3.3 %collective-permute-start.9 = (bf16[336,128]{1,0:T(8,128)(2,1)S(1)}, bf16[336,128]{1,0:T(8,128)(2,1)S(1)}, u32[]{:S(2)}, u32[]{:S(2)}) collective-permute-start(bf16[336,128]{1,0:T(8,128)(2,1)S(1)} %get-tuple-element.48), channel_id=1, source_target_pairs={{0,6},{1,7},{2,4},{3,5},{4,2},{5,3},{6,0},{7,1},{8,14},{9,15},{10,... | collective-permute-start | bytes 258056 | tf_op jit(solution)/shard_map/ppermute | solution.py:495
  52.9 1.6 %collective-permute-start.10 = (bf16[336,128]{1,0:T(8,128)(2,1)S(1)}, bf16[336,128]{1,0:T(8,128)(2,1)S(1)}, u32[]{:S(2)}, u32[]{:S(2)}) collective-permute-start(bf16[336,128]{1,0:T(8,128)(2,1)S(1)} %get-tuple-element.49), channel_id=1, source_target_pairs={{0,7},{1,6},{2,5},{3,4},{4,3},{5,2},{6,1},{7,0},{8,15},{9,14},{10,... | collective-permute-start | bytes 258056 | tf_op jit(solution)/shard_map/ppermute | solution.py:495
  54.5 0.0 collective-permute-done.6.rest_0_
  54.5 1.4 %collective-permute-start.11 = (bf16[336,128]{1,0:T(8,128)(2,1)S(1)}, bf16[336,128]{1,0:T(8,128)(2,1)S(1)}, u32[]{:S(2)}, u32[]{:S(2)}) collective-permute-start(bf16[336,128]{1,0:T(8,128)(2,1)S(1)} %get-tuple-element.50), channel_id=1, source_target_pairs={{0,3},{1,2},{2,1},{3,0},{4,7},{5,6},{6,5},{7,4},{8,11},{9,10},{10,... | collective-permute-start | bytes 258056 | tf_op jit(solution)/shard_map/ppermute | solution.py:495
  56.0 1.0 %collective-permute-done.7.rest_1_ = bf16[336,128]{1,0:T(8,128)(2,1)S(1)} collective-permute-done((bf16[336,128]{1,0:T(8,128)(2,1)S(1)}, bf16[336,128]{1,0:T(8,128)(2,1)S(1)}, u32[]{:S(2)}, u32[]{:S(2)}) %collective-permute-start.7) | collective-permute-done | bytes 86048 | tf_op jit(solution)/shard_map/ppermute | solution.py:495
  56.9 0.0 collective-permute-start.12
  56.9 4.2 %collective-permute-done.8.rest_2_ = bf16[336,128]{1,0:T(8,128)(2,1)S(1)} collective-permute-done((bf16[336,128]{1,0:T(8,128)(2,1)S(1)}, bf16[336,128]{1,0:T(8,128)(2,1)S(1)}, u32[]{:S(2)}, u32[]{:S(2)}) %collective-permute-start.8) | collective-permute-done | bytes 86048 | tf_op jit(solution)/shard_map/ppermute | solution.py:495
  61.1 0.0 collective-permute-done.9.rest_3_
  61.1 0.0 collective-permute-done.10.rest_4_
  61.1 0.4 collective-permute-done.11.rest_5_
  61.5 0.3 collective-permute-done.12.rest_6_
  61.8 0.0 copy-done.6
  61.8 1.5 %project.1 = (f32[128,1280]{1,0:T(8,128)S(1)}, bf16[128,1280]{1,0:T(8,128)(2,1)S(1)}) custom-call(s32[1]{0:T(128)} %bitcast.place, bf16[128,1280]{1,0:T(8,128)(2,1)S(1)} %bitcast.7, f32[1280]{0:T(1024)S(1)} %copy-done.6, bf16[1280,1280]{1,0:T(8,128)(2,1)S(1)} %get-tuple-element.44.w_out, bf16[336,128]{1,0:T(8,128)(2,1)S(1)} %collective-permute-done.6.rest_0_, ...), custom_call_target="tpu_custom_call" | custom-call | flops 419430400 | bytes 3276800 | tf_op jit(solution)/shard_map/project/pallas_call | solution.py:410
  63.3 0.1 collective-permute-start.14
  63.4 1.6 %collective-permute-start.13 = (bf16[128,1280]{1,0:T(8,128)(2,1)S(1)}, bf16[128,1280]{1,0:T(8,128)(2,1)S(1)}, u32[]{:S(2)}, u32[]{:S(2)}) collective-permute-start(bf16[128,1280]{1,0:T(8,128)(2,1)S(1)} %get-tuple-element.54.first), channel_id=1, source_target_pairs={{0,16},{8,24},{16,0},{24,8},{1,17},{9,25},{17,1},{25,9},{2,18},{10... | collective-permute-start | bytes 983048 | tf_op jit(solution)/shard_map/ppermute | solution.py:495
  65.0 0.1 collective-permute-done.14.second
  65.0 0.0 copy-done.4
  65.0 0.0 copy-done.5
  65.1 3.0 %mlp.2 = (f32[128,1280]{1,0:T(8,128)S(1)}, bf16[128,1280]{1,0:T(8,128)(2,1)S(1)}) custom-call(bf16[128,1280]{1,0:T(8,128)(2,1)S(1)} %get-tuple-element.54.first, bf16[128,1280]{1,0:T(8,128)(2,1)S(1)} %collective-permute-done.14.second, bf16[1280,1280]{1,0:T(8,128)(2,1)S(1)} %copy-done, bf16[1280,1280]{1,0:T(8,128)(2,1)S(1)} %copy-done.1, ...), custom_call_target="tpu_custom_call" | custom-call | flops 2516582400 | bytes 9830400 | tf_op jit(solution)/shard_map/mlp/pallas_call | solution.py:441
  68.1 5.5 %collective-permute-done.13.first = bf16[128,1280]{1,0:T(8,128)(2,1)S(1)} collective-permute-done((bf16[128,1280]{1,0:T(8,128)(2,1)S(1)}, bf16[128,1280]{1,0:T(8,128)(2,1)S(1)}, u32[]{:S(2)}, u32[]{:S(2)}) %collective-permute-start.13) | collective-permute-done | bytes 327712 | tf_op jit(solution)/shard_map/ppermute | solution.py:495
  73.5 0.0 collective-permute-start.16
  73.5 1.6 %collective-permute-done.16.second = bf16[128,1280]{1,0:T(8,128)(2,1)S(1)} collective-permute-done((bf16[128,1280]{1,0:T(8,128)(2,1)S(1)}, bf16[128,1280]{1,0:T(8,128)(2,1)S(1)}, u32[]{:S(2)}, u32[]{:S(2)}) %collective-permute-start.16) | collective-permute-done | bytes 327712 | tf_op jit(solution)/shard_map/ppermute | solution.py:495
  75.2 3.0 %mlp.3 = (f32[128,1280]{1,0:T(8,128)S(1)}, bf16[128,1280]{1,0:T(8,128)(2,1)S(1)}) custom-call(bf16[128,1280]{1,0:T(8,128)(2,1)S(1)} %collective-permute-done.13.first, bf16[128,1280]{1,0:T(8,128)(2,1)S(1)} %collective-permute-done.16.second, bf16[1280,1280]{1,0:T(8,128)(2,1)S(1)} %copy-done, bf16[1280,1280]{1,0:T(8,128)(2,1)S(1)} %copy-done.1, ...), custom_call_target="tpu_custom_call" | custom-call | flops 2516582400 | bytes 9830400 | tf_op jit(solution)/shard_map/mlp/pallas_call | solution.py:441
  78.2 0.2 collective-permute-start.17
  78.4 0.4 collective-permute-start.15
  78.7 1.1 %collective-permute-done.17.arrived = bf16[128,1280]{1,0:T(8,128)(2,1)S(1)} collective-permute-done((bf16[128,1280]{1,0:T(8,128)(2,1)S(1)}, bf16[128,1280]{1,0:T(8,128)(2,1)S(1)}, u32[]{:S(2)}, u32[]{:S(2)}) %collective-permute-start.17) | collective-permute-done | bytes 327712 | tf_op jit(solution)/shard_map/ppermute | solution.py:495
  79.9 0.1 add_partials.1
  79.9 1.6 %collective-permute-start.18 = (bf16[128,1280]{1,0:T(8,128)(2,1)S(1)}, bf16[128,1280]{1,0:T(8,128)(2,1)S(1)}, u32[]{:S(2)}, u32[]{:S(2)}) collective-permute-start(bf16[128,1280]{1,0:T(8,128)(2,1)S(1)} %add_partials.1), channel_id=1, source_target_pairs={{0,16},{8,24},{16,0},{24,8},{1,17},{9,25},{17,1},{25,9},{2,18},{10... | collective-permute-start | bytes 983048 | tf_op jit(solution)/shard_map/ppermute | solution.py:495
  81.5 0.0 collective-permute-done.15.rest_0_
  81.5 8.3 %collective-permute-done.18.rest_1_ = bf16[128,1280]{1,0:T(8,128)(2,1)S(1)} collective-permute-done((bf16[128,1280]{1,0:T(8,128)(2,1)S(1)}, bf16[128,1280]{1,0:T(8,128)(2,1)S(1)}, u32[]{:S(2)}, u32[]{:S(2)}) %collective-permute-start.18) | collective-permute-done | bytes 327712 | tf_op jit(solution)/shard_map/ppermute | solution.py:495
  89.7 1.3 %finish.1 = bf16[128,1280]{1,0:T(8,128)(2,1)} custom-call(f32[128,1280]{1,0:T(8,128)S(1)} %get-tuple-element.53.hidden, f32[1280]{0:T(1024)S(1)} %copy-done.7, f32[128,1280]{1,0:T(8,128)S(1)} %get-tuple-element.56.kept, bf16[128,1280]{1,0:T(8,128)(2,1)S(1)} %collective-permute-done.15.rest_0_, bf16[128,1280]{1,0:T(8,128)(2,1)S(1)} %collective-permute-done.18.rest_1_), custom_call_target="tpu_custom_call" | custom-call | flops 1638400 | bytes 1966080 | tf_op jit(solution)/shard_map/finish/pallas_call | solution.py:481
  (10 shorter events, 0.0 us)
Async XLA Ops:
  0.0 7.5 %copy-start.3 = (bf16[1,128,1280]{2,1,0:T(8,128)(2,1)S(1)}, bf16[1,128,1280]{2,1,0:T(8,128)(2,1)}, u32[]{:S(2)}) copy-start(bf16[1,128,1280]{2,1,0:T(8,128)(2,1)} %param.14) | copy-start | bytes 983044
  0.0 7.5 %copy-start.9 = (f32[1280]{0:T(1024)S(1)}, f32[1280]{0:T(1024)}, u32[]{:S(2)}) copy-start(f32[1280]{0:T(1024)} %rest_0_.1) | copy-start | bytes 15364
  2.9 19.2 %collective-permute-start = (bf16[640,256]{1,0:T(8,128)(2,1)}, bf16[640,256]{1,0:T(8,128)(2,1)S(1)}, u32[]{:S(2)}, u32[]{:S(2)}) collective-permute-start(bf16[640,256]{1,0:T(8,128)(2,1)} %get-tuple-element.35), channel_id=1, source_target_pairs={{0,1},{1,0},{2,3},{3,2},{4,5},{5,4},{6,7},{7,6},{8,9},{9,8},{10,11... | collective-permute-start | bytes 983048 | tf_op jit(solution)/shard_map/ppermute | solution.py:495
  5.9 16.3 %collective-permute-start.1 = (bf16[640,256]{1,0:T(8,128)(2,1)}, bf16[640,256]{1,0:T(8,128)(2,1)S(1)}, u32[]{:S(2)}, u32[]{:S(2)}) collective-permute-start(bf16[640,256]{1,0:T(8,128)(2,1)} %get-tuple-element.36), channel_id=1, source_target_pairs={{0,2},{1,3},{2,0},{3,1},{4,6},{5,7},{6,4},{7,5},{8,10},{9,11},{10,... | collective-permute-start | bytes 983048 | tf_op jit(solution)/shard_map/ppermute | solution.py:495
  7.5 16.5 %collective-permute-start.2 = (bf16[640,256]{1,0:T(8,128)(2,1)}, bf16[640,256]{1,0:T(8,128)(2,1)S(1)}, u32[]{:S(2)}, u32[]{:S(2)}) collective-permute-start(bf16[640,256]{1,0:T(8,128)(2,1)} %get-tuple-element.37), channel_id=1, source_target_pairs={{0,3},{1,2},{2,1},{3,0},{4,7},{5,6},{6,5},{7,4},{8,11},{9,10},{10,... | collective-permute-start | bytes 983048 | tf_op jit(solution)/shard_map/ppermute | solution.py:495
  7.5 16.5 %copy-start.11 = (bf16[640,256]{1,0:T(8,128)(2,1)S(1)}, bf16[640,256]{1,0:T(8,128)(2,1)}, u32[]{:S(2)}) copy-start(bf16[640,256]{1,0:T(8,128)(2,1)} %get-tuple-element.34.refs_0_.rest_0_) | copy-start | bytes 983044
  12.5 22.2 %all-to-all-start = ((bf16[8,320,128]{2,1,0:T(8,128)(2,1)}), bf16[8,320,128]{2,1,0:T(8,128)(2,1)S(1)}, u32[]{:S(2)}, u32[]{:S(2)}) async-start(bf16[8,320,128]{2,1,0:T(8,128)(2,1)} %bitcast.2), calls=%async_computation | async-start | bytes 1310720 | tf_op jit(solution)/shard_map/all_to_all | solution.py:524
  18.7 23.0 %collective-permute-start.3 = (bf16[640,128]{1,0:T(8,128)(2,1)S(1)}, bf16[640,128]{1,0:T(8,128)(2,1)S(1)}, u32[]{:S(2)}, u32[]{:S(2)}) collective-permute-start(bf16[640,128]{1,0:T(8,128)(2,1)S(1)} %get-tuple-element.41), channel_id=1, source_target_pairs={{0,1},{1,0},{2,3},{3,2},{4,5},{5,4},{6,7},{7,6},{8,9},{9,8},{10,11... | collective-permute-start | bytes 491528 | tf_op jit(solution)/shard_map/ppermute | solution.py:495
  20.7 21.0 %collective-permute-start.4 = (bf16[640,128]{1,0:T(8,128)(2,1)S(1)}, bf16[640,128]{1,0:T(8,128)(2,1)S(1)}, u32[]{:S(2)}, u32[]{:S(2)}) collective-permute-start(bf16[640,128]{1,0:T(8,128)(2,1)S(1)} %get-tuple-element.42), channel_id=1, source_target_pairs={{0,2},{1,3},{2,0},{3,1},{4,6},{5,7},{6,4},{7,5},{8,10},{9,11},{10,... | collective-permute-start | bytes 491528 | tf_op jit(solution)/shard_map/ppermute | solution.py:495
  22.2 19.5 %collective-permute-start.5 = (bf16[640,128]{1,0:T(8,128)(2,1)S(1)}, bf16[640,128]{1,0:T(8,128)(2,1)S(1)}, u32[]{:S(2)}, u32[]{:S(2)}) collective-permute-start(bf16[640,128]{1,0:T(8,128)(2,1)S(1)} %get-tuple-element.43), channel_id=1, source_target_pairs={{0,3},{1,2},{2,1},{3,0},{4,7},{5,6},{6,5},{7,4},{8,11},{9,10},{10,... | collective-permute-start | bytes 491528 | tf_op jit(solution)/shard_map/ppermute | solution.py:495
  24.0 17.7 %copy-start.10 = (s32[1,16]{1,0:T(1,128)S(1)}, s32[1,16]{1,0:T(1,128)}, u32[]{:S(2)}) copy-start(s32[1,16]{1,0:T(1,128)} %lengths.1) | copy-start | bytes 196
  34.7 7.0 %copy-start.8 = (bf16[1280,1280]{1,0:T(8,128)(2,1)S(1)}, bf16[1280,1280]{1,0:T(8,128)(2,1)}, u32[]{:S(2)}) copy-start(bf16[1280,1280]{1,0:T(8,128)(2,1)} %rest_4_.1) | copy-start | bytes 9830404
  41.7 20.1 %copy-start.6 = (f32[1280]{0:T(1024)S(1)}, f32[1280]{0:T(1024)}, u32[]{:S(2)}) copy-start(f32[1280]{0:T(1024)} %rate_hbm.2) | copy-start | bytes 15364
  41.7 23.3 %copy-start.1 = (bf16[1280,1280]{1,0:T(8,128)(2,1)S(1)}, bf16[1280,1280]{1,0:T(8,128)(2,1)}, u32[]{:S(2)}) copy-start(bf16[1280,1280]{1,0:T(8,128)(2,1)} %w_gate.3) | copy-start | bytes 9830404
  41.7 23.3 %copy-start.2 = (bf16[1280,1280]{1,0:T(8,128)(2,1)S(1)}, bf16[1280,1280]{1,0:T(8,128)(2,1)}, u32[]{:S(2)}) copy-start(bf16[1280,1280]{1,0:T(8,128)(2,1)} %w_down.3) | copy-start | bytes 9830404
  45.1 19.9 %copy-start = (bf16[1280,1280]{1,0:T(8,128)(2,1)S(1)}, bf16[1280,1280]{1,0:T(8,128)(2,1)}, u32[]{:S(2)}) copy-start(bf16[1280,1280]{1,0:T(8,128)(2,1)} %w_up.3) | copy-start | bytes 9830404
  45.1 19.9 %copy-start.4 = (f32[1280]{0:T(1024)S(1)}, f32[1280]{0:T(1024)}, u32[]{:S(2)}) copy-start(f32[1280]{0:T(1024)} %up_scale.3) | copy-start | bytes 15364
  45.1 19.9 %copy-start.5 = (f32[1280]{0:T(1024)S(1)}, f32[1280]{0:T(1024)}, u32[]{:S(2)}) copy-start(f32[1280]{0:T(1024)} %gate_scale.3) | copy-start | bytes 15364
  45.1 9.4 %collective-permute-start.6 = (bf16[336,128]{1,0:T(8,128)(2,1)S(1)}, bf16[336,128]{1,0:T(8,128)(2,1)S(1)}, u32[]{:S(2)}, u32[]{:S(2)}) collective-permute-start(bf16[336,128]{1,0:T(8,128)(2,1)S(1)} %get-tuple-element.45), channel_id=1, source_target_pairs={{0,1},{1,0},{2,3},{3,2},{4,5},{5,4},{6,7},{7,6},{8,9},{9,8},{10,11... | collective-permute-start | bytes 258056 | tf_op jit(solution)/shard_map/ppermute | solution.py:495
  46.8 10.1 %collective-permute-start.7 = (bf16[336,128]{1,0:T(8,128)(2,1)S(1)}, bf16[336,128]{1,0:T(8,128)(2,1)S(1)}, u32[]{:S(2)}, u32[]{:S(2)}) collective-permute-start(bf16[336,128]{1,0:T(8,128)(2,1)S(1)} %get-tuple-element.46), channel_id=1, source_target_pairs={{0,4},{1,5},{2,6},{3,7},{4,0},{5,1},{6,2},{7,3},{8,12},{9,13},{10,... | collective-permute-start | bytes 258056 | tf_op jit(solution)/shard_map/ppermute | solution.py:495
  48.6 12.5 %collective-permute-start.8 = (bf16[336,128]{1,0:T(8,128)(2,1)S(1)}, bf16[336,128]{1,0:T(8,128)(2,1)S(1)}, u32[]{:S(2)}, u32[]{:S(2)}) collective-permute-start(bf16[336,128]{1,0:T(8,128)(2,1)S(1)} %get-tuple-element.47), channel_id=1, source_target_pairs={{0,5},{1,4},{2,7},{3,6},{4,1},{5,0},{6,3},{7,2},{8,13},{9,12},{10,... | collective-permute-start | bytes 258056 | tf_op jit(solution)/shard_map/ppermute | solution.py:495
  49.6 11.5 %collective-permute-start.9 = (bf16[336,128]{1,0:T(8,128)(2,1)S(1)}, bf16[336,128]{1,0:T(8,128)(2,1)S(1)}, u32[]{:S(2)}, u32[]{:S(2)}) collective-permute-start(bf16[336,128]{1,0:T(8,128)(2,1)S(1)} %get-tuple-element.48), channel_id=1, source_target_pairs={{0,6},{1,7},{2,4},{3,5},{4,2},{5,3},{6,0},{7,1},{8,14},{9,15},{10,... | collective-permute-start | bytes 258056 | tf_op jit(solution)/shard_map/ppermute | solution.py:495
  52.9 8.2 %collective-permute-start.10 = (bf16[336,128]{1,0:T(8,128)(2,1)S(1)}, bf16[336,128]{1,0:T(8,128)(2,1)S(1)}, u32[]{:S(2)}, u32[]{:S(2)}) collective-permute-start(bf16[336,128]{1,0:T(8,128)(2,1)S(1)} %get-tuple-element.49), channel_id=1, source_target_pairs={{0,7},{1,6},{2,5},{3,4},{4,3},{5,2},{6,1},{7,0},{8,15},{9,14},{10,... | collective-permute-start | bytes 258056 | tf_op jit(solution)/shard_map/ppermute | solution.py:495
  54.5 7.0 %collective-permute-start.11 = (bf16[336,128]{1,0:T(8,128)(2,1)S(1)}, bf16[336,128]{1,0:T(8,128)(2,1)S(1)}, u32[]{:S(2)}, u32[]{:S(2)}) collective-permute-start(bf16[336,128]{1,0:T(8,128)(2,1)S(1)} %get-tuple-element.50), channel_id=1, source_target_pairs={{0,3},{1,2},{2,1},{3,0},{4,7},{5,6},{6,5},{7,4},{8,11},{9,10},{10,... | collective-permute-start | bytes 258056 | tf_op jit(solution)/shard_map/ppermute | solution.py:495
  56.9 4.9 %collective-permute-start.12 = (bf16[336,128]{1,0:T(8,128)(2,1)S(1)}, bf16[336,128]{1,0:T(8,128)(2,1)S(1)}, u32[]{:S(2)}, u32[]{:S(2)}) collective-permute-start(bf16[336,128]{1,0:T(8,128)(2,1)S(1)} %get-tuple-element.51), channel_id=1, source_target_pairs={{0,2},{1,3},{2,0},{3,1},{4,6},{5,7},{6,4},{7,5},{8,10},{9,11},{10,... | collective-permute-start | bytes 258056 | tf_op jit(solution)/shard_map/ppermute | solution.py:495
  63.3 1.7 %collective-permute-start.14 = (bf16[128,1280]{1,0:T(8,128)(2,1)S(1)}, bf16[128,1280]{1,0:T(8,128)(2,1)S(1)}, u32[]{:S(2)}, u32[]{:S(2)}) collective-permute-start(bf16[128,1280]{1,0:T(8,128)(2,1)S(1)} %get-tuple-element.54.first), channel_id=1, source_target_pairs={{0,8},{8,0},{16,24},{24,16},{1,9},{9,1},{17,25},{25,17},{2,10},{10... | collective-permute-start | bytes 983048 | tf_op jit(solution)/shard_map/ppermute | solution.py:495
  63.4 10.1 %collective-permute-start.13 = (bf16[128,1280]{1,0:T(8,128)(2,1)S(1)}, bf16[128,1280]{1,0:T(8,128)(2,1)S(1)}, u32[]{:S(2)}, u32[]{:S(2)}) collective-permute-start(bf16[128,1280]{1,0:T(8,128)(2,1)S(1)} %get-tuple-element.54.first), channel_id=1, source_target_pairs={{0,16},{8,24},{16,0},{24,8},{1,17},{9,25},{17,1},{25,9},{2,18},{10... | collective-permute-start | bytes 983048 | tf_op jit(solution)/shard_map/ppermute | solution.py:495
  73.5 16.2 %copy-start.7 = (f32[1280]{0:T(1024)S(1)}, f32[1280]{0:T(1024)}, u32[]{:S(2)}) copy-start(f32[1280]{0:T(1024)} %rate_hbm.3) | copy-start | bytes 15364
  73.5 1.6 %collective-permute-start.16 = (bf16[128,1280]{1,0:T(8,128)(2,1)S(1)}, bf16[128,1280]{1,0:T(8,128)(2,1)S(1)}, u32[]{:S(2)}, u32[]{:S(2)}) collective-permute-start(bf16[128,1280]{1,0:T(8,128)(2,1)S(1)} %collective-permute-done.13.first), channel_id=1, source_target_pairs={{0,8},{8,0},{16,24},{24,16},{1,9},{9,1},{17,25},{25,17},{2,10},{10... | collective-permute-start | bytes 983048 | tf_op jit(solution)/shard_map/ppermute | solution.py:495
  78.2 1.7 %collective-permute-start.17 = (bf16[128,1280]{1,0:T(8,128)(2,1)S(1)}, bf16[128,1280]{1,0:T(8,128)(2,1)S(1)}, u32[]{:S(2)}, u32[]{:S(2)}) collective-permute-start(bf16[128,1280]{1,0:T(8,128)(2,1)S(1)} %get-tuple-element.60), channel_id=1, source_target_pairs={{0,8},{8,0},{16,24},{24,16},{1,9},{9,1},{17,25},{25,17},{2,10},{10... | collective-permute-start | bytes 983048 | tf_op jit(solution)/shard_map/ppermute | solution.py:495
  78.4 3.1 %collective-permute-start.15 = (bf16[128,1280]{1,0:T(8,128)(2,1)S(1)}, bf16[128,1280]{1,0:T(8,128)(2,1)S(1)}, u32[]{:S(2)}, u32[]{:S(2)}) collective-permute-start(bf16[128,1280]{1,0:T(8,128)(2,1)S(1)} %get-tuple-element.57), channel_id=1, source_target_pairs={{0,8},{8,0},{16,24},{24,16},{1,9},{9,1},{17,25},{25,17},{2,10},{10... | collective-permute-start | bytes 983048 | tf_op jit(solution)/shard_map/ppermute | solution.py:495
  79.9 9.8 %collective-permute-start.18 = (bf16[128,1280]{1,0:T(8,128)(2,1)S(1)}, bf16[128,1280]{1,0:T(8,128)(2,1)S(1)}, u32[]{:S(2)}, u32[]{:S(2)}) collective-permute-start(bf16[128,1280]{1,0:T(8,128)(2,1)S(1)} %add_partials.1), channel_id=1, source_target_pairs={{0,16},{8,24},{16,0},{24,8},{1,17},{9,25},{17,1},{25,9},{2,18},{10... | collective-permute-start | bytes 983048 | tf_op jit(solution)/shard_map/ppermute | solution.py:495

commit v6 on v5

--- a/solution.py
+++ b/solution.py
@@ -89,20 +89,29 @@
 
 
 def prefix_kernel(place, *rest):
-    sources, outs, (parts, scale, keys, values, sems) = rest[:3], rest[3 : 3 + SQ], rest[3 + SQ :]
+    sources, outs, rest = rest[:3], rest[3 : 3 + SQ], rest[3 + SQ :]
+    *parts, scale, keys, values, sems, out_sems = rest
+    i = lax.rem(place[0], SQ)
+
+    def leave(half):
+        return fetch(
+            [parts[half].at[jnp.bitwise_xor(i, m)] for m in range(SQ)],
+            [out.at[pl.ds(half * QD, QD), :] for out in outs],
+            out_sems.at[half],
+        )
+
     copies = fetch(sources, (scale, keys, values), sems)
     rows = keys.shape[0]
     wait(copies[:2])
     for c in range(D // 128):
         cols = slice(c * 128, (c + 1) * 128)
         scale_t = jnp.concatenate([column(scale, c)] * (rows // 128), axis=1)
-        split(parts, 0, c, head_unit_t(keys[:, cols].T.astype(f32), scale_t).astype(bf16))
+        split(parts[0], 0, c, head_unit_t(keys[:, cols].T.astype(f32), scale_t).astype(bf16))
+    left = leave(0)
     wait(copies[2:])
     for c in range(D // 128):
-        split(parts, QD, c, values[:, c * 128 : (c + 1) * 128].T)
-    i = lax.rem(place[0], SQ)
-    for m in range(SQ):
-        outs[m][...] = parts[jnp.bitwise_xor(i, m)]
+        split(parts[1], 0, c, values[:, c * 128 : (c + 1) * 128].T)
+    wait(left + leave(1))
 
 
 def split(out, base, c, block):
@@ -118,8 +127,10 @@
         prefix_kernel,
         out_shape=[jax.ShapeDtypeStruct((2 * QD, rows), bf16)] * SQ,
         in_specs=[smem()] + [hbm()] * 3,
-        out_specs=[vmem()] * SQ,
-        scratch_shapes=[pltpu.VMEM((SQ, 2 * QD, rows), bf16)] + fetched(scale, keys, values),
+        out_specs=[hbm()] * SQ,
+        scratch_shapes=[pltpu.VMEM((SQ, QD, rows), bf16)] * 2
+        + fetched(scale, keys, values)
+        + [pltpu.SemaphoreType.DMA((2, SQ))],
         compiler_params=params(PREFIX_LIMIT),
         cost_estimate=cost(5e10, 4 * rows * D * 2),
         name="prefix_prep",
@@ -297,7 +308,8 @@
             key_at = (square * SQ + block) * rows + lax.broadcasted_iota(
                 jnp.int32, (rows, lanes.stop - lanes.start), 0
             )
-            masks.append((key_at >= first[:, lanes]) & (key_at <= position[:, lanes]))
+            allowed = (key_at >= first[:, lanes]) & (key_at <= position[:, lanes])
+            masks.append(jnp.where(allowed, 0.0, NEG))
         scores = []
         for h in range(HQ):
             head = slice(h * HEAD, (h + 1) * HEAD)
@@ -308,7 +320,7 @@
                     jnp.concatenate(query[begin:end], axis=1),
                     preferred_element_type=f32,
                 )
-                scores.append(jnp.where(mask, score, NEG))
+                scores.append(score + mask)
         states = []
         for h in range(HQ):
             cached_top = stats[query_square, h : h + 1, :]

time: 91.4 us -> 91.1 us (level)
  transfers between devices with their start and end apart: 20 -> 20, of which waited for: 11 -> 10; matrix products, arithmetic and copies ran while one was open for 0% -> 0% of each run, Pallas kernels for 16% -> 16%
where the time goes in v6:
time: 91.1 us; the launch traced here: 90.8 us
  waiting for transfers between devices  34.8 us (38%)
  starting transfers between devices  29 us (32%)
  Pallas kernels  26.6 us (29%)
    ppermute x19, waiting for transfers between devices, swap(): return lax.ppermute(shard, axis, [(j, j ^ mask) for j in range(length)])  24.2 us
    ppermute x19, starting transfers between devices, swap(): return lax.ppermute(shard, axis, [(j, j ^ mask) for j in range(length)])  22.8 us
    all_to_all x1, waiting for transfers between devices, body(): queries = lax.all_to_all(queries.reshape(extent, QD, rows), 'tok', 0, 0)  10.6 us
    pallas_call x1, Pallas kernels, cached_call(): pl.pallas_call(cached_kernel, out_shape=[jax.ShapeDtypeStruct((extent //...  6.98 us
    all_to_all x1, starting transfers between devices, body(): queries = lax.all_to_all(queries.reshape(extent, QD, rows), 'tok', 0, 0)  6.21 us
    pallas_call x2, Pallas kernels, mlp_call(): pl.pallas_call(mlp_kernel, out_shape=[jax.ShapeDtypeStruct((rows, D), f32...  5.97 us
    pallas_call x1, Pallas kernels, qkv_call(): pl.pallas_call(functools.partial(qkv_kernel, squares), out_shape=[jax.Sha...  4.92 us
    pallas_call x1, Pallas kernels, suffix_call(): pl.pallas_call(functools.partial(suffix_kernel, extent), out_shape=[jax.S...  3.18 us
  transfers between devices with their start and end apart: 20, of which 10 were waited for; matrix products, arithmetic and copies ran while one was open for 0% of the time, Pallas kernels for 16%

profile of v6, /device:TPU:0, one launch (start us, length us, event | category | flops | bytes accessed | tf_op | source)
XLA Modules:
  0.0 90.8 jit_solution(16963848376457956426)
XLA Ops:
  0.0 2.7 %prefix_prep.1 = (bf16[640,256]{1,0:T(8,128)(2,1)}, bf16[640,256]{1,0:T(8,128)(2,1)}, bf16[640,256]{1,0:T(8,128)(2,1)}, bf16[640,256]{1,0:T(8,128)(2,1)}) custom-call(s32[1]{0:T(128)} %bitcast.place, f32[1280]{0:T(1024)} %rest_0_.1, bf16[256,1280]{1,0:T(8,128)(2,1)} %bitcast.8, bf16[256,1280]{1,0:T(8,128)(2,1)} %bitcast.9), custom_call_target="tpu_custom_call" | custom-call | flops 49999998976 | bytes 2621440 | tf_op jit(solution)/shard_map/prefix_prep/pallas_call | solution.py:126
  2.7 3.0 %collective-permute-start = (bf16[640,256]{1,0:T(8,128)(2,1)}, bf16[640,256]{1,0:T(8,128)(2,1)S(1)}, u32[]{:S(2)}, u32[]{:S(2)}) collective-permute-start(bf16[640,256]{1,0:T(8,128)(2,1)} %get-tuple-element.35), channel_id=1, source_target_pairs={{0,1},{1,0},{2,3},{3,2},{4,5},{5,4},{6,7},{7,6},{8,9},{9,8},{10,11... | collective-permute-start | bytes 983048 | tf_op jit(solution)/shard_map/ppermute | solution.py:507
  5.8 1.6 %collective-permute-start.1 = (bf16[640,256]{1,0:T(8,128)(2,1)}, bf16[640,256]{1,0:T(8,128)(2,1)S(1)}, u32[]{:S(2)}, u32[]{:S(2)}) collective-permute-start(bf16[640,256]{1,0:T(8,128)(2,1)} %get-tuple-element.36), channel_id=1, source_target_pairs={{0,2},{1,3},{2,0},{3,1},{4,6},{5,7},{6,4},{7,5},{8,10},{9,11},{10,... | collective-permute-start | bytes 983048 | tf_op jit(solution)/shard_map/ppermute | solution.py:507
  7.3 0.0 collective-permute-start.2
  7.3 0.0 copy-done.3
  7.3 0.0 copy-done.9
  7.3 0.0 copy-start.11
  7.4 4.9 %qkv.1 = (bf16[2560,128]{1,0:T(8,128)(2,1)}, bf16[640,128]{1,0:T(8,128)(2,1)S(1)}, bf16[640,128]{1,0:T(8,128)(2,1)S(1)}, bf16[640,128]{1,0:T(8,128)(2,1)S(1)}, bf16[640,128]{1,0:T(8,128)(2,1)S(1)}) custom-call(s32[1]{0:T(128)} %bitcast.place, bf16[128,1280]{1,0:T(8,128)(2,1)S(1)} %bitcast.6, f32[1280]{0:T(1024)S(1)} %copy-done.9, bf16[1280,3840]{1,0:T(8,128)(2,1)} %w_hbm.1), custom_call_target="tpu_custom_call" | custom-call | flops 49999998976 | bytes 9830400 | tf_op jit(solution)/shard_map/qkv/pallas_call | solution.py:170
  12.3 6.2 %all-to-all-start = ((bf16[8,320,128]{2,1,0:T(8,128)(2,1)}), bf16[8,320,128]{2,1,0:T(8,128)(2,1)S(1)}, u32[]{:S(2)}, u32[]{:S(2)}) async-start(bf16[8,320,128]{2,1,0:T(8,128)(2,1)} %bitcast.2), calls=%async_computation | async-start | bytes 1310720 | tf_op jit(solution)/shard_map/all_to_all | solution.py:536
  18.5 2.0 %collective-permute-start.3 = (bf16[640,128]{1,0:T(8,128)(2,1)S(1)}, bf16[640,128]{1,0:T(8,128)(2,1)S(1)}, u32[]{:S(2)}, u32[]{:S(2)}) collective-permute-start(bf16[640,128]{1,0:T(8,128)(2,1)S(1)} %get-tuple-element.41), channel_id=1, source_target_pairs={{0,1},{1,0},{2,3},{3,2},{4,5},{5,4},{6,7},{7,6},{8,9},{9,8},{10,11... | collective-permute-start | bytes 491528 | tf_op jit(solution)/shard_map/ppermute | solution.py:507
  20.5 1.5 %collective-permute-start.4 = (bf16[640,128]{1,0:T(8,128)(2,1)S(1)}, bf16[640,128]{1,0:T(8,128)(2,1)S(1)}, u32[]{:S(2)}, u32[]{:S(2)}) collective-permute-start(bf16[640,128]{1,0:T(8,128)(2,1)S(1)} %get-tuple-element.42), channel_id=1, source_target_pairs={{0,2},{1,3},{2,0},{3,1},{4,6},{5,7},{6,4},{7,5},{8,10},{9,11},{10,... | collective-permute-start | bytes 491528 | tf_op jit(solution)/shard_map/ppermute | solution.py:507
  22.0 0.0 collective-permute-done.refs_1_.rest_1_
  22.0 0.0 collective-permute-start.5
  22.0 0.0 collective-permute-done.1.refs_2_.rest_2_
  22.0 1.8 %collective-permute-done.2.refs_3_.rest_3_ = bf16[640,256]{1,0:T(8,128)(2,1)S(1)} collective-permute-done((bf16[640,256]{1,0:T(8,128)(2,1)}, bf16[640,256]{1,0:T(8,128)(2,1)S(1)}, u32[]{:S(2)}, u32[]{:S(2)}) %collective-permute-start.2) | collective-permute-done | bytes 327712 | tf_op jit(solution)/shard_map/ppermute | solution.py:507
  23.8 0.0 copy-done.11
  23.9 0.0 copy-start.10
  23.9 10.6 %all-to-all-done.query_all = bf16[8,320,128]{2,1,0:T(8,128)(2,1)S(1)} async-done(((bf16[8,320,128]{2,1,0:T(8,128)(2,1)}), bf16[8,320,128]{2,1,0:T(8,128)(2,1)S(1)}, u32[]{:S(2)}, u32[]{:S(2)}) %all-to-all-start) | async-done | bytes 655392 | tf_op jit(solution)/shard_map/all_to_all | solution.py:536
  34.5 7.0 %attend_cached.1 = (f32[2,320,512]{2,1,0:T(8,128)S(1)}, f32[2,16,512]{2,1,0:T(8,128)S(1)}) custom-call(bf16[8,320,128]{2,1,0:T(8,128)(2,1)S(1)} %all-to-all-done.query_all, f32[16,128]{1,0:T(8,128)S(1)} %arrive.1._, bf16[640,256]{1,0:T(8,128)(2,1)S(1)} %copy-done.11, bf16[640,256]{1,0:T(8,128)(2,1)S(1)} %collective-permute-done.refs_1_.rest_1_, ...), custom_call_target="tpu_custom_call" | custom-call | flops 1000000000 | tf_op jit(solution)/shard_map/attend_cached/pallas_call | solution.py:252
  41.5 0.0 collective-permute-done.3.rest_1_
  41.5 0.0 collective-permute-done.4.rest_2_
  41.5 0.0 collective-permute-done.5.rest_3_
  41.5 0.0 copy-done.10
  41.5 0.0 copy-done.8
  41.5 0.0 copy-start.6
  41.6 0.0 copy-start.1
  41.6 0.0 copy-start.2
  41.6 3.2 %attend_suffix.1 = (bf16[336,128]{1,0:T(8,128)(2,1)S(1)}, bf16[336,128]{1,0:T(8,128)(2,1)S(1)}, bf16[336,128]{1,0:T(8,128)(2,1)S(1)}, bf16[336,128]{1,0:T(8,128)...) custom-call(s32[1]{0:T(128)} %bitcast.place, ...), custom_call_target="tpu_custom_call" | custom-call | flops 20000000000 | bytes 8388608 | tf_op jit(solution)/shard_map/attend_suffix/pallas_call | solution.py:366
  44.8 0.0 copy-start
  44.8 0.0 copy-start.4
  44.8 0.0 copy-start.5
  44.8 1.7 %collective-permute-start.6 = (bf16[336,128]{1,0:T(8,128)(2,1)S(1)}, bf16[336,128]{1,0:T(8,128)(2,1)S(1)}, u32[]{:S(2)}, u32[]{:S(2)}) collective-permute-start(bf16[336,128]{1,0:T(8,128)(2,1)S(1)} %get-tuple-element.45), channel_id=1, source_target_pairs={{0,1},{1,0},{2,3},{3,2},{4,5},{5,4},{6,7},{7,6},{8,9},{9,8},{10,11... | collective-permute-start | bytes 258056 | tf_op jit(solution)/shard_map/ppermute | solution.py:507
  46.5 1.8 %collective-permute-start.7 = (bf16[336,128]{1,0:T(8,128)(2,1)S(1)}, bf16[336,128]{1,0:T(8,128)(2,1)S(1)}, u32[]{:S(2)}, u32[]{:S(2)}) collective-permute-start(bf16[336,128]{1,0:T(8,128)(2,1)S(1)} %get-tuple-element.46), channel_id=1, source_target_pairs={{0,4},{1,5},{2,6},{3,7},{4,0},{5,1},{6,2},{7,3},{8,12},{9,13},{10,... | collective-permute-start | bytes 258056 | tf_op jit(solution)/shard_map/ppermute | solution.py:507
  48.3 1.0 %collective-permute-start.8 = (bf16[336,128]{1,0:T(8,128)(2,1)S(1)}, bf16[336,128]{1,0:T(8,128)(2,1)S(1)}, u32[]{:S(2)}, u32[]{:S(2)}) collective-permute-start(bf16[336,128]{1,0:T(8,128)(2,1)S(1)} %get-tuple-element.47), channel_id=1, source_target_pairs={{0,5},{1,4},{2,7},{3,6},{4,1},{5,0},{6,3},{7,2},{8,13},{9,12},{10,... | collective-permute-start | bytes 258056 | tf_op jit(solution)/shard_map/ppermute | solution.py:507
  49.3 3.3 %collective-permute-start.9 = (bf16[336,128]{1,0:T(8,128)(2,1)S(1)}, bf16[336,128]{1,0:T(8,128)(2,1)S(1)}, u32[]{:S(2)}, u32[]{:S(2)}) collective-permute-start(bf16[336,128]{1,0:T(8,128)(2,1)S(1)} %get-tuple-element.48), channel_id=1, source_target_pairs={{0,6},{1,7},{2,4},{3,5},{4,2},{5,3},{6,0},{7,1},{8,14},{9,15},{10,... | collective-permute-start | bytes 258056 | tf_op jit(solution)/shard_map/ppermute | solution.py:507
  52.5 1.6 %collective-permute-start.10 = (bf16[336,128]{1,0:T(8,128)(2,1)S(1)}, bf16[336,128]{1,0:T(8,128)(2,1)S(1)}, u32[]{:S(2)}, u32[]{:S(2)}) collective-permute-start(bf16[336,128]{1,0:T(8,128)(2,1)S(1)} %get-tuple-element.49), channel_id=1, source_target_pairs={{0,7},{1,6},{2,5},{3,4},{4,3},{5,2},{6,1},{7,0},{8,15},{9,14},{10,... | collective-permute-start | bytes 258056 | tf_op jit(solution)/shard_map/ppermute | solution.py:507
  54.1 0.0 collective-permute-done.6.rest_0_
  54.1 1.5 %collective-permute-start.11 = (bf16[336,128]{1,0:T(8,128)(2,1)S(1)}, bf16[336,128]{1,0:T(8,128)(2,1)S(1)}, u32[]{:S(2)}, u32[]{:S(2)}) collective-permute-start(bf16[336,128]{1,0:T(8,128)(2,1)S(1)} %get-tuple-element.50), channel_id=1, source_target_pairs={{0,3},{1,2},{2,1},{3,0},{4,7},{5,6},{6,5},{7,4},{8,11},{9,10},{10,... | collective-permute-start | bytes 258056 | tf_op jit(solution)/shard_map/ppermute | solution.py:507
  55.7 1.0 %collective-permute-done.7.rest_1_ = bf16[336,128]{1,0:T(8,128)(2,1)S(1)} collective-permute-done((bf16[336,128]{1,0:T(8,128)(2,1)S(1)}, bf16[336,128]{1,0:T(8,128)(2,1)S(1)}, u32[]{:S(2)}, u32[]{:S(2)}) %collective-permute-start.7) | collective-permute-done | bytes 86048 | tf_op jit(solution)/shard_map/ppermute | solution.py:507
  56.6 0.0 collective-permute-start.12
  56.6 4.1 %collective-permute-done.8.rest_2_ = bf16[336,128]{1,0:T(8,128)(2,1)S(1)} collective-permute-done((bf16[336,128]{1,0:T(8,128)(2,1)S(1)}, bf16[336,128]{1,0:T(8,128)(2,1)S(1)}, u32[]{:S(2)}, u32[]{:S(2)}) %collective-permute-start.8) | collective-permute-done | bytes 86048 | tf_op jit(solution)/shard_map/ppermute | solution.py:507
  60.7 0.0 collective-permute-done.9.rest_3_
  60.7 0.0 collective-permute-done.10.rest_4_
  60.7 0.4 collective-permute-done.11.rest_5_
  61.2 0.3 collective-permute-done.12.rest_6_
  61.5 0.0 copy-done.6
  61.5 1.5 %project.1 = (f32[128,1280]{1,0:T(8,128)S(1)}, bf16[128,1280]{1,0:T(8,128)(2,1)S(1)}) custom-call(s32[1]{0:T(128)} %bitcast.place, bf16[128,1280]{1,0:T(8,128)(2,1)S(1)} %bitcast.7, f32[1280]{0:T(1024)S(1)} %copy-done.6, bf16[1280,1280]{1,0:T(8,128)(2,1)S(1)} %get-tuple-element.44.w_out, bf16[336,128]{1,0:T(8,128)(2,1)S(1)} %collective-permute-done.6.rest_0_, ...), custom_call_target="tpu_custom_call" | custom-call | flops 419430400 | bytes 3276800 | tf_op jit(solution)/shard_map/project/pallas_call | solution.py:422
  63.0 0.1 collective-permute-start.14
  63.1 1.6 %collective-permute-start.13 = (bf16[128,1280]{1,0:T(8,128)(2,1)S(1)}, bf16[128,1280]{1,0:T(8,128)(2,1)S(1)}, u32[]{:S(2)}, u32[]{:S(2)}) collective-permute-start(bf16[128,1280]{1,0:T(8,128)(2,1)S(1)} %get-tuple-element.54.first), channel_id=1, source_target_pairs={{0,16},{8,24},{16,0},{24,8},{1,17},{9,25},{17,1},{25,9},{2,18},{10... | collective-permute-start | bytes 983048 | tf_op jit(solution)/shard_map/ppermute | solution.py:507
  64.7 0.0 collective-permute-done.14.second
  64.7 0.0 copy-done.1
  64.7 3.0 %mlp.2 = (f32[128,1280]{1,0:T(8,128)S(1)}, bf16[128,1280]{1,0:T(8,128)(2,1)S(1)}) custom-call(bf16[128,1280]{1,0:T(8,128)(2,1)S(1)} %get-tuple-element.54.first, bf16[128,1280]{1,0:T(8,128)(2,1)S(1)} %collective-permute-done.14.second, bf16[1280,1280]{1,0:T(8,128)(2,1)S(1)} %copy-done, bf16[1280,1280]{1,0:T(8,128)(2,1)S(1)} %copy-done.1, ...), custom_call_target="tpu_custom_call" | custom-call | flops 2516582400 | bytes 9830400 | tf_op jit(solution)/shard_map/mlp/pallas_call | solution.py:453
  67.7 5.5 %collective-permute-done.13.first = bf16[128,1280]{1,0:T(8,128)(2,1)S(1)} collective-permute-done((bf16[128,1280]{1,0:T(8,128)(2,1)S(1)}, bf16[128,1280]{1,0:T(8,128)(2,1)S(1)}, u32[]{:S(2)}, u32[]{:S(2)}) %collective-permute-start.13) | collective-permute-done | bytes 327712 | tf_op jit(solution)/shard_map/ppermute | solution.py:507
  73.2 0.0 collective-permute-start.16
  73.2 1.6 %collective-permute-done.16.second = bf16[128,1280]{1,0:T(8,128)(2,1)S(1)} collective-permute-done((bf16[128,1280]{1,0:T(8,128)(2,1)S(1)}, bf16[128,1280]{1,0:T(8,128)(2,1)S(1)}, u32[]{:S(2)}, u32[]{:S(2)}) %collective-permute-start.16) | collective-permute-done | bytes 327712 | tf_op jit(solution)/shard_map/ppermute | solution.py:507
  74.8 3.0 %mlp.3 = (f32[128,1280]{1,0:T(8,128)S(1)}, bf16[128,1280]{1,0:T(8,128)(2,1)S(1)}) custom-call(bf16[128,1280]{1,0:T(8,128)(2,1)S(1)} %collective-permute-done.13.first, bf16[128,1280]{1,0:T(8,128)(2,1)S(1)} %collective-permute-done.16.second, bf16[1280,1280]{1,0:T(8,128)(2,1)S(1)} %copy-done, bf16[1280,1280]{1,0:T(8,128)(2,1)S(1)} %copy-done.1, ...), custom_call_target="tpu_custom_call" | custom-call | flops 2516582400 | bytes 9830400 | tf_op jit(solution)/shard_map/mlp/pallas_call | solution.py:453
  77.8 0.2 collective-permute-start.17
  78.0 0.4 collective-permute-start.15
  78.4 1.1 %collective-permute-done.17.arrived = bf16[128,1280]{1,0:T(8,128)(2,1)S(1)} collective-permute-done((bf16[128,1280]{1,0:T(8,128)(2,1)S(1)}, bf16[128,1280]{1,0:T(8,128)(2,1)S(1)}, u32[]{:S(2)}, u32[]{:S(2)}) %collective-permute-start.17) | collective-permute-done | bytes 327712 | tf_op jit(solution)/shard_map/ppermute | solution.py:507
  79.5 0.1 add_partials.1
  79.6 1.6 %collective-permute-start.18 = (bf16[128,1280]{1,0:T(8,128)(2,1)S(1)}, bf16[128,1280]{1,0:T(8,128)(2,1)S(1)}, u32[]{:S(2)}, u32[]{:S(2)}) collective-permute-start(bf16[128,1280]{1,0:T(8,128)(2,1)S(1)} %add_partials.1), channel_id=1, source_target_pairs={{0,16},{8,24},{16,0},{24,8},{1,17},{9,25},{17,1},{25,9},{2,18},{10... | collective-permute-start | bytes 983048 | tf_op jit(solution)/shard_map/ppermute | solution.py:507
  81.2 0.0 collective-permute-done.15.rest_0_
  81.2 8.2 %collective-permute-done.18.rest_1_ = bf16[128,1280]{1,0:T(8,128)(2,1)S(1)} collective-permute-done((bf16[128,1280]{1,0:T(8,128)(2,1)S(1)}, bf16[128,1280]{1,0:T(8,128)(2,1)S(1)}, u32[]{:S(2)}, u32[]{:S(2)}) %collective-permute-start.18) | collective-permute-done | bytes 327712 | tf_op jit(solution)/shard_map/ppermute | solution.py:507
  89.4 1.3 %finish.1 = bf16[128,1280]{1,0:T(8,128)(2,1)} custom-call(f32[128,1280]{1,0:T(8,128)S(1)} %get-tuple-element.53.hidden, f32[1280]{0:T(1024)S(1)} %copy-done.7, f32[128,1280]{1,0:T(8,128)S(1)} %get-tuple-element.56.kept, bf16[128,1280]{1,0:T(8,128)(2,1)S(1)} %collective-permute-done.15.rest_0_, bf16[128,1280]{1,0:T(8,128)(2,1)S(1)} %collective-permute-done.18.rest_1_), custom_call_target="tpu_custom_call" | custom-call | flops 1638400 | bytes 1966080 | tf_op jit(solution)/shard_map/finish/pallas_call | solution.py:493
  (10 shorter events, 0.0 us)
Async XLA Ops:
  0.0 7.3 %copy-start.3 = (bf16[1,128,1280]{2,1,0:T(8,128)(2,1)S(1)}, bf16[1,128,1280]{2,1,0:T(8,128)(2,1)}, u32[]{:S(2)}) copy-start(bf16[1,128,1280]{2,1,0:T(8,128)(2,1)} %param.14) | copy-start | bytes 983044
  0.0 7.3 %copy-start.9 = (f32[1280]{0:T(1024)S(1)}, f32[1280]{0:T(1024)}, u32[]{:S(2)}) copy-start(f32[1280]{0:T(1024)} %rest_0_.1) | copy-start | bytes 15364
  2.7 19.2 %collective-permute-start = (bf16[640,256]{1,0:T(8,128)(2,1)}, bf16[640,256]{1,0:T(8,128)(2,1)S(1)}, u32[]{:S(2)}, u32[]{:S(2)}) collective-permute-start(bf16[640,256]{1,0:T(8,128)(2,1)} %get-tuple-element.35), channel_id=1, source_target_pairs={{0,1},{1,0},{2,3},{3,2},{4,5},{5,4},{6,7},{7,6},{8,9},{9,8},{10,11... | collective-permute-start | bytes 983048 | tf_op jit(solution)/shard_map/ppermute | solution.py:507
  5.8 16.3 %collective-permute-start.1 = (bf16[640,256]{1,0:T(8,128)(2,1)}, bf16[640,256]{1,0:T(8,128)(2,1)S(1)}, u32[]{:S(2)}, u32[]{:S(2)}) collective-permute-start(bf16[640,256]{1,0:T(8,128)(2,1)} %get-tuple-element.36), channel_id=1, source_target_pairs={{0,2},{1,3},{2,0},{3,1},{4,6},{5,7},{6,4},{7,5},{8,10},{9,11},{10,... | collective-permute-start | bytes 983048 | tf_op jit(solution)/shard_map/ppermute | solution.py:507
  7.3 16.5 %collective-permute-start.2 = (bf16[640,256]{1,0:T(8,128)(2,1)}, bf16[640,256]{1,0:T(8,128)(2,1)S(1)}, u32[]{:S(2)}, u32[]{:S(2)}) collective-permute-start(bf16[640,256]{1,0:T(8,128)(2,1)} %get-tuple-element.37), channel_id=1, source_target_pairs={{0,3},{1,2},{2,1},{3,0},{4,7},{5,6},{6,5},{7,4},{8,11},{9,10},{10,... | collective-permute-start | bytes 983048 | tf_op jit(solution)/shard_map/ppermute | solution.py:507
  7.3 16.5 %copy-start.11 = (bf16[640,256]{1,0:T(8,128)(2,1)S(1)}, bf16[640,256]{1,0:T(8,128)(2,1)}, u32[]{:S(2)}) copy-start(bf16[640,256]{1,0:T(8,128)(2,1)} %get-tuple-element.34.refs_0_.rest_0_) | copy-start | bytes 983044
  12.3 22.2 %all-to-all-start = ((bf16[8,320,128]{2,1,0:T(8,128)(2,1)}), bf16[8,320,128]{2,1,0:T(8,128)(2,1)S(1)}, u32[]{:S(2)}, u32[]{:S(2)}) async-start(bf16[8,320,128]{2,1,0:T(8,128)(2,1)} %bitcast.2), calls=%async_computation | async-start | bytes 1310720 | tf_op jit(solution)/shard_map/all_to_all | solution.py:536
  18.5 23.0 %collective-permute-start.3 = (bf16[640,128]{1,0:T(8,128)(2,1)S(1)}, bf16[640,128]{1,0:T(8,128)(2,1)S(1)}, u32[]{:S(2)}, u32[]{:S(2)}) collective-permute-start(bf16[640,128]{1,0:T(8,128)(2,1)S(1)} %get-tuple-element.41), channel_id=1, source_target_pairs={{0,1},{1,0},{2,3},{3,2},{4,5},{5,4},{6,7},{7,6},{8,9},{9,8},{10,11... | collective-permute-start | bytes 491528 | tf_op jit(solution)/shard_map/ppermute | solution.py:507
  20.5 21.0 %collective-permute-start.4 = (bf16[640,128]{1,0:T(8,128)(2,1)S(1)}, bf16[640,128]{1,0:T(8,128)(2,1)S(1)}, u32[]{:S(2)}, u32[]{:S(2)}) collective-permute-start(bf16[640,128]{1,0:T(8,128)(2,1)S(1)} %get-tuple-element.42), channel_id=1, source_target_pairs={{0,2},{1,3},{2,0},{3,1},{4,6},{5,7},{6,4},{7,5},{8,10},{9,11},{10,... | collective-permute-start | bytes 491528 | tf_op jit(solution)/shard_map/ppermute | solution.py:507
  22.0 19.5 %collective-permute-start.5 = (bf16[640,128]{1,0:T(8,128)(2,1)S(1)}, bf16[640,128]{1,0:T(8,128)(2,1)S(1)}, u32[]{:S(2)}, u32[]{:S(2)}) collective-permute-start(bf16[640,128]{1,0:T(8,128)(2,1)S(1)} %get-tuple-element.43), channel_id=1, source_target_pairs={{0,3},{1,2},{2,1},{3,0},{4,7},{5,6},{6,5},{7,4},{8,11},{9,10},{10,... | collective-permute-start | bytes 491528 | tf_op jit(solution)/shard_map/ppermute | solution.py:507
  23.9 17.7 %copy-start.10 = (s32[1,16]{1,0:T(1,128)S(1)}, s32[1,16]{1,0:T(1,128)}, u32[]{:S(2)}) copy-start(s32[1,16]{1,0:T(1,128)} %lengths.1) | copy-start | bytes 196
  34.5 7.0 %copy-start.8 = (bf16[1280,1280]{1,0:T(8,128)(2,1)S(1)}, bf16[1280,1280]{1,0:T(8,128)(2,1)}, u32[]{:S(2)}) copy-start(bf16[1280,1280]{1,0:T(8,128)(2,1)} %rest_4_.1) | copy-start | bytes 9830404
  41.5 19.9 %copy-start.6 = (f32[1280]{0:T(1024)S(1)}, f32[1280]{0:T(1024)}, u32[]{:S(2)}) copy-start(f32[1280]{0:T(1024)} %rate_hbm.2) | copy-start | bytes 15364
  41.6 23.1 %copy-start.1 = (bf16[1280,1280]{1,0:T(8,128)(2,1)S(1)}, bf16[1280,1280]{1,0:T(8,128)(2,1)}, u32[]{:S(2)}) copy-start(bf16[1280,1280]{1,0:T(8,128)(2,1)} %w_gate.3) | copy-start | bytes 9830404
  41.6 23.1 %copy-start.2 = (bf16[1280,1280]{1,0:T(8,128)(2,1)S(1)}, bf16[1280,1280]{1,0:T(8,128)(2,1)}, u32[]{:S(2)}) copy-start(bf16[1280,1280]{1,0:T(8,128)(2,1)} %w_down.3) | copy-start | bytes 9830404
  44.8 19.9 %copy-start = (bf16[1280,1280]{1,0:T(8,128)(2,1)S(1)}, bf16[1280,1280]{1,0:T(8,128)(2,1)}, u32[]{:S(2)}) copy-start(bf16[1280,1280]{1,0:T(8,128)(2,1)} %w_up.3) | copy-start | bytes 9830404
  44.8 19.9 %copy-start.4 = (f32[1280]{0:T(1024)S(1)}, f32[1280]{0:T(1024)}, u32[]{:S(2)}) copy-start(f32[1280]{0:T(1024)} %up_scale.3) | copy-start | bytes 15364
  44.8 19.9 %copy-start.5 = (f32[1280]{0:T(1024)S(1)}, f32[1280]{0:T(1024)}, u32[]{:S(2)}) copy-start(f32[1280]{0:T(1024)} %gate_scale.3) | copy-start | bytes 15364
  44.8 9.3 %collective-permute-start.6 = (bf16[336,128]{1,0:T(8,128)(2,1)S(1)}, bf16[336,128]{1,0:T(8,128)(2,1)S(1)}, u32[]{:S(2)}, u32[]{:S(2)}) collective-permute-start(bf16[336,128]{1,0:T(8,128)(2,1)S(1)} %get-tuple-element.45), channel_id=1, source_target_pairs={{0,1},{1,0},{2,3},{3,2},{4,5},{5,4},{6,7},{7,6},{8,9},{9,8},{10,11... | collective-permute-start | bytes 258056 | tf_op jit(solution)/shard_map/ppermute | solution.py:507
  46.5 10.2 %collective-permute-start.7 = (bf16[336,128]{1,0:T(8,128)(2,1)S(1)}, bf16[336,128]{1,0:T(8,128)(2,1)S(1)}, u32[]{:S(2)}, u32[]{:S(2)}) collective-permute-start(bf16[336,128]{1,0:T(8,128)(2,1)S(1)} %get-tuple-element.46), channel_id=1, source_target_pairs={{0,4},{1,5},{2,6},{3,7},{4,0},{5,1},{6,2},{7,3},{8,12},{9,13},{10,... | collective-permute-start | bytes 258056 | tf_op jit(solution)/shard_map/ppermute | solution.py:507
  48.3 12.4 %collective-permute-start.8 = (bf16[336,128]{1,0:T(8,128)(2,1)S(1)}, bf16[336,128]{1,0:T(8,128)(2,1)S(1)}, u32[]{:S(2)}, u32[]{:S(2)}) collective-permute-start(bf16[336,128]{1,0:T(8,128)(2,1)S(1)} %get-tuple-element.47), channel_id=1, source_target_pairs={{0,5},{1,4},{2,7},{3,6},{4,1},{5,0},{6,3},{7,2},{8,13},{9,12},{10,... | collective-permute-start | bytes 258056 | tf_op jit(solution)/shard_map/ppermute | solution.py:507
  49.3 11.5 %collective-permute-start.9 = (bf16[336,128]{1,0:T(8,128)(2,1)S(1)}, bf16[336,128]{1,0:T(8,128)(2,1)S(1)}, u32[]{:S(2)}, u32[]{:S(2)}) collective-permute-start(bf16[336,128]{1,0:T(8,128)(2,1)S(1)} %get-tuple-element.48), channel_id=1, source_target_pairs={{0,6},{1,7},{2,4},{3,5},{4,2},{5,3},{6,0},{7,1},{8,14},{9,15},{10,... | collective-permute-start | bytes 258056 | tf_op jit(solution)/shard_map/ppermute | solution.py:507
  52.5 8.2 %collective-permute-start.10 = (bf16[336,128]{1,0:T(8,128)(2,1)S(1)}, bf16[336,128]{1,0:T(8,128)(2,1)S(1)}, u32[]{:S(2)}, u32[]{:S(2)}) collective-permute-start(bf16[336,128]{1,0:T(8,128)(2,1)S(1)} %get-tuple-element.49), channel_id=1, source_target_pairs={{0,7},{1,6},{2,5},{3,4},{4,3},{5,2},{6,1},{7,0},{8,15},{9,14},{10,... | collective-permute-start | bytes 258056 | tf_op jit(solution)/shard_map/ppermute | solution.py:507
  54.1 7.1 %collective-permute-start.11 = (bf16[336,128]{1,0:T(8,128)(2,1)S(1)}, bf16[336,128]{1,0:T(8,128)(2,1)S(1)}, u32[]{:S(2)}, u32[]{:S(2)}) collective-permute-start(bf16[336,128]{1,0:T(8,128)(2,1)S(1)} %get-tuple-element.50), channel_id=1, source_target_pairs={{0,3},{1,2},{2,1},{3,0},{4,7},{5,6},{6,5},{7,4},{8,11},{9,10},{10,... | collective-permute-start | bytes 258056 | tf_op jit(solution)/shard_map/ppermute | solution.py:507
  56.6 4.8 %collective-permute-start.12 = (bf16[336,128]{1,0:T(8,128)(2,1)S(1)}, bf16[336,128]{1,0:T(8,128)(2,1)S(1)}, u32[]{:S(2)}, u32[]{:S(2)}) collective-permute-start(bf16[336,128]{1,0:T(8,128)(2,1)S(1)} %get-tuple-element.51), channel_id=1, source_target_pairs={{0,2},{1,3},{2,0},{3,1},{4,6},{5,7},{6,4},{7,5},{8,10},{9,11},{10,... | collective-permute-start | bytes 258056 | tf_op jit(solution)/shard_map/ppermute | solution.py:507
  63.0 1.7 %collective-permute-start.14 = (bf16[128,1280]{1,0:T(8,128)(2,1)S(1)}, bf16[128,1280]{1,0:T(8,128)(2,1)S(1)}, u32[]{:S(2)}, u32[]{:S(2)}) collective-permute-start(bf16[128,1280]{1,0:T(8,128)(2,1)S(1)} %get-tuple-element.54.first), channel_id=1, source_target_pairs={{0,8},{8,0},{16,24},{24,16},{1,9},{9,1},{17,25},{25,17},{2,10},{10... | collective-permute-start | bytes 983048 | tf_op jit(solution)/shard_map/ppermute | solution.py:507
  63.1 10.1 %collective-permute-start.13 = (bf16[128,1280]{1,0:T(8,128)(2,1)S(1)}, bf16[128,1280]{1,0:T(8,128)(2,1)S(1)}, u32[]{:S(2)}, u32[]{:S(2)}) collective-permute-start(bf16[128,1280]{1,0:T(8,128)(2,1)S(1)} %get-tuple-element.54.first), channel_id=1, source_target_pairs={{0,16},{8,24},{16,0},{24,8},{1,17},{9,25},{17,1},{25,9},{2,18},{10... | collective-permute-start | bytes 983048 | tf_op jit(solution)/shard_map/ppermute | solution.py:507
  73.2 16.2 %copy-start.7 = (f32[1280]{0:T(1024)S(1)}, f32[1280]{0:T(1024)}, u32[]{:S(2)}) copy-start(f32[1280]{0:T(1024)} %rate_hbm.3) | copy-start | bytes 15364
  73.2 1.6 %collective-permute-start.16 = (bf16[128,1280]{1,0:T(8,128)(2,1)S(1)}, bf16[128,1280]{1,0:T(8,128)(2,1)S(1)}, u32[]{:S(2)}, u32[]{:S(2)}) collective-permute-start(bf16[128,1280]{1,0:T(8,128)(2,1)S(1)} %collective-permute-done.13.first), channel_id=1, source_target_pairs={{0,8},{8,0},{16,24},{24,16},{1,9},{9,1},{17,25},{25,17},{2,10},{10... | collective-permute-start | bytes 983048 | tf_op jit(solution)/shard_map/ppermute | solution.py:507
  77.8 1.7 %collective-permute-start.17 = (bf16[128,1280]{1,0:T(8,128)(2,1)S(1)}, bf16[128,1280]{1,0:T(8,128)(2,1)S(1)}, u32[]{:S(2)}, u32[]{:S(2)}) collective-permute-start(bf16[128,1280]{1,0:T(8,128)(2,1)S(1)} %get-tuple-element.60), channel_id=1, source_target_pairs={{0,8},{8,0},{16,24},{24,16},{1,9},{9,1},{17,25},{25,17},{2,10},{10... | collective-permute-start | bytes 983048 | tf_op jit(solution)/shard_map/ppermute | solution.py:507
  78.0 3.1 %collective-permute-start.15 = (bf16[128,1280]{1,0:T(8,128)(2,1)S(1)}, bf16[128,1280]{1,0:T(8,128)(2,1)S(1)}, u32[]{:S(2)}, u32[]{:S(2)}) collective-permute-start(bf16[128,1280]{1,0:T(8,128)(2,1)S(1)} %get-tuple-element.57), channel_id=1, source_target_pairs={{0,8},{8,0},{16,24},{24,16},{1,9},{9,1},{17,25},{25,17},{2,10},{10... | collective-permute-start | bytes 983048 | tf_op jit(solution)/shard_map/ppermute | solution.py:507
  79.6 9.8 %collective-permute-start.18 = (bf16[128,1280]{1,0:T(8,128)(2,1)S(1)}, bf16[128,1280]{1,0:T(8,128)(2,1)S(1)}, u32[]{:S(2)}, u32[]{:S(2)}) collective-permute-start(bf16[128,1280]{1,0:T(8,128)(2,1)S(1)} %add_partials.1), channel_id=1, source_target_pairs={{0,16},{8,24},{16,0},{24,8},{1,17},{9,25},{17,1},{25,9},{2,18},{10... | collective-permute-start | bytes 983048 | tf_op jit(solution)/shard_map/ppermute | solution.py:507

commit v7 on v6

--- a/solution.py
+++ b/solution.py
@@ -383,14 +383,14 @@
 def project_kernel(order, place, tokens_hbm, rate_hbm, w_out, *rest):
     count = len(order)
     arrived, rest = rest[:count], rest[count:]
-    hidden_out, flat_out, mix, parts, tokens, rate, sems = rest
+    hidden_out, flat_out, mix, tokens, rate, sems = rest
     copies = fetch((tokens_hbm, rate_hbm), (tokens, rate), sems)
     squares = count // SQ
     i = lax.rem(place[0], SQ)
-    for m, part in zip(order, arrived):
-        parts[m // SQ * SQ + jnp.bitwise_xor(i, m % SQ)] = part[...]
-    for j in range(SQ):
-        group = [parts.at[s * SQ + j] for s in range(squares)]
+    parts = dict(zip(order, arrived))
+    for m in range(SQ):
+        group = [parts[s * SQ + m] for s in range(squares)]
+        start = jnp.bitwise_xor(i, m) * QD
         levels = []
         for part in group:
             pieces = part[QD:, :].astype(f32)
@@ -404,8 +404,8 @@
             mixed = functools.reduce(
                 jnp.add, [w[h : h + 1, :] * p[head, :].astype(f32) for w, p in zip(weights, group)]
             )
-            at = j * QD + h * HEAD
-            mix[at : at + HEAD, :] = mixed.astype(bf16)
+            at = pl.multiple_of(start + h * HEAD, HEAD)
+            mix[pl.ds(at, HEAD), :] = mixed.astype(bf16)
     wait(copies)
     hidden = unit(tokens[...].astype(f32))
     attn = jnp.concatenate(
@@ -426,7 +426,6 @@
         out_specs=[vmem()] * 2,
         scratch_shapes=[
             pltpu.VMEM((D, rows), bf16),
-            pltpu.VMEM((len(parts), *parts[0].shape), bf16),
             *fetched(tokens, rate),
         ],
         compiler_params=params(8),

time: 91.1 us -> 91 us (level)
  no operation moved by 1% of the time
where the time goes in v7:
time: 91 us; the launch traced here: 90.8 us
  waiting for transfers between devices  34.8 us (38%)
  starting transfers between devices  29 us (32%)
  Pallas kernels  26.6 us (29%)
    ppermute x19, waiting for transfers between devices, swap(): return lax.ppermute(shard, axis, [(j, j ^ mask) for j in range(length)])  24.1 us
    ppermute x19, starting transfers between devices, swap(): return lax.ppermute(shard, axis, [(j, j ^ mask) for j in range(length)])  22.8 us
    all_to_all x1, waiting for transfers between devices, body(): queries = lax.all_to_all(queries.reshape(extent, QD, rows), 'tok', 0, 0)  10.6 us
    pallas_call x1, Pallas kernels, cached_call(): pl.pallas_call(cached_kernel, out_shape=[jax.ShapeDtypeStruct((extent //...  6.98 us
    all_to_all x1, starting transfers between devices, body(): queries = lax.all_to_all(queries.reshape(extent, QD, rows), 'tok', 0, 0)  6.21 us
    pallas_call x2, Pallas kernels, mlp_call(): pl.pallas_call(mlp_kernel, out_shape=[jax.ShapeDtypeStruct((rows, D), f32...  5.98 us
    pallas_call x1, Pallas kernels, qkv_call(): pl.pallas_call(functools.partial(qkv_kernel, squares), out_shape=[jax.Sha...  4.92 us
    pallas_call x1, Pallas kernels, suffix_call(): pl.pallas_call(functools.partial(suffix_kernel, extent), out_shape=[jax.S...  3.18 us
  transfers between devices with their start and end apart: 20, of which 10 were waited for; matrix products, arithmetic and copies ran while one was open for 0% of the time, Pallas kernels for 16%

profile of v7, /device:TPU:0, one launch (start us, length us, event | category | flops | bytes accessed | tf_op | source)
XLA Modules:
  0.0 90.8 jit_solution(9660935970221600978)
XLA Ops:
  0.0 2.7 %prefix_prep.1 = (bf16[640,256]{1,0:T(8,128)(2,1)}, bf16[640,256]{1,0:T(8,128)(2,1)}, bf16[640,256]{1,0:T(8,128)(2,1)}, bf16[640,256]{1,0:T(8,128)(2,1)}) custom-call(s32[1]{0:T(128)} %bitcast.place, f32[1280]{0:T(1024)} %rest_0_.1, bf16[256,1280]{1,0:T(8,128)(2,1)} %bitcast.8, bf16[256,1280]{1,0:T(8,128)(2,1)} %bitcast.9), custom_call_target="tpu_custom_call" | custom-call | flops 49999998976 | bytes 2621440 | tf_op jit(solution)/shard_map/prefix_prep/pallas_call | solution.py:126
  2.7 3.0 %collective-permute-start = (bf16[640,256]{1,0:T(8,128)(2,1)}, bf16[640,256]{1,0:T(8,128)(2,1)S(1)}, u32[]{:S(2)}, u32[]{:S(2)}) collective-permute-start(bf16[640,256]{1,0:T(8,128)(2,1)} %get-tuple-element.35), channel_id=1, source_target_pairs={{0,1},{1,0},{2,3},{3,2},{4,5},{5,4},{6,7},{7,6},{8,9},{9,8},{10,11... | collective-permute-start | bytes 983048 | tf_op jit(solution)/shard_map/ppermute | solution.py:506
  5.8 1.6 %collective-permute-start.1 = (bf16[640,256]{1,0:T(8,128)(2,1)}, bf16[640,256]{1,0:T(8,128)(2,1)S(1)}, u32[]{:S(2)}, u32[]{:S(2)}) collective-permute-start(bf16[640,256]{1,0:T(8,128)(2,1)} %get-tuple-element.36), channel_id=1, source_target_pairs={{0,2},{1,3},{2,0},{3,1},{4,6},{5,7},{6,4},{7,5},{8,10},{9,11},{10,... | collective-permute-start | bytes 983048 | tf_op jit(solution)/shard_map/ppermute | solution.py:506
  7.3 0.0 collective-permute-start.2
  7.3 0.0 copy-done.3
  7.3 0.0 copy-done.9
  7.3 0.0 copy-start.11
  7.4 4.9 %qkv.1 = (bf16[2560,128]{1,0:T(8,128)(2,1)}, bf16[640,128]{1,0:T(8,128)(2,1)S(1)}, bf16[640,128]{1,0:T(8,128)(2,1)S(1)}, bf16[640,128]{1,0:T(8,128)(2,1)S(1)}, bf16[640,128]{1,0:T(8,128)(2,1)S(1)}) custom-call(s32[1]{0:T(128)} %bitcast.place, bf16[128,1280]{1,0:T(8,128)(2,1)S(1)} %bitcast.6, f32[1280]{0:T(1024)S(1)} %copy-done.9, bf16[1280,3840]{1,0:T(8,128)(2,1)} %w_hbm.1), custom_call_target="tpu_custom_call" | custom-call | flops 49999998976 | bytes 9830400 | tf_op jit(solution)/shard_map/qkv/pallas_call | solution.py:170
  12.3 6.2 %all-to-all-start = ((bf16[8,320,128]{2,1,0:T(8,128)(2,1)}), bf16[8,320,128]{2,1,0:T(8,128)(2,1)S(1)}, u32[]{:S(2)}, u32[]{:S(2)}) async-start(bf16[8,320,128]{2,1,0:T(8,128)(2,1)} %bitcast.2), calls=%async_computation | async-start | bytes 1310720 | tf_op jit(solution)/shard_map/all_to_all | solution.py:535
  18.5 2.0 %collective-permute-start.3 = (bf16[640,128]{1,0:T(8,128)(2,1)S(1)}, bf16[640,128]{1,0:T(8,128)(2,1)S(1)}, u32[]{:S(2)}, u32[]{:S(2)}) collective-permute-start(bf16[640,128]{1,0:T(8,128)(2,1)S(1)} %get-tuple-element.41), channel_id=1, source_target_pairs={{0,1},{1,0},{2,3},{3,2},{4,5},{5,4},{6,7},{7,6},{8,9},{9,8},{10,11... | collective-permute-start | bytes 491528 | tf_op jit(solution)/shard_map/ppermute | solution.py:506
  20.5 1.5 %collective-permute-start.4 = (bf16[640,128]{1,0:T(8,128)(2,1)S(1)}, bf16[640,128]{1,0:T(8,128)(2,1)S(1)}, u32[]{:S(2)}, u32[]{:S(2)}) collective-permute-start(bf16[640,128]{1,0:T(8,128)(2,1)S(1)} %get-tuple-element.42), channel_id=1, source_target_pairs={{0,2},{1,3},{2,0},{3,1},{4,6},{5,7},{6,4},{7,5},{8,10},{9,11},{10,... | collective-permute-start | bytes 491528 | tf_op jit(solution)/shard_map/ppermute | solution.py:506
  22.0 0.0 collective-permute-done.refs_1_.rest_1_
  22.0 0.0 collective-permute-start.5
  22.0 0.0 collective-permute-done.1.refs_2_.rest_2_
  22.0 1.8 %collective-permute-done.2.refs_3_.rest_3_ = bf16[640,256]{1,0:T(8,128)(2,1)S(1)} collective-permute-done((bf16[640,256]{1,0:T(8,128)(2,1)}, bf16[640,256]{1,0:T(8,128)(2,1)S(1)}, u32[]{:S(2)}, u32[]{:S(2)}) %collective-permute-start.2) | collective-permute-done | bytes 327712 | tf_op jit(solution)/shard_map/ppermute | solution.py:506
  23.8 0.0 copy-done.11
  23.9 0.0 copy-start.10
  23.9 10.6 %all-to-all-done.query_all = bf16[8,320,128]{2,1,0:T(8,128)(2,1)S(1)} async-done(((bf16[8,320,128]{2,1,0:T(8,128)(2,1)}), bf16[8,320,128]{2,1,0:T(8,128)(2,1)S(1)}, u32[]{:S(2)}, u32[]{:S(2)}) %all-to-all-start) | async-done | bytes 655392 | tf_op jit(solution)/shard_map/all_to_all | solution.py:535
  34.5 7.0 %attend_cached.1 = (f32[2,320,512]{2,1,0:T(8,128)S(1)}, f32[2,16,512]{2,1,0:T(8,128)S(1)}) custom-call(bf16[8,320,128]{2,1,0:T(8,128)(2,1)S(1)} %all-to-all-done.query_all, f32[16,128]{1,0:T(8,128)S(1)} %arrive.1._, bf16[640,256]{1,0:T(8,128)(2,1)S(1)} %copy-done.11, bf16[640,256]{1,0:T(8,128)(2,1)S(1)} %collective-permute-done.refs_1_.rest_1_, ...), custom_call_target="tpu_custom_call" | custom-call | flops 1000000000 | tf_op jit(solution)/shard_map/attend_cached/pallas_call | solution.py:252
  41.5 0.0 collective-permute-done.3.rest_1_
  41.5 0.0 collective-permute-done.4.rest_2_
  41.5 0.0 collective-permute-done.5.rest_3_
  41.5 0.0 copy-done.10
  41.5 0.0 copy-done.8
  41.5 0.0 copy-start.6
  41.6 0.0 copy-start.1
  41.6 0.0 copy-start.2
  41.6 3.2 %attend_suffix.1 = (bf16[336,128]{1,0:T(8,128)(2,1)S(1)}, bf16[336,128]{1,0:T(8,128)(2,1)S(1)}, bf16[336,128]{1,0:T(8,128)(2,1)S(1)}, bf16[336,128]{1,0:T(8,128)...) custom-call(s32[1]{0:T(128)} %bitcast.place, ...), custom_call_target="tpu_custom_call" | custom-call | flops 20000000000 | bytes 8388608 | tf_op jit(solution)/shard_map/attend_suffix/pallas_call | solution.py:366
  44.8 0.0 copy-start
  44.8 0.0 copy-start.4
  44.8 0.0 copy-start.5
  44.8 1.7 %collective-permute-start.6 = (bf16[336,128]{1,0:T(8,128)(2,1)S(1)}, bf16[336,128]{1,0:T(8,128)(2,1)S(1)}, u32[]{:S(2)}, u32[]{:S(2)}) collective-permute-start(bf16[336,128]{1,0:T(8,128)(2,1)S(1)} %get-tuple-element.45), channel_id=1, source_target_pairs={{0,1},{1,0},{2,3},{3,2},{4,5},{5,4},{6,7},{7,6},{8,9},{9,8},{10,11... | collective-permute-start | bytes 258056 | tf_op jit(solution)/shard_map/ppermute | solution.py:506
  46.5 1.8 %collective-permute-start.7 = (bf16[336,128]{1,0:T(8,128)(2,1)S(1)}, bf16[336,128]{1,0:T(8,128)(2,1)S(1)}, u32[]{:S(2)}, u32[]{:S(2)}) collective-permute-start(bf16[336,128]{1,0:T(8,128)(2,1)S(1)} %get-tuple-element.46), channel_id=1, source_target_pairs={{0,4},{1,5},{2,6},{3,7},{4,0},{5,1},{6,2},{7,3},{8,12},{9,13},{10,... | collective-permute-start | bytes 258056 | tf_op jit(solution)/shard_map/ppermute | solution.py:506
  48.3 1.0 %collective-permute-start.8 = (bf16[336,128]{1,0:T(8,128)(2,1)S(1)}, bf16[336,128]{1,0:T(8,128)(2,1)S(1)}, u32[]{:S(2)}, u32[]{:S(2)}) collective-permute-start(bf16[336,128]{1,0:T(8,128)(2,1)S(1)} %get-tuple-element.47), channel_id=1, source_target_pairs={{0,5},{1,4},{2,7},{3,6},{4,1},{5,0},{6,3},{7,2},{8,13},{9,12},{10,... | collective-permute-start | bytes 258056 | tf_op jit(solution)/shard_map/ppermute | solution.py:506
  49.3 3.3 %collective-permute-start.9 = (bf16[336,128]{1,0:T(8,128)(2,1)S(1)}, bf16[336,128]{1,0:T(8,128)(2,1)S(1)}, u32[]{:S(2)}, u32[]{:S(2)}) collective-permute-start(bf16[336,128]{1,0:T(8,128)(2,1)S(1)} %get-tuple-element.48), channel_id=1, source_target_pairs={{0,6},{1,7},{2,4},{3,5},{4,2},{5,3},{6,0},{7,1},{8,14},{9,15},{10,... | collective-permute-start | bytes 258056 | tf_op jit(solution)/shard_map/ppermute | solution.py:506
  52.5 1.6 %collective-permute-start.10 = (bf16[336,128]{1,0:T(8,128)(2,1)S(1)}, bf16[336,128]{1,0:T(8,128)(2,1)S(1)}, u32[]{:S(2)}, u32[]{:S(2)}) collective-permute-start(bf16[336,128]{1,0:T(8,128)(2,1)S(1)} %get-tuple-element.49), channel_id=1, source_target_pairs={{0,7},{1,6},{2,5},{3,4},{4,3},{5,2},{6,1},{7,0},{8,15},{9,14},{10,... | collective-permute-start | bytes 258056 | tf_op jit(solution)/shard_map/ppermute | solution.py:506
  54.1 0.0 collective-permute-done.6.rest_0_
  54.1 1.5 %collective-permute-start.11 = (bf16[336,128]{1,0:T(8,128)(2,1)S(1)}, bf16[336,128]{1,0:T(8,128)(2,1)S(1)}, u32[]{:S(2)}, u32[]{:S(2)}) collective-permute-start(bf16[336,128]{1,0:T(8,128)(2,1)S(1)} %get-tuple-element.50), channel_id=1, source_target_pairs={{0,3},{1,2},{2,1},{3,0},{4,7},{5,6},{6,5},{7,4},{8,11},{9,10},{10,... | collective-permute-start | bytes 258056 | tf_op jit(solution)/shard_map/ppermute | solution.py:506
  55.7 1.0 %collective-permute-done.7.rest_1_ = bf16[336,128]{1,0:T(8,128)(2,1)S(1)} collective-permute-done((bf16[336,128]{1,0:T(8,128)(2,1)S(1)}, bf16[336,128]{1,0:T(8,128)(2,1)S(1)}, u32[]{:S(2)}, u32[]{:S(2)}) %collective-permute-start.7) | collective-permute-done | bytes 86048 | tf_op jit(solution)/shard_map/ppermute | solution.py:506
  56.6 0.0 collective-permute-start.12
  56.6 4.1 %collective-permute-done.8.rest_2_ = bf16[336,128]{1,0:T(8,128)(2,1)S(1)} collective-permute-done((bf16[336,128]{1,0:T(8,128)(2,1)S(1)}, bf16[336,128]{1,0:T(8,128)(2,1)S(1)}, u32[]{:S(2)}, u32[]{:S(2)}) %collective-permute-start.8) | collective-permute-done | bytes 86048 | tf_op jit(solution)/shard_map/ppermute | solution.py:506
  60.7 0.0 collective-permute-done.9.rest_3_
  60.7 0.0 collective-permute-done.10.rest_4_
  60.7 0.4 collective-permute-done.11.rest_5_
  61.2 0.3 collective-permute-done.12.rest_6_
  61.5 1.5 %project.1 = (f32[128,1280]{1,0:T(8,128)S(1)}, bf16[128,1280]{1,0:T(8,128)(2,1)S(1)}) custom-call(s32[1]{0:T(128)} %bitcast.place, bf16[128,1280]{1,0:T(8,128)(2,1)S(1)} %bitcast.7, f32[1280]{0:T(1024)S(1)} %copy-done.6, bf16[1280,1280]{1,0:T(8,128)(2,1)S(1)} %get-tuple-element.44.w_out, bf16[336,128]{1,0:T(8,128)(2,1)S(1)} %collective-permute-done.6.rest_0_, ...), custom_call_target="tpu_custom_call" | custom-call | flops 419430400 | bytes 3276800 | tf_op jit(solution)/shard_map/project/pallas_call | solution.py:422
  63.0 0.1 collective-permute-start.14
  63.0 1.6 %collective-permute-start.13 = (bf16[128,1280]{1,0:T(8,128)(2,1)S(1)}, bf16[128,1280]{1,0:T(8,128)(2,1)S(1)}, u32[]{:S(2)}, u32[]{:S(2)}) collective-permute-start(bf16[128,1280]{1,0:T(8,128)(2,1)S(1)} %get-tuple-element.54.first), channel_id=1, source_target_pairs={{0,16},{8,24},{16,0},{24,8},{1,17},{9,25},{17,1},{25,9},{2,18},{10... | collective-permute-start | bytes 983048 | tf_op jit(solution)/shard_map/ppermute | solution.py:506
  64.6 0.0 collective-permute-done.14.second
  64.7 0.0 copy-done.2
  64.7 3.0 %mlp.2 = (f32[128,1280]{1,0:T(8,128)S(1)}, bf16[128,1280]{1,0:T(8,128)(2,1)S(1)}) custom-call(bf16[128,1280]{1,0:T(8,128)(2,1)S(1)} %get-tuple-element.54.first, bf16[128,1280]{1,0:T(8,128)(2,1)S(1)} %collective-permute-done.14.second, bf16[1280,1280]{1,0:T(8,128)(2,1)S(1)} %copy-done, bf16[1280,1280]{1,0:T(8,128)(2,1)S(1)} %copy-done.1, ...), custom_call_target="tpu_custom_call" | custom-call | flops 2516582400 | bytes 9830400 | tf_op jit(solution)/shard_map/mlp/pallas_call | solution.py:452
  67.7 5.5 %collective-permute-done.13.first = bf16[128,1280]{1,0:T(8,128)(2,1)S(1)} collective-permute-done((bf16[128,1280]{1,0:T(8,128)(2,1)S(1)}, bf16[128,1280]{1,0:T(8,128)(2,1)S(1)}, u32[]{:S(2)}, u32[]{:S(2)}) %collective-permute-start.13) | collective-permute-done | bytes 327712 | tf_op jit(solution)/shard_map/ppermute | solution.py:506
  73.2 0.0 collective-permute-start.16
  73.2 1.6 %collective-permute-done.16.second = bf16[128,1280]{1,0:T(8,128)(2,1)S(1)} collective-permute-done((bf16[128,1280]{1,0:T(8,128)(2,1)S(1)}, bf16[128,1280]{1,0:T(8,128)(2,1)S(1)}, u32[]{:S(2)}, u32[]{:S(2)}) %collective-permute-start.16) | collective-permute-done | bytes 327712 | tf_op jit(solution)/shard_map/ppermute | solution.py:506
  74.8 3.0 %mlp.3 = (f32[128,1280]{1,0:T(8,128)S(1)}, bf16[128,1280]{1,0:T(8,128)(2,1)S(1)}) custom-call(bf16[128,1280]{1,0:T(8,128)(2,1)S(1)} %collective-permute-done.13.first, bf16[128,1280]{1,0:T(8,128)(2,1)S(1)} %collective-permute-done.16.second, bf16[1280,1280]{1,0:T(8,128)(2,1)S(1)} %copy-done, bf16[1280,1280]{1,0:T(8,128)(2,1)S(1)} %copy-done.1, ...), custom_call_target="tpu_custom_call" | custom-call | flops 2516582400 | bytes 9830400 | tf_op jit(solution)/shard_map/mlp/pallas_call | solution.py:452
  77.8 0.2 collective-permute-start.17
  78.0 0.4 collective-permute-start.15
  78.4 1.1 %collective-permute-done.17.arrived = bf16[128,1280]{1,0:T(8,128)(2,1)S(1)} collective-permute-done((bf16[128,1280]{1,0:T(8,128)(2,1)S(1)}, bf16[128,1280]{1,0:T(8,128)(2,1)S(1)}, u32[]{:S(2)}, u32[]{:S(2)}) %collective-permute-start.17) | collective-permute-done | bytes 327712 | tf_op jit(solution)/shard_map/ppermute | solution.py:506
  79.5 0.1 add_partials.1
  79.6 1.6 %collective-permute-start.18 = (bf16[128,1280]{1,0:T(8,128)(2,1)S(1)}, bf16[128,1280]{1,0:T(8,128)(2,1)S(1)}, u32[]{:S(2)}, u32[]{:S(2)}) collective-permute-start(bf16[128,1280]{1,0:T(8,128)(2,1)S(1)} %add_partials.1), channel_id=1, source_target_pairs={{0,16},{8,24},{16,0},{24,8},{1,17},{9,25},{17,1},{25,9},{2,18},{10... | collective-permute-start | bytes 983048 | tf_op jit(solution)/shard_map/ppermute | solution.py:506
  81.1 0.0 collective-permute-done.15.rest_0_
  81.1 8.2 %collective-permute-done.18.rest_1_ = bf16[128,1280]{1,0:T(8,128)(2,1)S(1)} collective-permute-done((bf16[128,1280]{1,0:T(8,128)(2,1)S(1)}, bf16[128,1280]{1,0:T(8,128)(2,1)S(1)}, u32[]{:S(2)}, u32[]{:S(2)}) %collective-permute-start.18) | collective-permute-done | bytes 327712 | tf_op jit(solution)/shard_map/ppermute | solution.py:506
  89.4 0.0 copy-done.7
  89.4 1.3 %finish.1 = bf16[128,1280]{1,0:T(8,128)(2,1)} custom-call(f32[128,1280]{1,0:T(8,128)S(1)} %get-tuple-element.53.hidden, f32[1280]{0:T(1024)S(1)} %copy-done.7, f32[128,1280]{1,0:T(8,128)S(1)} %get-tuple-element.56.kept, bf16[128,1280]{1,0:T(8,128)(2,1)S(1)} %collective-permute-done.15.rest_0_, bf16[128,1280]{1,0:T(8,128)(2,1)S(1)} %collective-permute-done.18.rest_1_), custom_call_target="tpu_custom_call" | custom-call | flops 1638400 | bytes 1966080 | tf_op jit(solution)/shard_map/finish/pallas_call | solution.py:492
  (10 shorter events, 0.0 us)
Async XLA Ops:
  0.0 7.3 %copy-start.3 = (bf16[1,128,1280]{2,1,0:T(8,128)(2,1)S(1)}, bf16[1,128,1280]{2,1,0:T(8,128)(2,1)}, u32[]{:S(2)}) copy-start(bf16[1,128,1280]{2,1,0:T(8,128)(2,1)} %param.14) | copy-start | bytes 983044
  0.0 7.3 %copy-start.9 = (f32[1280]{0:T(1024)S(1)}, f32[1280]{0:T(1024)}, u32[]{:S(2)}) copy-start(f32[1280]{0:T(1024)} %rest_0_.1) | copy-start | bytes 15364
  2.7 19.2 %collective-permute-start = (bf16[640,256]{1,0:T(8,128)(2,1)}, bf16[640,256]{1,0:T(8,128)(2,1)S(1)}, u32[]{:S(2)}, u32[]{:S(2)}) collective-permute-start(bf16[640,256]{1,0:T(8,128)(2,1)} %get-tuple-element.35), channel_id=1, source_target_pairs={{0,1},{1,0},{2,3},{3,2},{4,5},{5,4},{6,7},{7,6},{8,9},{9,8},{10,11... | collective-permute-start | bytes 983048 | tf_op jit(solution)/shard_map/ppermute | solution.py:506
  5.8 16.3 %collective-permute-start.1 = (bf16[640,256]{1,0:T(8,128)(2,1)}, bf16[640,256]{1,0:T(8,128)(2,1)S(1)}, u32[]{:S(2)}, u32[]{:S(2)}) collective-permute-start(bf16[640,256]{1,0:T(8,128)(2,1)} %get-tuple-element.36), channel_id=1, source_target_pairs={{0,2},{1,3},{2,0},{3,1},{4,6},{5,7},{6,4},{7,5},{8,10},{9,11},{10,... | collective-permute-start | bytes 983048 | tf_op jit(solution)/shard_map/ppermute | solution.py:506
  7.3 16.5 %collective-permute-start.2 = (bf16[640,256]{1,0:T(8,128)(2,1)}, bf16[640,256]{1,0:T(8,128)(2,1)S(1)}, u32[]{:S(2)}, u32[]{:S(2)}) collective-permute-start(bf16[640,256]{1,0:T(8,128)(2,1)} %get-tuple-element.37), channel_id=1, source_target_pairs={{0,3},{1,2},{2,1},{3,0},{4,7},{5,6},{6,5},{7,4},{8,11},{9,10},{10,... | collective-permute-start | bytes 983048 | tf_op jit(solution)/shard_map/ppermute | solution.py:506
  7.3 16.5 %copy-start.11 = (bf16[640,256]{1,0:T(8,128)(2,1)S(1)}, bf16[640,256]{1,0:T(8,128)(2,1)}, u32[]{:S(2)}) copy-start(bf16[640,256]{1,0:T(8,128)(2,1)} %get-tuple-element.34.refs_0_.rest_0_) | copy-start | bytes 983044
  12.3 22.2 %all-to-all-start = ((bf16[8,320,128]{2,1,0:T(8,128)(2,1)}), bf16[8,320,128]{2,1,0:T(8,128)(2,1)S(1)}, u32[]{:S(2)}, u32[]{:S(2)}) async-start(bf16[8,320,128]{2,1,0:T(8,128)(2,1)} %bitcast.2), calls=%async_computation | async-start | bytes 1310720 | tf_op jit(solution)/shard_map/all_to_all | solution.py:535
  18.5 23.0 %collective-permute-start.3 = (bf16[640,128]{1,0:T(8,128)(2,1)S(1)}, bf16[640,128]{1,0:T(8,128)(2,1)S(1)}, u32[]{:S(2)}, u32[]{:S(2)}) collective-permute-start(bf16[640,128]{1,0:T(8,128)(2,1)S(1)} %get-tuple-element.41), channel_id=1, source_target_pairs={{0,1},{1,0},{2,3},{3,2},{4,5},{5,4},{6,7},{7,6},{8,9},{9,8},{10,11... | collective-permute-start | bytes 491528 | tf_op jit(solution)/shard_map/ppermute | solution.py:506
  20.5 21.0 %collective-permute-start.4 = (bf16[640,128]{1,0:T(8,128)(2,1)S(1)}, bf16[640,128]{1,0:T(8,128)(2,1)S(1)}, u32[]{:S(2)}, u32[]{:S(2)}) collective-permute-start(bf16[640,128]{1,0:T(8,128)(2,1)S(1)} %get-tuple-element.42), channel_id=1, source_target_pairs={{0,2},{1,3},{2,0},{3,1},{4,6},{5,7},{6,4},{7,5},{8,10},{9,11},{10,... | collective-permute-start | bytes 491528 | tf_op jit(solution)/shard_map/ppermute | solution.py:506
  22.0 19.5 %collective-permute-start.5 = (bf16[640,128]{1,0:T(8,128)(2,1)S(1)}, bf16[640,128]{1,0:T(8,128)(2,1)S(1)}, u32[]{:S(2)}, u32[]{:S(2)}) collective-permute-start(bf16[640,128]{1,0:T(8,128)(2,1)S(1)} %get-tuple-element.43), channel_id=1, source_target_pairs={{0,3},{1,2},{2,1},{3,0},{4,7},{5,6},{6,5},{7,4},{8,11},{9,10},{10,... | collective-permute-start | bytes 491528 | tf_op jit(solution)/shard_map/ppermute | solution.py:506
  23.9 17.7 %copy-start.10 = (s32[1,16]{1,0:T(1,128)S(1)}, s32[1,16]{1,0:T(1,128)}, u32[]{:S(2)}) copy-start(s32[1,16]{1,0:T(1,128)} %lengths.1) | copy-start | bytes 196
  34.5 7.0 %copy-start.8 = (bf16[1280,1280]{1,0:T(8,128)(2,1)S(1)}, bf16[1280,1280]{1,0:T(8,128)(2,1)}, u32[]{:S(2)}) copy-start(bf16[1280,1280]{1,0:T(8,128)(2,1)} %rest_4_.1) | copy-start | bytes 9830404
  41.5 19.9 %copy-start.6 = (f32[1280]{0:T(1024)S(1)}, f32[1280]{0:T(1024)}, u32[]{:S(2)}) copy-start(f32[1280]{0:T(1024)} %rate_hbm.2) | copy-start | bytes 15364
  41.6 23.1 %copy-start.1 = (bf16[1280,1280]{1,0:T(8,128)(2,1)S(1)}, bf16[1280,1280]{1,0:T(8,128)(2,1)}, u32[]{:S(2)}) copy-start(bf16[1280,1280]{1,0:T(8,128)(2,1)} %w_gate.3) | copy-start | bytes 9830404
  41.6 23.1 %copy-start.2 = (bf16[1280,1280]{1,0:T(8,128)(2,1)S(1)}, bf16[1280,1280]{1,0:T(8,128)(2,1)}, u32[]{:S(2)}) copy-start(bf16[1280,1280]{1,0:T(8,128)(2,1)} %w_down.3) | copy-start | bytes 9830404
  44.8 19.9 %copy-start = (bf16[1280,1280]{1,0:T(8,128)(2,1)S(1)}, bf16[1280,1280]{1,0:T(8,128)(2,1)}, u32[]{:S(2)}) copy-start(bf16[1280,1280]{1,0:T(8,128)(2,1)} %w_up.3) | copy-start | bytes 9830404
  44.8 19.9 %copy-start.4 = (f32[1280]{0:T(1024)S(1)}, f32[1280]{0:T(1024)}, u32[]{:S(2)}) copy-start(f32[1280]{0:T(1024)} %up_scale.3) | copy-start | bytes 15364
  44.8 19.9 %copy-start.5 = (f32[1280]{0:T(1024)S(1)}, f32[1280]{0:T(1024)}, u32[]{:S(2)}) copy-start(f32[1280]{0:T(1024)} %gate_scale.3) | copy-start | bytes 15364
  44.8 9.3 %collective-permute-start.6 = (bf16[336,128]{1,0:T(8,128)(2,1)S(1)}, bf16[336,128]{1,0:T(8,128)(2,1)S(1)}, u32[]{:S(2)}, u32[]{:S(2)}) collective-permute-start(bf16[336,128]{1,0:T(8,128)(2,1)S(1)} %get-tuple-element.45), channel_id=1, source_target_pairs={{0,1},{1,0},{2,3},{3,2},{4,5},{5,4},{6,7},{7,6},{8,9},{9,8},{10,11... | collective-permute-start | bytes 258056 | tf_op jit(solution)/shard_map/ppermute | solution.py:506
  46.5 10.2 %collective-permute-start.7 = (bf16[336,128]{1,0:T(8,128)(2,1)S(1)}, bf16[336,128]{1,0:T(8,128)(2,1)S(1)}, u32[]{:S(2)}, u32[]{:S(2)}) collective-permute-start(bf16[336,128]{1,0:T(8,128)(2,1)S(1)} %get-tuple-element.46), channel_id=1, source_target_pairs={{0,4},{1,5},{2,6},{3,7},{4,0},{5,1},{6,2},{7,3},{8,12},{9,13},{10,... | collective-permute-start | bytes 258056 | tf_op jit(solution)/shard_map/ppermute | solution.py:506
  48.3 12.4 %collective-permute-start.8 = (bf16[336,128]{1,0:T(8,128)(2,1)S(1)}, bf16[336,128]{1,0:T(8,128)(2,1)S(1)}, u32[]{:S(2)}, u32[]{:S(2)}) collective-permute-start(bf16[336,128]{1,0:T(8,128)(2,1)S(1)} %get-tuple-element.47), channel_id=1, source_target_pairs={{0,5},{1,4},{2,7},{3,6},{4,1},{5,0},{6,3},{7,2},{8,13},{9,12},{10,... | collective-permute-start | bytes 258056 | tf_op jit(solution)/shard_map/ppermute | solution.py:506
  49.3 11.5 %collective-permute-start.9 = (bf16[336,128]{1,0:T(8,128)(2,1)S(1)}, bf16[336,128]{1,0:T(8,128)(2,1)S(1)}, u32[]{:S(2)}, u32[]{:S(2)}) collective-permute-start(bf16[336,128]{1,0:T(8,128)(2,1)S(1)} %get-tuple-element.48), channel_id=1, source_target_pairs={{0,6},{1,7},{2,4},{3,5},{4,2},{5,3},{6,0},{7,1},{8,14},{9,15},{10,... | collective-permute-start | bytes 258056 | tf_op jit(solution)/shard_map/ppermute | solution.py:506
  52.5 8.2 %collective-permute-start.10 = (bf16[336,128]{1,0:T(8,128)(2,1)S(1)}, bf16[336,128]{1,0:T(8,128)(2,1)S(1)}, u32[]{:S(2)}, u32[]{:S(2)}) collective-permute-start(bf16[336,128]{1,0:T(8,128)(2,1)S(1)} %get-tuple-element.49), channel_id=1, source_target_pairs={{0,7},{1,6},{2,5},{3,4},{4,3},{5,2},{6,1},{7,0},{8,15},{9,14},{10,... | collective-permute-start | bytes 258056 | tf_op jit(solution)/shard_map/ppermute | solution.py:506
  54.1 7.1 %collective-permute-start.11 = (bf16[336,128]{1,0:T(8,128)(2,1)S(1)}, bf16[336,128]{1,0:T(8,128)(2,1)S(1)}, u32[]{:S(2)}, u32[]{:S(2)}) collective-permute-start(bf16[336,128]{1,0:T(8,128)(2,1)S(1)} %get-tuple-element.50), channel_id=1, source_target_pairs={{0,3},{1,2},{2,1},{3,0},{4,7},{5,6},{6,5},{7,4},{8,11},{9,10},{10,... | collective-permute-start | bytes 258056 | tf_op jit(solution)/shard_map/ppermute | solution.py:506
  56.6 4.8 %collective-permute-start.12 = (bf16[336,128]{1,0:T(8,128)(2,1)S(1)}, bf16[336,128]{1,0:T(8,128)(2,1)S(1)}, u32[]{:S(2)}, u32[]{:S(2)}) collective-permute-start(bf16[336,128]{1,0:T(8,128)(2,1)S(1)} %get-tuple-element.51), channel_id=1, source_target_pairs={{0,2},{1,3},{2,0},{3,1},{4,6},{5,7},{6,4},{7,5},{8,10},{9,11},{10,... | collective-permute-start | bytes 258056 | tf_op jit(solution)/shard_map/ppermute | solution.py:506
  63.0 1.7 %collective-permute-start.14 = (bf16[128,1280]{1,0:T(8,128)(2,1)S(1)}, bf16[128,1280]{1,0:T(8,128)(2,1)S(1)}, u32[]{:S(2)}, u32[]{:S(2)}) collective-permute-start(bf16[128,1280]{1,0:T(8,128)(2,1)S(1)} %get-tuple-element.54.first), channel_id=1, source_target_pairs={{0,8},{8,0},{16,24},{24,16},{1,9},{9,1},{17,25},{25,17},{2,10},{10... | collective-permute-start | bytes 983048 | tf_op jit(solution)/shard_map/ppermute | solution.py:506
  63.0 10.1 %collective-permute-start.13 = (bf16[128,1280]{1,0:T(8,128)(2,1)S(1)}, bf16[128,1280]{1,0:T(8,128)(2,1)S(1)}, u32[]{:S(2)}, u32[]{:S(2)}) collective-permute-start(bf16[128,1280]{1,0:T(8,128)(2,1)S(1)} %get-tuple-element.54.first), channel_id=1, source_target_pairs={{0,16},{8,24},{16,0},{24,8},{1,17},{9,25},{17,1},{25,9},{2,18},{10... | collective-permute-start | bytes 983048 | tf_op jit(solution)/shard_map/ppermute | solution.py:506
  73.2 16.2 %copy-start.7 = (f32[1280]{0:T(1024)S(1)}, f32[1280]{0:T(1024)}, u32[]{:S(2)}) copy-start(f32[1280]{0:T(1024)} %rate_hbm.3) | copy-start | bytes 15364
  73.2 1.6 %collective-permute-start.16 = (bf16[128,1280]{1,0:T(8,128)(2,1)S(1)}, bf16[128,1280]{1,0:T(8,128)(2,1)S(1)}, u32[]{:S(2)}, u32[]{:S(2)}) collective-permute-start(bf16[128,1280]{1,0:T(8,128)(2,1)S(1)} %collective-permute-done.13.first), channel_id=1, source_target_pairs={{0,8},{8,0},{16,24},{24,16},{1,9},{9,1},{17,25},{25,17},{2,10},{10... | collective-permute-start | bytes 983048 | tf_op jit(solution)/shard_map/ppermute | solution.py:506
  77.8 1.7 %collective-permute-start.17 = (bf16[128,1280]{1,0:T(8,128)(2,1)S(1)}, bf16[128,1280]{1,0:T(8,128)(2,1)S(1)}, u32[]{:S(2)}, u32[]{:S(2)}) collective-permute-start(bf16[128,1280]{1,0:T(8,128)(2,1)S(1)} %get-tuple-element.60), channel_id=1, source_target_pairs={{0,8},{8,0},{16,24},{24,16},{1,9},{9,1},{17,25},{25,17},{2,10},{10... | collective-permute-start | bytes 983048 | tf_op jit(solution)/shard_map/ppermute | solution.py:506
  78.0 3.2 %collective-permute-start.15 = (bf16[128,1280]{1,0:T(8,128)(2,1)S(1)}, bf16[128,1280]{1,0:T(8,128)(2,1)S(1)}, u32[]{:S(2)}, u32[]{:S(2)}) collective-permute-start(bf16[128,1280]{1,0:T(8,128)(2,1)S(1)} %get-tuple-element.57), channel_id=1, source_target_pairs={{0,8},{8,0},{16,24},{24,16},{1,9},{9,1},{17,25},{25,17},{2,10},{10... | collective-permute-start | bytes 983048 | tf_op jit(solution)/shard_map/ppermute | solution.py:506
  79.6 9.8 %collective-permute-start.18 = (bf16[128,1280]{1,0:T(8,128)(2,1)S(1)}, bf16[128,1280]{1,0:T(8,128)(2,1)S(1)}, u32[]{:S(2)}, u32[]{:S(2)}) collective-permute-start(bf16[128,1280]{1,0:T(8,128)(2,1)S(1)} %add_partials.1), channel_id=1, source_target_pairs={{0,16},{8,24},{16,0},{24,8},{1,17},{9,25},{17,1},{25,9},{2,18},{10... | collective-permute-start | bytes 983048 | tf_op jit(solution)/shard_map/ppermute | solution.py:506

commit v8 on v7

--- a/solution.py
+++ b/solution.py
@@ -437,10 +437,11 @@
 def mlp_kernel(first, second, w_up, w_gate, w_down, up_scale, gate_scale, keep, send):
     rows = first.shape[0]
     data = jnp.concatenate([first[...], second[...]], axis=0)
-    up = jnp.dot(data, w_up[...], preferred_element_type=f32) * over_rows(up_scale, 2 * rows)
     gate = jnp.dot(data, w_gate[...], preferred_element_type=f32)
     gate = gate * (over_rows(gate_scale, 2 * rows) * math.sqrt(D))
-    act = (up * (gate / (1.0 + jnp.exp(-gate)))).astype(bf16)
+    gate = gate / (1.0 + jnp.exp(-gate))
+    up = jnp.dot(data, w_up[...], preferred_element_type=f32) * over_rows(up_scale, 2 * rows)
+    act = (up * gate).astype(bf16)
     part = jnp.dot(act, w_down[...], preferred_element_type=f32)
     keep[...] = part[:rows, :]
     send[...] = part[rows:, :].astype(bf16)

time: 91 us -> 90.9 us (level)
  no operation moved by 1% of the time
where the time goes in v8:
time: 90.9 us; the launch traced here: 90.7 us
  waiting for transfers between devices  34.8 us (38%)
  starting transfers between devices  29 us (32%)
  Pallas kernels  26.4 us (29%)
    ppermute x19, waiting for transfers between devices, swap(): return lax.ppermute(shard, axis, [(j, j ^ mask) for j in range(length)])  24.2 us
    ppermute x19, starting transfers between devices, swap(): return lax.ppermute(shard, axis, [(j, j ^ mask) for j in range(length)])  22.8 us
    all_to_all x1, waiting for transfers between devices, body(): queries = lax.all_to_all(queries.reshape(extent, QD, rows), 'tok', 0, 0)  10.6 us
    pallas_call x1, Pallas kernels, cached_call(): pl.pallas_call(cached_kernel, out_shape=[jax.ShapeDtypeStruct((extent //...  6.98 us
    all_to_all x1, starting transfers between devices, body(): queries = lax.all_to_all(queries.reshape(extent, QD, rows), 'tok', 0, 0)  6.21 us
    pallas_call x2, Pallas kernels, mlp_call(): pl.pallas_call(mlp_kernel, out_shape=[jax.ShapeDtypeStruct((rows, D), f32...  5.8 us
    pallas_call x1, Pallas kernels, qkv_call(): pl.pallas_call(functools.partial(qkv_kernel, squares), out_shape=[jax.Sha...  4.92 us
    pallas_call x1, Pallas kernels, suffix_call(): pl.pallas_call(functools.partial(suffix_kernel, extent), out_shape=[jax.S...  3.18 us
  transfers between devices with their start and end apart: 20, of which 10 were waited for; matrix products, arithmetic and copies ran while one was open for 0% of the time, Pallas kernels for 16%

profile of v8, /device:TPU:0, one launch (start us, length us, event | category | flops | bytes accessed | tf_op | source)
XLA Modules:
  0.0 90.7 jit_solution(12117806204983041530)
XLA Ops:
  0.0 2.7 %prefix_prep.1 = (bf16[640,256]{1,0:T(8,128)(2,1)}, bf16[640,256]{1,0:T(8,128)(2,1)}, bf16[640,256]{1,0:T(8,128)(2,1)}, bf16[640,256]{1,0:T(8,128)(2,1)}) custom-call(s32[1]{0:T(128)} %bitcast.place, f32[1280]{0:T(1024)} %rest_0_.1, bf16[256,1280]{1,0:T(8,128)(2,1)} %bitcast.8, bf16[256,1280]{1,0:T(8,128)(2,1)} %bitcast.9), custom_call_target="tpu_custom_call" | custom-call | flops 49999998976 | bytes 2621440 | tf_op jit(solution)/shard_map/prefix_prep/pallas_call | solution.py:126
  2.7 3.0 %collective-permute-start = (bf16[640,256]{1,0:T(8,128)(2,1)}, bf16[640,256]{1,0:T(8,128)(2,1)S(1)}, u32[]{:S(2)}, u32[]{:S(2)}) collective-permute-start(bf16[640,256]{1,0:T(8,128)(2,1)} %get-tuple-element.35), channel_id=1, source_target_pairs={{0,1},{1,0},{2,3},{3,2},{4,5},{5,4},{6,7},{7,6},{8,9},{9,8},{10,11... | collective-permute-start | bytes 983048 | tf_op jit(solution)/shard_map/ppermute | solution.py:507
  5.8 1.6 %collective-permute-start.1 = (bf16[640,256]{1,0:T(8,128)(2,1)}, bf16[640,256]{1,0:T(8,128)(2,1)S(1)}, u32[]{:S(2)}, u32[]{:S(2)}) collective-permute-start(bf16[640,256]{1,0:T(8,128)(2,1)} %get-tuple-element.36), channel_id=1, source_target_pairs={{0,2},{1,3},{2,0},{3,1},{4,6},{5,7},{6,4},{7,5},{8,10},{9,11},{10,... | collective-permute-start | bytes 983048 | tf_op jit(solution)/shard_map/ppermute | solution.py:507
  7.3 0.0 collective-permute-start.2
  7.3 0.0 copy-done.3
  7.3 0.0 copy-done.9
  7.3 0.0 copy-start.11
  7.4 4.9 %qkv.1 = (bf16[2560,128]{1,0:T(8,128)(2,1)}, bf16[640,128]{1,0:T(8,128)(2,1)S(1)}, bf16[640,128]{1,0:T(8,128)(2,1)S(1)}, bf16[640,128]{1,0:T(8,128)(2,1)S(1)}, bf16[640,128]{1,0:T(8,128)(2,1)S(1)}) custom-call(s32[1]{0:T(128)} %bitcast.place, bf16[128,1280]{1,0:T(8,128)(2,1)S(1)} %bitcast.6, f32[1280]{0:T(1024)S(1)} %copy-done.9, bf16[1280,3840]{1,0:T(8,128)(2,1)} %w_hbm.1), custom_call_target="tpu_custom_call" | custom-call | flops 49999998976 | bytes 9830400 | tf_op jit(solution)/shard_map/qkv/pallas_call | solution.py:170
  12.3 6.2 %all-to-all-start = ((bf16[8,320,128]{2,1,0:T(8,128)(2,1)}), bf16[8,320,128]{2,1,0:T(8,128)(2,1)S(1)}, u32[]{:S(2)}, u32[]{:S(2)}) async-start(bf16[8,320,128]{2,1,0:T(8,128)(2,1)} %bitcast.2), calls=%async_computation | async-start | bytes 1310720 | tf_op jit(solution)/shard_map/all_to_all | solution.py:536
  18.5 2.0 %collective-permute-start.3 = (bf16[640,128]{1,0:T(8,128)(2,1)S(1)}, bf16[640,128]{1,0:T(8,128)(2,1)S(1)}, u32[]{:S(2)}, u32[]{:S(2)}) collective-permute-start(bf16[640,128]{1,0:T(8,128)(2,1)S(1)} %get-tuple-element.41), channel_id=1, source_target_pairs={{0,1},{1,0},{2,3},{3,2},{4,5},{5,4},{6,7},{7,6},{8,9},{9,8},{10,11... | collective-permute-start | bytes 491528 | tf_op jit(solution)/shard_map/ppermute | solution.py:507
  20.5 1.5 %collective-permute-start.4 = (bf16[640,128]{1,0:T(8,128)(2,1)S(1)}, bf16[640,128]{1,0:T(8,128)(2,1)S(1)}, u32[]{:S(2)}, u32[]{:S(2)}) collective-permute-start(bf16[640,128]{1,0:T(8,128)(2,1)S(1)} %get-tuple-element.42), channel_id=1, source_target_pairs={{0,2},{1,3},{2,0},{3,1},{4,6},{5,7},{6,4},{7,5},{8,10},{9,11},{10,... | collective-permute-start | bytes 491528 | tf_op jit(solution)/shard_map/ppermute | solution.py:507
  22.0 0.0 collective-permute-done.refs_1_.rest_1_
  22.0 0.0 collective-permute-start.5
  22.0 0.0 collective-permute-done.1.refs_2_.rest_2_
  22.0 1.8 %collective-permute-done.2.refs_3_.rest_3_ = bf16[640,256]{1,0:T(8,128)(2,1)S(1)} collective-permute-done((bf16[640,256]{1,0:T(8,128)(2,1)}, bf16[640,256]{1,0:T(8,128)(2,1)S(1)}, u32[]{:S(2)}, u32[]{:S(2)}) %collective-permute-start.2) | collective-permute-done | bytes 327712 | tf_op jit(solution)/shard_map/ppermute | solution.py:507
  23.8 0.0 copy-done.11
  23.9 0.0 copy-start.10
  23.9 10.6 %all-to-all-done.query_all = bf16[8,320,128]{2,1,0:T(8,128)(2,1)S(1)} async-done(((bf16[8,320,128]{2,1,0:T(8,128)(2,1)}), bf16[8,320,128]{2,1,0:T(8,128)(2,1)S(1)}, u32[]{:S(2)}, u32[]{:S(2)}) %all-to-all-start) | async-done | bytes 655392 | tf_op jit(solution)/shard_map/all_to_all | solution.py:536
  34.5 7.0 %attend_cached.1 = (f32[2,320,512]{2,1,0:T(8,128)S(1)}, f32[2,16,512]{2,1,0:T(8,128)S(1)}) custom-call(bf16[8,320,128]{2,1,0:T(8,128)(2,1)S(1)} %all-to-all-done.query_all, f32[16,128]{1,0:T(8,128)S(1)} %arrive.1._, bf16[640,256]{1,0:T(8,128)(2,1)S(1)} %copy-done.11, bf16[640,256]{1,0:T(8,128)(2,1)S(1)} %collective-permute-done.refs_1_.rest_1_, ...), custom_call_target="tpu_custom_call" | custom-call | flops 1000000000 | tf_op jit(solution)/shard_map/attend_cached/pallas_call | solution.py:252
  41.5 0.0 collective-permute-done.3.rest_1_
  41.5 0.0 collective-permute-done.4.rest_2_
  41.5 0.0 collective-permute-done.5.rest_3_
  41.5 0.0 copy-done.10
  41.5 0.0 copy-done.8
  41.5 0.0 copy-start.6
  41.6 0.0 copy-start.1
  41.6 0.0 copy-start.2
  41.6 3.2 %attend_suffix.1 = (bf16[336,128]{1,0:T(8,128)(2,1)S(1)}, bf16[336,128]{1,0:T(8,128)(2,1)S(1)}, bf16[336,128]{1,0:T(8,128)(2,1)S(1)}, bf16[336,128]{1,0:T(8,128)...) custom-call(s32[1]{0:T(128)} %bitcast.place, ...), custom_call_target="tpu_custom_call" | custom-call | flops 20000000000 | bytes 8388608 | tf_op jit(solution)/shard_map/attend_suffix/pallas_call | solution.py:366
  44.8 0.0 copy-start
  44.8 0.0 copy-start.4
  44.8 0.0 copy-start.5
  44.8 1.7 %collective-permute-start.6 = (bf16[336,128]{1,0:T(8,128)(2,1)S(1)}, bf16[336,128]{1,0:T(8,128)(2,1)S(1)}, u32[]{:S(2)}, u32[]{:S(2)}) collective-permute-start(bf16[336,128]{1,0:T(8,128)(2,1)S(1)} %get-tuple-element.45), channel_id=1, source_target_pairs={{0,1},{1,0},{2,3},{3,2},{4,5},{5,4},{6,7},{7,6},{8,9},{9,8},{10,11... | collective-permute-start | bytes 258056 | tf_op jit(solution)/shard_map/ppermute | solution.py:507
  46.5 1.8 %collective-permute-start.7 = (bf16[336,128]{1,0:T(8,128)(2,1)S(1)}, bf16[336,128]{1,0:T(8,128)(2,1)S(1)}, u32[]{:S(2)}, u32[]{:S(2)}) collective-permute-start(bf16[336,128]{1,0:T(8,128)(2,1)S(1)} %get-tuple-element.46), channel_id=1, source_target_pairs={{0,4},{1,5},{2,6},{3,7},{4,0},{5,1},{6,2},{7,3},{8,12},{9,13},{10,... | collective-permute-start | bytes 258056 | tf_op jit(solution)/shard_map/ppermute | solution.py:507
  48.3 1.0 %collective-permute-start.8 = (bf16[336,128]{1,0:T(8,128)(2,1)S(1)}, bf16[336,128]{1,0:T(8,128)(2,1)S(1)}, u32[]{:S(2)}, u32[]{:S(2)}) collective-permute-start(bf16[336,128]{1,0:T(8,128)(2,1)S(1)} %get-tuple-element.47), channel_id=1, source_target_pairs={{0,5},{1,4},{2,7},{3,6},{4,1},{5,0},{6,3},{7,2},{8,13},{9,12},{10,... | collective-permute-start | bytes 258056 | tf_op jit(solution)/shard_map/ppermute | solution.py:507
  49.3 3.3 %collective-permute-start.9 = (bf16[336,128]{1,0:T(8,128)(2,1)S(1)}, bf16[336,128]{1,0:T(8,128)(2,1)S(1)}, u32[]{:S(2)}, u32[]{:S(2)}) collective-permute-start(bf16[336,128]{1,0:T(8,128)(2,1)S(1)} %get-tuple-element.48), channel_id=1, source_target_pairs={{0,6},{1,7},{2,4},{3,5},{4,2},{5,3},{6,0},{7,1},{8,14},{9,15},{10,... | collective-permute-start | bytes 258056 | tf_op jit(solution)/shard_map/ppermute | solution.py:507
  52.5 1.6 %collective-permute-start.10 = (bf16[336,128]{1,0:T(8,128)(2,1)S(1)}, bf16[336,128]{1,0:T(8,128)(2,1)S(1)}, u32[]{:S(2)}, u32[]{:S(2)}) collective-permute-start(bf16[336,128]{1,0:T(8,128)(2,1)S(1)} %get-tuple-element.49), channel_id=1, source_target_pairs={{0,7},{1,6},{2,5},{3,4},{4,3},{5,2},{6,1},{7,0},{8,15},{9,14},{10,... | collective-permute-start | bytes 258056 | tf_op jit(solution)/shard_map/ppermute | solution.py:507
  54.1 0.0 collective-permute-done.6.rest_0_
  54.1 1.5 %collective-permute-start.11 = (bf16[336,128]{1,0:T(8,128)(2,1)S(1)}, bf16[336,128]{1,0:T(8,128)(2,1)S(1)}, u32[]{:S(2)}, u32[]{:S(2)}) collective-permute-start(bf16[336,128]{1,0:T(8,128)(2,1)S(1)} %get-tuple-element.50), channel_id=1, source_target_pairs={{0,3},{1,2},{2,1},{3,0},{4,7},{5,6},{6,5},{7,4},{8,11},{9,10},{10,... | collective-permute-start | bytes 258056 | tf_op jit(solution)/shard_map/ppermute | solution.py:507
  55.7 1.0 %collective-permute-done.7.rest_1_ = bf16[336,128]{1,0:T(8,128)(2,1)S(1)} collective-permute-done((bf16[336,128]{1,0:T(8,128)(2,1)S(1)}, bf16[336,128]{1,0:T(8,128)(2,1)S(1)}, u32[]{:S(2)}, u32[]{:S(2)}) %collective-permute-start.7) | collective-permute-done | bytes 86048 | tf_op jit(solution)/shard_map/ppermute | solution.py:507
  56.6 0.0 collective-permute-start.12
  56.6 4.1 %collective-permute-done.8.rest_2_ = bf16[336,128]{1,0:T(8,128)(2,1)S(1)} collective-permute-done((bf16[336,128]{1,0:T(8,128)(2,1)S(1)}, bf16[336,128]{1,0:T(8,128)(2,1)S(1)}, u32[]{:S(2)}, u32[]{:S(2)}) %collective-permute-start.8) | collective-permute-done | bytes 86048 | tf_op jit(solution)/shard_map/ppermute | solution.py:507
  60.7 0.0 collective-permute-done.9.rest_3_
  60.7 0.0 collective-permute-done.10.rest_4_
  60.7 0.4 collective-permute-done.11.rest_5_
  61.2 0.3 collective-permute-done.12.rest_6_
  61.5 0.0 copy-done.6
  61.5 1.5 %project.1 = (f32[128,1280]{1,0:T(8,128)S(1)}, bf16[128,1280]{1,0:T(8,128)(2,1)S(1)}) custom-call(s32[1]{0:T(128)} %bitcast.place, bf16[128,1280]{1,0:T(8,128)(2,1)S(1)} %bitcast.7, f32[1280]{0:T(1024)S(1)} %copy-done.6, bf16[1280,1280]{1,0:T(8,128)(2,1)S(1)} %get-tuple-element.44.w_out, bf16[336,128]{1,0:T(8,128)(2,1)S(1)} %collective-permute-done.6.rest_0_, ...), custom_call_target="tpu_custom_call" | custom-call | flops 419430400 | bytes 3276800 | tf_op jit(solution)/shard_map/project/pallas_call | solution.py:422
  63.0 0.1 collective-permute-start.14
  63.0 1.6 %collective-permute-start.13 = (bf16[128,1280]{1,0:T(8,128)(2,1)S(1)}, bf16[128,1280]{1,0:T(8,128)(2,1)S(1)}, u32[]{:S(2)}, u32[]{:S(2)}) collective-permute-start(bf16[128,1280]{1,0:T(8,128)(2,1)S(1)} %get-tuple-element.54.first), channel_id=1, source_target_pairs={{0,16},{8,24},{16,0},{24,8},{1,17},{9,25},{17,1},{25,9},{2,18},{10... | collective-permute-start | bytes 983048 | tf_op jit(solution)/shard_map/ppermute | solution.py:507
  64.6 0.0 collective-permute-done.14.second
  64.7 0.0 copy-done.2
  64.7 2.9 %mlp.2 = (f32[128,1280]{1,0:T(8,128)S(1)}, bf16[128,1280]{1,0:T(8,128)(2,1)S(1)}) custom-call(bf16[128,1280]{1,0:T(8,128)(2,1)S(1)} %get-tuple-element.54.first, bf16[128,1280]{1,0:T(8,128)(2,1)S(1)} %collective-permute-done.14.second, bf16[1280,1280]{1,0:T(8,128)(2,1)S(1)} %copy-done, bf16[1280,1280]{1,0:T(8,128)(2,1)S(1)} %copy-done.1, ...), custom_call_target="tpu_custom_call" | custom-call | flops 2516582400 | bytes 9830400 | tf_op jit(solution)/shard_map/mlp/pallas_call | solution.py:453
  67.6 5.6 %collective-permute-done.13.first = bf16[128,1280]{1,0:T(8,128)(2,1)S(1)} collective-permute-done((bf16[128,1280]{1,0:T(8,128)(2,1)S(1)}, bf16[128,1280]{1,0:T(8,128)(2,1)S(1)}, u32[]{:S(2)}, u32[]{:S(2)}) %collective-permute-start.13) | collective-permute-done | bytes 327712 | tf_op jit(solution)/shard_map/ppermute | solution.py:507
  73.2 0.0 collective-permute-start.16
  73.2 1.6 %collective-permute-done.16.second = bf16[128,1280]{1,0:T(8,128)(2,1)S(1)} collective-permute-done((bf16[128,1280]{1,0:T(8,128)(2,1)S(1)}, bf16[128,1280]{1,0:T(8,128)(2,1)S(1)}, u32[]{:S(2)}, u32[]{:S(2)}) %collective-permute-start.16) | collective-permute-done | bytes 327712 | tf_op jit(solution)/shard_map/ppermute | solution.py:507
  74.8 2.9 %mlp.3 = (f32[128,1280]{1,0:T(8,128)S(1)}, bf16[128,1280]{1,0:T(8,128)(2,1)S(1)}) custom-call(bf16[128,1280]{1,0:T(8,128)(2,1)S(1)} %collective-permute-done.13.first, bf16[128,1280]{1,0:T(8,128)(2,1)S(1)} %collective-permute-done.16.second, bf16[1280,1280]{1,0:T(8,128)(2,1)S(1)} %copy-done, bf16[1280,1280]{1,0:T(8,128)(2,1)S(1)} %copy-done.1, ...), custom_call_target="tpu_custom_call" | custom-call | flops 2516582400 | bytes 9830400 | tf_op jit(solution)/shard_map/mlp/pallas_call | solution.py:453
  77.7 0.2 collective-permute-start.17
  77.9 0.4 collective-permute-start.15
  78.3 1.1 %collective-permute-done.17.arrived = bf16[128,1280]{1,0:T(8,128)(2,1)S(1)} collective-permute-done((bf16[128,1280]{1,0:T(8,128)(2,1)S(1)}, bf16[128,1280]{1,0:T(8,128)(2,1)S(1)}, u32[]{:S(2)}, u32[]{:S(2)}) %collective-permute-start.17) | collective-permute-done | bytes 327712 | tf_op jit(solution)/shard_map/ppermute | solution.py:507
  79.4 0.1 add_partials.1
  79.5 1.6 %collective-permute-start.18 = (bf16[128,1280]{1,0:T(8,128)(2,1)S(1)}, bf16[128,1280]{1,0:T(8,128)(2,1)S(1)}, u32[]{:S(2)}, u32[]{:S(2)}) collective-permute-start(bf16[128,1280]{1,0:T(8,128)(2,1)S(1)} %add_partials.1), channel_id=1, source_target_pairs={{0,16},{8,24},{16,0},{24,8},{1,17},{9,25},{17,1},{25,9},{2,18},{10... | collective-permute-start | bytes 983048 | tf_op jit(solution)/shard_map/ppermute | solution.py:507
  81.1 0.0 collective-permute-done.15.rest_0_
  81.1 8.2 %collective-permute-done.18.rest_1_ = bf16[128,1280]{1,0:T(8,128)(2,1)S(1)} collective-permute-done((bf16[128,1280]{1,0:T(8,128)(2,1)S(1)}, bf16[128,1280]{1,0:T(8,128)(2,1)S(1)}, u32[]{:S(2)}, u32[]{:S(2)}) %collective-permute-start.18) | collective-permute-done | bytes 327712 | tf_op jit(solution)/shard_map/ppermute | solution.py:507
  89.3 1.3 %finish.1 = bf16[128,1280]{1,0:T(8,128)(2,1)} custom-call(f32[128,1280]{1,0:T(8,128)S(1)} %get-tuple-element.53.hidden, f32[1280]{0:T(1024)S(1)} %copy-done.7, f32[128,1280]{1,0:T(8,128)S(1)} %get-tuple-element.56.kept, bf16[128,1280]{1,0:T(8,128)(2,1)S(1)} %collective-permute-done.15.rest_0_, bf16[128,1280]{1,0:T(8,128)(2,1)S(1)} %collective-permute-done.18.rest_1_), custom_call_target="tpu_custom_call" | custom-call | flops 1638400 | bytes 1966080 | tf_op jit(solution)/shard_map/finish/pallas_call | solution.py:493
  (10 shorter events, 0.0 us)
Async XLA Ops:
  0.0 7.3 %copy-start.3 = (bf16[1,128,1280]{2,1,0:T(8,128)(2,1)S(1)}, bf16[1,128,1280]{2,1,0:T(8,128)(2,1)}, u32[]{:S(2)}) copy-start(bf16[1,128,1280]{2,1,0:T(8,128)(2,1)} %param.14) | copy-start | bytes 983044
  0.0 7.3 %copy-start.9 = (f32[1280]{0:T(1024)S(1)}, f32[1280]{0:T(1024)}, u32[]{:S(2)}) copy-start(f32[1280]{0:T(1024)} %rest_0_.1) | copy-start | bytes 15364
  2.7 19.2 %collective-permute-start = (bf16[640,256]{1,0:T(8,128)(2,1)}, bf16[640,256]{1,0:T(8,128)(2,1)S(1)}, u32[]{:S(2)}, u32[]{:S(2)}) collective-permute-start(bf16[640,256]{1,0:T(8,128)(2,1)} %get-tuple-element.35), channel_id=1, source_target_pairs={{0,1},{1,0},{2,3},{3,2},{4,5},{5,4},{6,7},{7,6},{8,9},{9,8},{10,11... | collective-permute-start | bytes 983048 | tf_op jit(solution)/shard_map/ppermute | solution.py:507
  5.8 16.3 %collective-permute-start.1 = (bf16[640,256]{1,0:T(8,128)(2,1)}, bf16[640,256]{1,0:T(8,128)(2,1)S(1)}, u32[]{:S(2)}, u32[]{:S(2)}) collective-permute-start(bf16[640,256]{1,0:T(8,128)(2,1)} %get-tuple-element.36), channel_id=1, source_target_pairs={{0,2},{1,3},{2,0},{3,1},{4,6},{5,7},{6,4},{7,5},{8,10},{9,11},{10,... | collective-permute-start | bytes 983048 | tf_op jit(solution)/shard_map/ppermute | solution.py:507
  7.3 16.5 %collective-permute-start.2 = (bf16[640,256]{1,0:T(8,128)(2,1)}, bf16[640,256]{1,0:T(8,128)(2,1)S(1)}, u32[]{:S(2)}, u32[]{:S(2)}) collective-permute-start(bf16[640,256]{1,0:T(8,128)(2,1)} %get-tuple-element.37), channel_id=1, source_target_pairs={{0,3},{1,2},{2,1},{3,0},{4,7},{5,6},{6,5},{7,4},{8,11},{9,10},{10,... | collective-permute-start | bytes 983048 | tf_op jit(solution)/shard_map/ppermute | solution.py:507
  7.3 16.5 %copy-start.11 = (bf16[640,256]{1,0:T(8,128)(2,1)S(1)}, bf16[640,256]{1,0:T(8,128)(2,1)}, u32[]{:S(2)}) copy-start(bf16[640,256]{1,0:T(8,128)(2,1)} %get-tuple-element.34.refs_0_.rest_0_) | copy-start | bytes 983044
  12.3 22.2 %all-to-all-start = ((bf16[8,320,128]{2,1,0:T(8,128)(2,1)}), bf16[8,320,128]{2,1,0:T(8,128)(2,1)S(1)}, u32[]{:S(2)}, u32[]{:S(2)}) async-start(bf16[8,320,128]{2,1,0:T(8,128)(2,1)} %bitcast.2), calls=%async_computation | async-start | bytes 1310720 | tf_op jit(solution)/shard_map/all_to_all | solution.py:536
  18.5 23.0 %collective-permute-start.3 = (bf16[640,128]{1,0:T(8,128)(2,1)S(1)}, bf16[640,128]{1,0:T(8,128)(2,1)S(1)}, u32[]{:S(2)}, u32[]{:S(2)}) collective-permute-start(bf16[640,128]{1,0:T(8,128)(2,1)S(1)} %get-tuple-element.41), channel_id=1, source_target_pairs={{0,1},{1,0},{2,3},{3,2},{4,5},{5,4},{6,7},{7,6},{8,9},{9,8},{10,11... | collective-permute-start | bytes 491528 | tf_op jit(solution)/shard_map/ppermute | solution.py:507
  20.5 21.0 %collective-permute-start.4 = (bf16[640,128]{1,0:T(8,128)(2,1)S(1)}, bf16[640,128]{1,0:T(8,128)(2,1)S(1)}, u32[]{:S(2)}, u32[]{:S(2)}) collective-permute-start(bf16[640,128]{1,0:T(8,128)(2,1)S(1)} %get-tuple-element.42), channel_id=1, source_target_pairs={{0,2},{1,3},{2,0},{3,1},{4,6},{5,7},{6,4},{7,5},{8,10},{9,11},{10,... | collective-permute-start | bytes 491528 | tf_op jit(solution)/shard_map/ppermute | solution.py:507
  22.0 19.5 %collective-permute-start.5 = (bf16[640,128]{1,0:T(8,128)(2,1)S(1)}, bf16[640,128]{1,0:T(8,128)(2,1)S(1)}, u32[]{:S(2)}, u32[]{:S(2)}) collective-permute-start(bf16[640,128]{1,0:T(8,128)(2,1)S(1)} %get-tuple-element.43), channel_id=1, source_target_pairs={{0,3},{1,2},{2,1},{3,0},{4,7},{5,6},{6,5},{7,4},{8,11},{9,10},{10,... | collective-permute-start | bytes 491528 | tf_op jit(solution)/shard_map/ppermute | solution.py:507
  23.9 17.7 %copy-start.10 = (s32[1,16]{1,0:T(1,128)S(1)}, s32[1,16]{1,0:T(1,128)}, u32[]{:S(2)}) copy-start(s32[1,16]{1,0:T(1,128)} %lengths.1) | copy-start | bytes 196
  34.5 7.0 %copy-start.8 = (bf16[1280,1280]{1,0:T(8,128)(2,1)S(1)}, bf16[1280,1280]{1,0:T(8,128)(2,1)}, u32[]{:S(2)}) copy-start(bf16[1280,1280]{1,0:T(8,128)(2,1)} %rest_4_.1) | copy-start | bytes 9830404
  41.5 19.9 %copy-start.6 = (f32[1280]{0:T(1024)S(1)}, f32[1280]{0:T(1024)}, u32[]{:S(2)}) copy-start(f32[1280]{0:T(1024)} %rate_hbm.2) | copy-start | bytes 15364
  41.6 23.1 %copy-start.1 = (bf16[1280,1280]{1,0:T(8,128)(2,1)S(1)}, bf16[1280,1280]{1,0:T(8,128)(2,1)}, u32[]{:S(2)}) copy-start(bf16[1280,1280]{1,0:T(8,128)(2,1)} %w_gate.3) | copy-start | bytes 9830404
  41.6 23.1 %copy-start.2 = (bf16[1280,1280]{1,0:T(8,128)(2,1)S(1)}, bf16[1280,1280]{1,0:T(8,128)(2,1)}, u32[]{:S(2)}) copy-start(bf16[1280,1280]{1,0:T(8,128)(2,1)} %w_down.3) | copy-start | bytes 9830404
  44.8 19.9 %copy-start = (bf16[1280,1280]{1,0:T(8,128)(2,1)S(1)}, bf16[1280,1280]{1,0:T(8,128)(2,1)}, u32[]{:S(2)}) copy-start(bf16[1280,1280]{1,0:T(8,128)(2,1)} %w_up.3) | copy-start | bytes 9830404
  44.8 19.9 %copy-start.4 = (f32[1280]{0:T(1024)S(1)}, f32[1280]{0:T(1024)}, u32[]{:S(2)}) copy-start(f32[1280]{0:T(1024)} %up_scale.3) | copy-start | bytes 15364
  44.8 19.9 %copy-start.5 = (f32[1280]{0:T(1024)S(1)}, f32[1280]{0:T(1024)}, u32[]{:S(2)}) copy-start(f32[1280]{0:T(1024)} %gate_scale.3) | copy-start | bytes 15364
  44.8 9.3 %collective-permute-start.6 = (bf16[336,128]{1,0:T(8,128)(2,1)S(1)}, bf16[336,128]{1,0:T(8,128)(2,1)S(1)}, u32[]{:S(2)}, u32[]{:S(2)}) collective-permute-start(bf16[336,128]{1,0:T(8,128)(2,1)S(1)} %get-tuple-element.45), channel_id=1, source_target_pairs={{0,1},{1,0},{2,3},{3,2},{4,5},{5,4},{6,7},{7,6},{8,9},{9,8},{10,11... | collective-permute-start | bytes 258056 | tf_op jit(solution)/shard_map/ppermute | solution.py:507
  46.5 10.2 %collective-permute-start.7 = (bf16[336,128]{1,0:T(8,128)(2,1)S(1)}, bf16[336,128]{1,0:T(8,128)(2,1)S(1)}, u32[]{:S(2)}, u32[]{:S(2)}) collective-permute-start(bf16[336,128]{1,0:T(8,128)(2,1)S(1)} %get-tuple-element.46), channel_id=1, source_target_pairs={{0,4},{1,5},{2,6},{3,7},{4,0},{5,1},{6,2},{7,3},{8,12},{9,13},{10,... | collective-permute-start | bytes 258056 | tf_op jit(solution)/shard_map/ppermute | solution.py:507
  48.3 12.4 %collective-permute-start.8 = (bf16[336,128]{1,0:T(8,128)(2,1)S(1)}, bf16[336,128]{1,0:T(8,128)(2,1)S(1)}, u32[]{:S(2)}, u32[]{:S(2)}) collective-permute-start(bf16[336,128]{1,0:T(8,128)(2,1)S(1)} %get-tuple-element.47), channel_id=1, source_target_pairs={{0,5},{1,4},{2,7},{3,6},{4,1},{5,0},{6,3},{7,2},{8,13},{9,12},{10,... | collective-permute-start | bytes 258056 | tf_op jit(solution)/shard_map/ppermute | solution.py:507
  49.3 11.5 %collective-permute-start.9 = (bf16[336,128]{1,0:T(8,128)(2,1)S(1)}, bf16[336,128]{1,0:T(8,128)(2,1)S(1)}, u32[]{:S(2)}, u32[]{:S(2)}) collective-permute-start(bf16[336,128]{1,0:T(8,128)(2,1)S(1)} %get-tuple-element.48), channel_id=1, source_target_pairs={{0,6},{1,7},{2,4},{3,5},{4,2},{5,3},{6,0},{7,1},{8,14},{9,15},{10,... | collective-permute-start | bytes 258056 | tf_op jit(solution)/shard_map/ppermute | solution.py:507
  52.5 8.2 %collective-permute-start.10 = (bf16[336,128]{1,0:T(8,128)(2,1)S(1)}, bf16[336,128]{1,0:T(8,128)(2,1)S(1)}, u32[]{:S(2)}, u32[]{:S(2)}) collective-permute-start(bf16[336,128]{1,0:T(8,128)(2,1)S(1)} %get-tuple-element.49), channel_id=1, source_target_pairs={{0,7},{1,6},{2,5},{3,4},{4,3},{5,2},{6,1},{7,0},{8,15},{9,14},{10,... | collective-permute-start | bytes 258056 | tf_op jit(solution)/shard_map/ppermute | solution.py:507
  54.1 7.1 %collective-permute-start.11 = (bf16[336,128]{1,0:T(8,128)(2,1)S(1)}, bf16[336,128]{1,0:T(8,128)(2,1)S(1)}, u32[]{:S(2)}, u32[]{:S(2)}) collective-permute-start(bf16[336,128]{1,0:T(8,128)(2,1)S(1)} %get-tuple-element.50), channel_id=1, source_target_pairs={{0,3},{1,2},{2,1},{3,0},{4,7},{5,6},{6,5},{7,4},{8,11},{9,10},{10,... | collective-permute-start | bytes 258056 | tf_op jit(solution)/shard_map/ppermute | solution.py:507
  56.6 4.8 %collective-permute-start.12 = (bf16[336,128]{1,0:T(8,128)(2,1)S(1)}, bf16[336,128]{1,0:T(8,128)(2,1)S(1)}, u32[]{:S(2)}, u32[]{:S(2)}) collective-permute-start(bf16[336,128]{1,0:T(8,128)(2,1)S(1)} %get-tuple-element.51), channel_id=1, source_target_pairs={{0,2},{1,3},{2,0},{3,1},{4,6},{5,7},{6,4},{7,5},{8,10},{9,11},{10,... | collective-permute-start | bytes 258056 | tf_op jit(solution)/shard_map/ppermute | solution.py:507
  63.0 1.7 %collective-permute-start.14 = (bf16[128,1280]{1,0:T(8,128)(2,1)S(1)}, bf16[128,1280]{1,0:T(8,128)(2,1)S(1)}, u32[]{:S(2)}, u32[]{:S(2)}) collective-permute-start(bf16[128,1280]{1,0:T(8,128)(2,1)S(1)} %get-tuple-element.54.first), channel_id=1, source_target_pairs={{0,8},{8,0},{16,24},{24,16},{1,9},{9,1},{17,25},{25,17},{2,10},{10... | collective-permute-start | bytes 983048 | tf_op jit(solution)/shard_map/ppermute | solution.py:507
  63.0 10.1 %collective-permute-start.13 = (bf16[128,1280]{1,0:T(8,128)(2,1)S(1)}, bf16[128,1280]{1,0:T(8,128)(2,1)S(1)}, u32[]{:S(2)}, u32[]{:S(2)}) collective-permute-start(bf16[128,1280]{1,0:T(8,128)(2,1)S(1)} %get-tuple-element.54.first), channel_id=1, source_target_pairs={{0,16},{8,24},{16,0},{24,8},{1,17},{9,25},{17,1},{25,9},{2,18},{10... | collective-permute-start | bytes 983048 | tf_op jit(solution)/shard_map/ppermute | solution.py:507
  73.2 16.1 %copy-start.7 = (f32[1280]{0:T(1024)S(1)}, f32[1280]{0:T(1024)}, u32[]{:S(2)}) copy-start(f32[1280]{0:T(1024)} %rate_hbm.3) | copy-start | bytes 15364
  73.2 1.6 %collective-permute-start.16 = (bf16[128,1280]{1,0:T(8,128)(2,1)S(1)}, bf16[128,1280]{1,0:T(8,128)(2,1)S(1)}, u32[]{:S(2)}, u32[]{:S(2)}) collective-permute-start(bf16[128,1280]{1,0:T(8,128)(2,1)S(1)} %collective-permute-done.13.first), channel_id=1, source_target_pairs={{0,8},{8,0},{16,24},{24,16},{1,9},{9,1},{17,25},{25,17},{2,10},{10... | collective-permute-start | bytes 983048 | tf_op jit(solution)/shard_map/ppermute | solution.py:507
  77.7 1.7 %collective-permute-start.17 = (bf16[128,1280]{1,0:T(8,128)(2,1)S(1)}, bf16[128,1280]{1,0:T(8,128)(2,1)S(1)}, u32[]{:S(2)}, u32[]{:S(2)}) collective-permute-start(bf16[128,1280]{1,0:T(8,128)(2,1)S(1)} %get-tuple-element.60), channel_id=1, source_target_pairs={{0,8},{8,0},{16,24},{24,16},{1,9},{9,1},{17,25},{25,17},{2,10},{10... | collective-permute-start | bytes 983048 | tf_op jit(solution)/shard_map/ppermute | solution.py:507
  77.9 3.2 %collective-permute-start.15 = (bf16[128,1280]{1,0:T(8,128)(2,1)S(1)}, bf16[128,1280]{1,0:T(8,128)(2,1)S(1)}, u32[]{:S(2)}, u32[]{:S(2)}) collective-permute-start(bf16[128,1280]{1,0:T(8,128)(2,1)S(1)} %get-tuple-element.57), channel_id=1, source_target_pairs={{0,8},{8,0},{16,24},{24,16},{1,9},{9,1},{17,25},{25,17},{2,10},{10... | collective-permute-start | bytes 983048 | tf_op jit(solution)/shard_map/ppermute | solution.py:507
  79.5 9.8 %collective-permute-start.18 = (bf16[128,1280]{1,0:T(8,128)(2,1)S(1)}, bf16[128,1280]{1,0:T(8,128)(2,1)S(1)}, u32[]{:S(2)}, u32[]{:S(2)}) collective-permute-start(bf16[128,1280]{1,0:T(8,128)(2,1)S(1)} %add_partials.1), channel_id=1, source_target_pairs={{0,16},{8,24},{16,0},{24,8},{1,17},{9,25},{17,1},{25,9},{2,18},{10... | collective-permute-start | bytes 983048 | tf_op jit(solution)/shard_map/ppermute | solution.py:507
